TPU v7x, 32 devices: a whole 2x2x4 slice. The times are simulated.
32 devices in a mesh: az: 8 (over z, x), rad: 4 (over y, core).
Axes of the slice: x: 2, y: 2, z: 4, core: 2. Of those that a mesh axis runs over, the one named last changes fastest.
Arguments:
- potential: float32 [3, 3, 2048, 512], P(None, None, 'az', 'rad'), may hold values from -6 to 6
- current: float32 [3, 3, 2048, 512], P(None, None, 'az', 'rad'), may hold values from -24 to 24
- material: int32 [3, 2048, 512], P(None, 'az', 'rad'), may hold values from 0 to 7
- nu_table: float32 [8], replicated, may hold values from 0.2 to 2
- sat_table: float32 [8], replicated, may hold values from 0.2 to 3
- panel_flux: float32 [9, 2048], P(None, 'az'), may hold values from -48 to 48
- panel_jitter: int32 [2048], P('az'), may hold values from 0 to 2047
- rotor_offset: int32 [1], replicated, may hold values from 0 to 2047
Outputs:
- updated: float32 [3, 3, 2048, 512], P(None, None, 'az', 'rad')
All inputs are finite; a program needn't handle non-finite values.
Results may differ from a plain program's by a relative error of at most 0.000064.
Values sent between devices are 32-bit elements; how exact they have to be, the bound alone decides.
No kernel may reach another device: no remote copies, remote signals or barrier semaphores. Data moves between devices by JAX's collectives and lax.ppermute only.
A program may use at most 64 MiB of HBM per device.

v0:
```python
import jax
import jax.numpy as jnp
from jax import lax
from jax.sharding import PartitionSpec as P

sigma_term = 1.0
neighbour_steps = ((0, 1, 0), (0, -1, 0), (0, 0, 1), (0, 0, -1), (1, 0, 0), (-1, 0, 0))


def with_halo(x, sides, width, wrap):
    for axis, dim in sides:
        peers, length = (lax.axis_size(axis), x.shape[dim])
        up = [(i, (i + 1) % peers) for i in range(peers if wrap else peers - 1)]
        down = [(j, i) for i, j in up]
        last = lax.slice_in_dim(x, length - width, length, axis=dim)
        first = lax.slice_in_dim(x, 0, width, axis=dim)
        before = lax.ppermute(last, axis, up)
        after = lax.ppermute(first, axis, down)
        x = jnp.concatenate([before, x, after], axis=dim)
    return x


def lookup(material, values_table):
    result = jnp.zeros(material.shape, values_table.dtype)
    for entry in range(values_table.shape[0]):
        result = result + jnp.where(
            material == entry, values_table[entry], jnp.zeros((), values_table.dtype)
        )
    return result


def extend_cells(field, width):
    widened = with_halo(field, (("az", 2),), width, True)
    return with_halo(widened, (("rad", 3),), width, False)


def strength(extended):
    centre = extended[:, :, 1:-1, 1:-1]
    azimuth_diff = extended[:, :, 2:, 1:-1] - centre
    radial_diff = extended[:, :, 1:-1, 2:] - centre
    return jnp.sum(azimuth_diff * azimuth_diff + radial_diff * radial_diff, axis=0, keepdims=True)


def offset_view(field, layer_step, az_step, rad_step):
    return field[
        :,
        1 + layer_step : field.shape[1] - 1 + layer_step,
        1 + az_step : field.shape[2] - 1 + az_step,
        1 + rad_step : field.shape[3] - 1 + rad_step,
    ]


def jacobi_sweep(field, coef, source):
    padded_field = jnp.pad(field, ((0, 0), (1, 1), (0, 0), (0, 0)))
    padded_coef = jnp.pad(coef, ((0, 0), (1, 1), (0, 0), (0, 0)))
    centre = offset_view(padded_coef, 0, 0, 0)
    numerator = source
    denominator = jnp.full_like(centre, sigma_term)
    for layer_step, az_step, rad_step in neighbour_steps:
        face_coef = 0.5 * (centre + offset_view(padded_coef, layer_step, az_step, rad_step))
        numerator = numerator + face_coef * offset_view(padded_field, layer_step, az_step, rad_step)
        denominator = denominator + face_coef
    return numerator / denominator


def deposit(block_piece, offset, cell_count, cycle_cells, base_cell):
    values = block_piece[:-1]
    jitter = block_piece[-1].astype(jnp.int32)
    position = (offset + jitter) % cycle_cells
    local_cell = position - base_cell
    onehot = (local_cell[:, None] == jnp.arange(cell_count, dtype=jnp.int32)[None, :]).astype(
        jnp.float32
    )
    return jnp.dot(
        values, onehot, precision=lax.Precision.HIGHEST, preferred_element_type=jnp.float32
    )


def local(
    potential, current, material, nu_table, sat_table, panel_flux, panel_jitter, rotor_offset
):
    layers = potential.shape[1]
    tile_cells = potential.shape[2]
    radial_cells = potential.shape[3]
    az_count = lax.axis_size("az")
    cycle_cells = tile_cells * az_count
    own_tile = lax.axis_index("az")
    base_cell = own_tile * tile_cells
    offset = rotor_offset[0]
    packed = jnp.concatenate([panel_flux, panel_jitter.astype(jnp.float32)[None, :]], axis=0)
    airgap = deposit(
        lax.all_gather(packed, "az", axis=1, tiled=True), offset, tile_cells, cycle_cells, base_cell
    )
    stator_row = lax.axis_index("rad") == lax.axis_size("rad") // 2
    airgap = jnp.where(stator_row, airgap, 0.0).reshape(3, layers, tile_cells)
    source = current.at[:, :, :, 0].add(airgap)
    base_reluct = lookup(material, nu_table)[None]
    saturation = lookup(material, sat_table)[None]
    stacked = jnp.concatenate([potential, source, base_reluct, saturation], axis=0)
    extended = extend_cells(stacked, 3)
    field_wide = extended[0:3]
    source_wide = extended[3:6]
    base_wide = extended[6:7]
    sat_wide = extended[7:8]
    flux_sq = strength(field_wide)
    reluct = base_wide[:, :, 1:-1, 1:-1] * (
        1.0 + sat_wide[:, :, 1:-1, 1:-1] * flux_sq / (1.0 + flux_sq)
    )
    sweep_one = jacobi_sweep(field_wide[:, :, 1:-1, 1:-1], reluct, source_wide[:, :, 2:-2, 2:-2])
    global_rows = (
        lax.axis_index("rad") * radial_cells + jnp.arange(radial_cells + 2, dtype=jnp.int32) - 1
    )
    inside = ((global_rows >= 0) & (global_rows < radial_cells * lax.axis_size("rad"))).astype(
        jnp.float32
    )
    sweep_one = sweep_one * inside
    result = jacobi_sweep(sweep_one, reluct[:, :, 1:-1, 1:-1], source_wide[:, :, 3:-3, 3:-3])
    return result


def solution(mesh):
    placed = (
        P(None, None, "az", "rad"),
        P(None, None, "az", "rad"),
        P(None, "az", "rad"),
        P(),
        P(),
        P(None, "az"),
        P("az"),
        P(),
    )
    return jax.shard_map(
        local, mesh=mesh, in_specs=placed, out_specs=P(None, None, "az", "rad"), check_vma=False
    )
```

profile of v0, /device:TPU:30, one launch (start us, length us, event | category | flops | bytes accessed | tf_op | source)
XLA Modules:
  0.0 93.3 jit_solution(10172694383558987797)
XLA Ops:
  1.4 1.6 %fusion.66 = (f32[1]{0:T(128)}, f32[1]{0:T(128)}, f32[1]{0:T(128)}, f32[1]{0:T(128)}, f32[1]{0:T(128)}, /*index=5*/f32[1]{0:T(128)}, f32[1]{0:T(128)}, f32[1]{0:T(128)}) fusion(f32[8]{0:T(128)} %param.13), kind=kLoop, calls=%fused_computation.131 | loop fusion | bytes 64 | tf_op jit(solution)/shard_map/slice | solution.py:27
  3.1 1.6 %fusion.65 = (f32[1]{0:T(128)}, f32[1]{0:T(128)}, f32[1]{0:T(128)}, f32[1]{0:T(128)}, f32[1]{0:T(128)}, /*index=5*/f32[1]{0:T(128)}, f32[1]{0:T(128)}, f32[1]{0:T(128)}) fusion(f32[8]{0:T(128)} %param.14), kind=kLoop, calls=%fused_computation.130 | loop fusion | bytes 64 | tf_op jit(solution)/shard_map/slice | solution.py:27
  4.7 1.7 %copy.54 = f32[3,3,256,128]{2,3,1,0:T(8,128)S(1)} copy(f32[3,3,256,128]{3,2,1,0:T(8,128)} %param.11) | data formatting | bytes 2359296 | tf_op args[1]
  6.9 30.5 %all_gather.3 = f32[10,2048]{1,0:T(8,128)S(1)} all-gather(f32[10,256]{1,0:T(8,128)S(1)} %pad_maximum_fusion.20), channel_id=1, replica_groups=mesh['az'=8,'rad'=4] {'az'}, dimensions={1}, use_global_device_ids=true | all-gather | bytes 92160 | tf_op jit(solution)/shard_map/all_gather | solution.py:92
  38.3 5.6 %add_bitcast_fusion.3 = (f32[1,3,256,128]{3,2,1,0:T(8,128)S(1)}, pred[3,256,128]{2,1,0:T(8,128)(4,1)S(1)}, pred[3,256,128]{2,1,0:T(8,128)(4,1)S(1)}, pred[3,256,...) fusion(f32[]{:T(128)} %bitcast.10, f32[]{:T(128)} %bitcast.9, ...), kind=kLoop, calls=%fused_computation.91 | loop fusion | flops 2260992 | bytes 1572896 | tf_op jit(solution)/shard_map/broadcast_in_dim | solution.py:97
  44.2 5.5 %add_bitcast_fusion.2 = f32[1,3,256,128]{3,2,1,0:T(8,128)S(1)} fusion(pred[3,256,128]{2,1,0:T(8,128)(4,1)S(1)} %get-tuple-element.25, pred[3,256,128]{2,1,0:T(8,128)(4,1)S(1)} %get-tuple-element.24, pred[3,256,128]{2,1,0:T(8,128)(4,1)S(1)} %get-tuple-element.23, pred[3,256,128]{2,1,0:T(8,128)(4,1)S(1)} %get-tuple-element.22, ...), kind=kLoop, calls=%fused_computation.90 | loop fusion | flops 1474560 | bytes 1179680 | tf_op jit(solution)/shard_map/broadcast_in_dim | solution.py:98
  49.8 1.6 %copy.56 = f32[3,3,256,128]{2,3,1,0:T(8,128)S(1)} copy(f32[3,3,256,128]{3,2,1,0:T(8,128)} %param.10) | data formatting | bytes 2359296 | tf_op args[0]
  51.8 2.2 %fusion.63 = (f32[8,3,3,128]{2,3,1,0:T(8,128)}, f32[8,3,3,128]{2,3,1,0:T(8,128)}) fusion(f32[8,3,256,128]{2,3,1,0:T(8,128)S(1)} %pad_maximum_fusion.1), kind=kLoop, calls=%fused_computation.128 | loop fusion | bytes 147456 | tf_op jit(solution)/shard_map/slice | solution.py:15
  54.0 1.9 %copy.59 = f32[8,3,3,128]{3,0,2,1:T(8,128)S(1)} copy(f32[8,3,3,128]{2,3,1,0:T(8,128)} %get-tuple-element.30) | data formatting | bytes 73728 | tf_op jit(solution)/shard_map/slice | solution.py:15
  56.4 1.9 %copy.60 = f32[8,3,3,128]{3,0,2,1:T(8,128)S(1)} copy(f32[8,3,3,128]{2,3,1,0:T(8,128)} %get-tuple-element.31) | data formatting | bytes 73728 | tf_op jit(solution)/shard_map/slice | solution.py:16
  58.3 1.5 %collective-permute-start.1 = (f32[8,3,3,128]{3,0,2,1:T(8,128)S(1)}, f32[8,3,3,128]{3,0,2,1:T(8,128)S(1)}, u32[]{:S(2)}, u32[]{:S(2)}) collective-permute-start(f32[8,3,3,128]{3,0,2,1:T(8,128)S(1)} %copy.60), channel_id=1, source_target_pairs={{4,0},{8,4},{12,8},{16,12},{20,16},{24,20},{28,24},{0,28},{5,1},{9... | collective-permute-start | bytes 110600 | tf_op jit(solution)/shard_map/ppermute | solution.py:18
  59.8 1.7 %copy.61 = f32[8,3,3,128]{2,3,1,0:T(8,128)} copy(f32[8,3,3,128]{3,0,2,1:T(8,128)S(1)} %collective-permute-done) | data formatting | bytes 73728 | tf_op jit(solution)/shard_map/ppermute | solution.py:17
  61.5 3.5 %collective-permute-done.1 = f32[8,3,3,128]{3,0,2,1:T(8,128)S(1)} collective-permute-done((f32[8,3,3,128]{3,0,2,1:T(8,128)S(1)}, f32[8,3,3,128]{3,0,2,1:T(8,128)S(1)}, u32[]{:S(2)}, u32[]{:S(2)}) %collective-permute-start.1) | collective-permute-done | bytes 36896 | tf_op jit(solution)/shard_map/ppermute | solution.py:18
  65.0 1.7 %copy.62 = f32[8,3,3,128]{2,3,1,0:T(8,128)} copy(f32[8,3,3,128]{3,0,2,1:T(8,128)S(1)} %collective-permute-done.1) | data formatting | bytes 73728 | tf_op jit(solution)/shard_map/ppermute | solution.py:18
  66.7 1.5 %pad_maximum_fusion.19 = (f32[8,3,262,3]{2,3,1,0:T(4,128)S(1)}, f32[8,3,262,3]{2,3,1,0:T(4,128)S(1)}) fusion(f32[8,3,3,128]{2,3,1,0:T(8,128)} %copy.62, f32[8,3,3,128]{2,3,1,0:T(8,128)} %copy.61, f32[1,3,256,128]{2,3,1,0:T(8,128)S(1)} %copy.58, f32[1,3,256,128]{2,3,1,0:T(8,128)S(1)} %copy.57, f32[3,3,256,128]{2,3,1,0:T(8,128)S(1)} %scatter-add.4, ...), kind=kLoop, calls=%fused_computation.109 | loop fusion | flops 188640 | bytes 3370368 | tf_op jit(solution)/shard_map/slice | solution.py:15
  68.2 1.9 %collective-permute-start.3 = (f32[8,3,262,3]{2,0,3,1:T(8,128)S(1)}, f32[8,3,262,3]{2,0,3,1:T(8,128)S(1)}, u32[]{:S(2)}, u32[]{:S(2)}) collective-permute-start(f32[8,3,262,3]{2,0,3,1:T(8,128)S(1)} %copy.64), channel_id=1, source_target_pairs={{1,0},{2,1},{3,2},{5,4},{6,5},{7,6},{9,8},{10,9},{11,10},{13,12},{... | collective-permute-start | bytes 226376 | tf_op jit(solution)/shard_map/ppermute | solution.py:18
  70.1 2.6 %collective-permute-start.2 = (f32[8,3,262,3]{2,0,3,1:T(8,128)S(1)}, f32[8,3,262,3]{2,0,3,1:T(8,128)S(1)}, u32[]{:S(2)}, u32[]{:S(2)}) collective-permute-start(f32[8,3,262,3]{2,0,3,1:T(8,128)S(1)} %copy.63), channel_id=1, source_target_pairs={{0,1},{1,2},{2,3},{4,5},{5,6},{6,7},{8,9},{9,10},{10,11},{12,13},{... | collective-permute-start | bytes 226376 | tf_op jit(solution)/shard_map/ppermute | solution.py:17
  72.8 3.4 %collective-permute-done.2 = f32[8,3,262,3]{2,0,3,1:T(8,128)S(1)} collective-permute-done((f32[8,3,262,3]{2,0,3,1:T(8,128)S(1)}, f32[8,3,262,3]{2,0,3,1:T(8,128)S(1)}, u32[]{:S(2)}, u32[]{:S(2)}) %collective-permute-start.2) | collective-permute-done | bytes 75488 | tf_op jit(solution)/shard_map/ppermute | solution.py:17
  76.2 3.8 %pad_maximum_fusion = f32[8,3,262,134]{2,3,1,0:T(8,128)S(1)} fusion(f32[8,3,262,3]{2,3,1,0:T(4,128)S(1)} %copy.66, f32[8,3,3,128]{2,3,1,0:T(8,128)S(1)} %copy-done.1, f32[1,3,256,128]{2,3,1,0:T(8,128)S(1)} %copy.58, f32[1,3,256,128]{2,3,1,0:T(8,128)S(1)} %copy.57, f32[3,3,256,128]{2,3,1,0:T(8,128)S(1)} %scatter-add.4, f32[3,3,256,128]{2,3,1,0:T(8,128)S(1)} %copy.56, ...), kind=kLoop, calls=%fused_computation | loop fusion | flops 5898144 | bytes 6740736 | tf_op jit(solution)/shard_map/concatenate | solution.py:19
  80.0 1.5 %fusion.15 = (f32[3,260,132]{1,2,0:T(8,128)S(1)}, f32[3,3,260,132]{2,3,1,0:T(8,128)S(1)}) fusion(f32[8,3,262,134]{2,3,1,0:T(8,128)S(1)} %pad_maximum_fusion), kind=kLoop, calls=%fused_computation.37 | loop fusion | flops 1750320 | bytes 5353920 | tf_op jit(solution)/shard_map/reduce_sum | solution.py:41
  82.0 1.2 %fusion.64 = (f32[1,3,258,130]{2,3,1,0:T(8,128)S(1)}, f32[3,258,130]{1,2,0:T(8,128)S(1)}, f32[3,258,130]{1,2,0:T(8,128)S(1)}, f32[3,258,130]{1,2,0:T(8,128)S(1)}...) fusion(f32[1,3,260,132]{2,3,1,0:T(8,128)S(1)} %fusion.38), kind=kLoop, calls=%fused_computation.129 | loop fusion | flops 2213640 | bytes 6979968 | tf_op jit(solution)/shard_map/slice | solution.py:45
  84.0 6.4 %fusion.5 = f32[3,3,258,130]{2,3,1,0:T(8,128)S(1)} fusion(f32[3,3,260,132]{2,3,1,0:T(8,128)S(1)} %get-tuple-element.29, f32[8,3,262,3]{2,3,1,0:T(4,128)S(1)} %copy.65, f32[8,3,3,128]{2,3,1,0:T(8,128)S(1)} %copy-done.1, f32[8,3,3,128]{2,3,1,0:T(8,128)S(1)} %copy-done, f32[1,3,256,128]{2,3,1,0:T(8,128)S(1)} %copy.58, f32[1,3,256,128]{2,3,1,0:T(8,128)S(1)} %copy.57, ...), kind=kLoop, calls=%fused_computation.12 | loop fusion | flops 7848360 | bytes 12253528 | tf_op jit(solution)/shard_map/mul | solution.py:116
  90.4 1.5 %fusion.20 = f32[3,3,256,128]{2,3,1,0:T(8,128)S(1)} fusion(f32[3,3,258,130]{2,3,1,0:T(8,128)S(1)} %fusion.5, f32[3,3,256,128]{2,3,1,0:T(8,128)S(1)} %scatter-add.4, f32[3,256,128]{1,2,0:T(8,128)S(1)} %get-tuple-element.40, f32[3,256,128]{1,2,0:T(8,128)S(1)} %get-tuple-element.39, f32[3,256,128]{1,2,0:T(8,128)S(1)} %get-tuple-element.41, ...), kind=kLoop, calls=%fused_computation.47 | loop fusion | flops 3833856 | bytes 11710464 | tf_op jit(solution)/shard_map/div | solution.py:63
  91.9 1.4 %copy.83 = f32[3,3,256,128]{3,2,1,0:T(8,128)} copy(f32[3,3,256,128]{2,3,1,0:T(8,128)S(1)} %fusion.20) | data formatting | bytes 2359296 | tf_op jit(solution)/shard_map/div | solution.py:63
  (33 shorter events, 4.6 us)
Async XLA Ops:
  0.0 6.4 %copy-start.2 = (f32[3,3,256,128]{3,2,1,0:T(8,128)S(1)}, f32[3,3,256,128]{3,2,1,0:T(8,128)}, u32[]{:S(2)}) copy-start(f32[3,3,256,128]{3,2,1,0:T(8,128)} %param.11) | copy-start | bytes 3538948
  0.0 6.9 %copy-start.4 = (f32[9,256]{1,0:T(8,128)S(1)}, f32[9,256]{1,0:T(8,128)}, u32[]{:S(2)}) copy-start(f32[9,256]{1,0:T(8,128)} %param.15) | copy-start | bytes 27652
  4.7 33.6 %copy-start.3 = (s32[3,256,128]{2,1,0:T(8,128)S(1)}, s32[3,256,128]{2,1,0:T(8,128)}, u32[]{:S(2)}) copy-start(s32[3,256,128]{2,1,0:T(8,128)} %param.12) | copy-start | bytes 1179652
  55.9 4.0 %collective-permute-start = (f32[8,3,3,128]{3,0,2,1:T(8,128)S(1)}, f32[8,3,3,128]{3,0,2,1:T(8,128)S(1)}, u32[]{:S(2)}, u32[]{:S(2)}) collective-permute-start(f32[8,3,3,128]{3,0,2,1:T(8,128)S(1)} %copy.59), channel_id=1, source_target_pairs={{0,4},{4,8},{8,12},{12,16},{16,20},{20,24},{24,28},{28,0},{1,5},{5... | collective-permute-start | bytes 110600 | tf_op jit(solution)/shard_map/ppermute | solution.py:17
  58.3 6.7 %collective-permute-start.1 = (f32[8,3,3,128]{3,0,2,1:T(8,128)S(1)}, f32[8,3,3,128]{3,0,2,1:T(8,128)S(1)}, u32[]{:S(2)}, u32[]{:S(2)}) collective-permute-start(f32[8,3,3,128]{3,0,2,1:T(8,128)S(1)} %copy.60), channel_id=1, source_target_pairs={{4,0},{8,4},{12,8},{16,12},{20,16},{24,20},{28,24},{0,28},{5,1},{9... | collective-permute-start | bytes 110600 | tf_op jit(solution)/shard_map/ppermute | solution.py:18
  66.6 9.5 %copy-start = (f32[8,3,3,128]{2,3,1,0:T(8,128)S(1)}, f32[8,3,3,128]{2,3,1,0:T(8,128)}, u32[]{:S(2)}) copy-start(f32[8,3,3,128]{2,3,1,0:T(8,128)} %copy.61) | copy-start | bytes 110596
  66.7 9.5 %copy-start.1 = (f32[8,3,3,128]{2,3,1,0:T(8,128)S(1)}, f32[8,3,3,128]{2,3,1,0:T(8,128)}, u32[]{:S(2)}) copy-start(f32[8,3,3,128]{2,3,1,0:T(8,128)} %copy.62) | copy-start | bytes 110596
  68.2 4.5 %collective-permute-start.3 = (f32[8,3,262,3]{2,0,3,1:T(8,128)S(1)}, f32[8,3,262,3]{2,0,3,1:T(8,128)S(1)}, u32[]{:S(2)}, u32[]{:S(2)}) collective-permute-start(f32[8,3,262,3]{2,0,3,1:T(8,128)S(1)} %copy.64), channel_id=1, source_target_pairs={{1,0},{2,1},{3,2},{5,4},{6,5},{7,6},{9,8},{10,9},{11,10},{13,12},{... | collective-permute-start | bytes 226376 | tf_op jit(solution)/shard_map/ppermute | solution.py:18
  70.1 6.1 %collective-permute-start.2 = (f32[8,3,262,3]{2,0,3,1:T(8,128)S(1)}, f32[8,3,262,3]{2,0,3,1:T(8,128)S(1)}, u32[]{:S(2)}, u32[]{:S(2)}) collective-permute-start(f32[8,3,262,3]{2,0,3,1:T(8,128)S(1)} %copy.63), channel_id=1, source_target_pairs={{0,1},{1,2},{2,3},{4,5},{5,6},{6,7},{8,9},{9,10},{10,11},{12,13},{... | collective-permute-start | bytes 226376 | tf_op jit(solution)/shard_map/ppermute | solution.py:17
where the time goes:
time: 93.8 us; the launch traced here: 93.3 us
  blocking collectives  30.5 us (33%)
  other arithmetic  29.2 us (31%)
  local copies, waits for them, and re-layouts  18.3 us (20%)
  waiting for transfers between devices  6.91 us (7%)
  starting transfers between devices  6.58 us (7%)
  between operations  1 us (1%)
    all_gather x1, blocking collectives, local(): lax.all_gather(packed, 'az', axis=1, tiled=True)  30.5 us
    mul x1, other arithmetic, local(): sweep_one = sweep_one * inside  6.44 us
    broadcast_in_dim x1, other arithmetic, local(): base_reluct = lookup(material, nu_table)[None]  5.65 us
    broadcast_in_dim x1, other arithmetic, local(): saturation = lookup(material, sat_table)[None]  5.51 us
    slice x3, local copies, waits for them, and re-layouts, with_halo(): last = lax.slice_in_dim(x, length - width, length, axis=dim)  4.09 us
    unnamed x13, local copies, waits for them, and re-layouts  3.82 us
    concatenate x1, other arithmetic, with_halo(): x = jnp.concatenate([before, x, after], axis=dim)  3.79 us
    ppermute x2, waiting for transfers between devices, with_halo(): after = lax.ppermute(first, axis, down)  3.48 us
  transfers between devices with their start and end apart: 4, of which 2 were waited for; matrix products, arithmetic and copies ran while one was open for 4% of the time, Pallas kernels for 0%

commit v1 on v0

v1 whole, which is shorter than its diff:
```python
import functools

import jax
import jax.numpy as jnp
from jax import lax
from jax.experimental import pallas as pl
from jax.experimental.pallas import tpu as pltpu
from jax.sharding import PartitionSpec as P

sigma_term = 1.0
halo = 3
low_own, high_own = 6, 5
slot = low_own + high_own
f32 = jnp.float32
VMEM = pl.BlockSpec(memory_space=pltpu.VMEM)
SMEM = pl.BlockSpec(memory_space=pltpu.SMEM)


def params(mib=48):
    return pltpu.CompilerParams(vmem_limit_bytes=mib * 1024 * 1024)


def rim_rows(fields, layers):
    return halo * (fields + layers) + fields


def round_up(n, m):
    return (n + m - 1) // m * m


def slot_base(j, cols):
    per = cols // slot
    return (j // per) * cols + (j % per) * slot


def lookup(material, table):
    values = [table[e] for e in range(table.shape[0])]
    bit = 1
    while len(values) > 1:
        take = (material & bit) != 0
        values = [jnp.where(take, values[i + 1], values[i]) for i in range(0, len(values), 2)]
        bit *= 2
    return values[0]


def half_reluct(base, saturation, flux_sq):
    return (0.5 * base) * (1.0 + saturation * flux_sq / (1.0 + flux_sq))


def sweep_cells(coef, field, source, moves):
    layers = len(coef)
    out = [[None] * layers for _ in field]
    for l in range(layers):
        centre = coef[l]
        total = jnp.full_like(centre, sigma_term)
        num = [source[c][l] for c in range(len(field))]
        for move_coef, move_field in moves:
            w = centre + move_coef(l)
            total = total + w
            for c in range(len(field)):
                num[c] = num[c] + w * move_field(c, l)
        for other in (l + 1, l - 1):
            if 0 <= other < layers:
                w = centre + coef[other]
                total = total + w
                for c in range(len(field)):
                    num[c] = num[c] + w * field[c][other]
            else:
                total = total + centre
        inverse = 1.0 / total
        for c in range(len(field)):
            out[c][l] = num[c] * inverse
    return out


def pack_kernel(
    cycle, off_ref, pot_ref, cur_ref, mat_ref, flux_ref, jit_ref, strips_ref, re_ref, ro_ref, pan_ref, slots_ref
):
    fields, layers = pot_ref.shape[0], mat_ref.shape[0]
    rows, cols = mat_ref.shape[1:]
    total = 2 * fields + layers
    per = cols // slot
    groups = -(-total // per)
    odd = lax.rem(lax.axis_index("rad"), 2) == 1

    panels = flux_ref.shape[1]
    where = jit_ref[...] + off_ref[0]
    where = jnp.where(where >= cycle, where - cycle, where).astype(f32)
    for h in range(panels // 128):
        at = h * (fields + 1)
        pan_ref[at : at + fields, :] = flux_ref[:, h * 128 : (h + 1) * 128]
        pan_ref[at + fields : at + fields + 1, :] = where[:, h * 128 : (h + 1) * 128]

    lane = lax.broadcasted_iota(jnp.int32, (8, cols), 1)

    @pl.loop(0, rows // 8, unroll=2)
    def _(i):
        at = pl.ds(pl.multiple_of(i * 8, 8), 8)
        for g in range(groups):
            acc = None
            for k in range(min(per, total - g * per)):
                j = g * per + k
                if j < fields:
                    x = pot_ref[j, at, :]
                elif j < fields + layers:
                    x = mat_ref[j - fields, at, :].astype(f32)
                else:
                    x = cur_ref[j - fields - layers, at, :]
                x = pltpu.roll(x, (k * slot + high_own) % cols, 1)
                acc = x if acc is None else jnp.where(lane >= k * slot, x, acc)
            slots_ref[g, at, :] = acc

    for g in range(groups):
        strips_ref[g * cols : (g + 1) * cols, :] = slots_ref[g].T
    for j in range(total):
        b = slot_base(j, cols)
        if j < fields + layers:
            left, right, n, to = b + high_own, b + high_own - halo, halo, halo * j
        else:
            left, right, n, to = b + high_own, b + high_own - 1, 1, halo * (fields + layers) + j - fields - layers
        lo, hi = strips_ref[left : left + n, :], strips_ref[right : right + n, :]
        re_ref[to : to + n, :] = jnp.where(odd, lo, hi)
        ro_ref[to : to + n, :] = jnp.where(odd, hi, lo)


def pack(offset, pot, cur, mat, flux, jitter, cycle):
    fields, rows, cols = pot.shape
    layers = mat.shape[0]
    total = 2 * fields + layers
    groups = -(-total // (cols // slot))
    send = round_up(rim_rows(fields, layers), 8)
    panels = flux.shape[1]
    return pl.pallas_call(
        functools.partial(pack_kernel, cycle),
        out_shape=[
            jax.ShapeDtypeStruct((groups * cols, rows), f32),
            jax.ShapeDtypeStruct((send, rows), f32),
            jax.ShapeDtypeStruct((send, rows), f32),
            jax.ShapeDtypeStruct((panels // 128 * (fields + 1), 128), f32),
        ],
        in_specs=[SMEM] + [VMEM] * 5,
        out_specs=[VMEM] * 4,
        scratch_shapes=[pltpu.VMEM((groups, rows, cols), f32)],
        compiler_params=params(),
        cost_estimate=pl.CostEstimate(flops=40_000_000, bytes_accessed=3_000_000, transcendentals=0),
        name="pack_columns",
    )(offset, pot, cur, mat, flux, jitter)


def middle_kernel(
    n_pans, strips_ref, re_ref, ro_ref, pt, pb, ct, cb, mt, mb, *refs
):
    pan_refs, (ext_ref, even_ref, odd_ref, pans_ref, up_ref, down_ref) = refs[:n_pans], refs[n_pans:]
    fields, layers = pt.shape[0], mt.shape[0]
    rows = strips_ref.shape[1]
    cols = pt.shape[2]
    total = 2 * fields + layers
    odd_r = lax.rem(lax.axis_index("rad"), 2) == 1
    odd_a = lax.rem(lax.axis_index("az"), 2) == 1
    scalars = halo * (fields + layers)

    at = 0
    for ref in pan_refs:
        pans_ref[at : at + ref.shape[0], :] = ref[...]
        at += ref.shape[0]

    lane = lax.broadcasted_iota(jnp.int32, (16, 128), 1)
    up = down = None
    for j in range(total):
        b = slot_base(j, cols)
        ext_ref[j, 0:8, :] = strips_ref[b + high_own - 2 : b + high_own + 6, :]
        ext_ref[j, 8:16, :] = strips_ref[b : b + 8, :]
        if j < fields + layers:
            s = halo * j
            ext_ref[j, 0:2, :] = jnp.where(odd_r, re_ref[s + 1 : s + 3, :], ro_ref[s + 1 : s + 3, :])
            ext_ref[j, 13:16, :] = jnp.where(odd_r, ro_ref[s : s + 3, :], re_ref[s : s + 3, :])
        else:
            s = scalars + j - fields - layers
            ext_ref[j, 1:2, :] = jnp.where(odd_r, re_ref[s : s + 1, :], ro_ref[s : s + 1, :])
            ext_ref[j, 13:14, :] = jnp.where(odd_r, ro_ref[s : s + 1, :], re_ref[s : s + 1, :])
        first = pltpu.roll(ext_ref[j, :, 0:128], 4 * j, 1)
        last = pltpu.roll(ext_ref[j, :, rows - 128 : rows], (4 * j + halo) % 128, 1)
        up = first if up is None else jnp.where(lane >= 4 * j, first, up)
        down = last if down is None else jnp.where(lane >= 4 * j, last, down)

    for j in range(fields):
        up_ref[halo * j : halo * j + halo, :] = pt[j, 0:halo, :]
        down_ref[halo * j : halo * j + halo, :] = pb[j, 8 - halo : 8, :]
        up_ref[scalars + j : scalars + j + 1, :] = ct[j, 0:1, :]
        down_ref[scalars + j : scalars + j + 1, :] = cb[j, 7:8, :]
    for l in range(layers):
        s = halo * (fields + l)
        up_ref[s : s + halo, :] = mt[l, 0:halo, :].astype(f32)
        down_ref[s : s + halo, :] = mb[l, 8 - halo : 8, :].astype(f32)
    n = up_ref.shape[0]
    even_ref[0:n, :] = jnp.where(odd_a, up_ref[...], down_ref[...])
    odd_ref[0:n, :] = jnp.where(odd_a, down_ref[...], up_ref[...])
    even_ref[n : n + 16, :] = jnp.where(odd_a, up, down)
    odd_ref[n : n + 16, :] = jnp.where(odd_a, down, up)
    even_ref[n + 16 :, :] = pans_ref[...]
    odd_ref[n + 16 :, :] = pans_ref[...]


def edge_specs(lead, rows, cols):
    last = rows // 8 - 1
    return [
        pl.BlockSpec((lead, 8, cols), lambda i: (0, 0, 0)),
        pl.BlockSpec((lead, 8, cols), lambda i: (0, last, 0)),
    ]


def whole(shape):
    return pl.BlockSpec(shape, lambda i: (0,) * len(shape))


def middle(strips, re_got, ro_got, pot, cur, mat, pans):
    fields, rows, cols = pot.shape
    layers = mat.shape[0]
    total = 2 * fields + layers
    send = round_up(rim_rows(fields, layers), 8)
    pan_rows = sum(p.shape[0] for p in pans)
    out_shape = [
        jax.ShapeDtypeStruct((total, 16, rows), f32),
        jax.ShapeDtypeStruct((send + 16 + pan_rows, cols), f32),
        jax.ShapeDtypeStruct((send + 16 + pan_rows, cols), f32),
        jax.ShapeDtypeStruct((pan_rows, cols), f32),
    ]
    return pl.pallas_call(
        functools.partial(middle_kernel, len(pans)),
        grid=(1,),
        out_shape=out_shape,
        in_specs=[whole(strips.shape), whole(re_got.shape), whole(ro_got.shape)]
        + edge_specs(fields, rows, cols)
        + edge_specs(fields, rows, cols)
        + edge_specs(layers, rows, cols)
        + [whole(p.shape) for p in pans],
        out_specs=[whole(o.shape) for o in out_shape],
        scratch_shapes=[pltpu.VMEM((send, cols), f32), pltpu.VMEM((send, cols), f32)],
        compiler_params=params(),
        cost_estimate=pl.CostEstimate(flops=5_000_000, bytes_accessed=1_000_000, transcendentals=0),
        name="pack_rows",
    )(strips, re_got, ro_got, pot, pot, cur, cur, mat, mat, *pans)


def tile_kernel(nu_ref, sat_ref, pot_hbm, cur_ref, mat_ref, out_ref, pot_ref, coef_ref, one_ref, sem):
    fields, rows, cols = out_ref.shape
    layers = mat_ref.shape[0]
    comps = fields // layers
    copy = pltpu.make_async_copy(pot_hbm, pot_ref.at[:, 8 : 8 + rows, :], sem)
    copy.start()
    blank = jnp.zeros((8, cols), f32)
    for j in range(fields):
        for ref in (pot_ref, one_ref):
            ref[j, 0:8, :] = blank
            ref[j, 8 + rows : 16 + rows, :] = blank
    for l in range(layers):
        coef_ref[l, 0:8, :] = blank
        coef_ref[l, 8 + rows : 16 + rows, :] = blank
    copy.wait()

    def shifted(ref, j, i, step):
        return ref[j, pl.ds(i * 8 + 8 + step, 8), :]

    def right(x):
        return pltpu.roll(x, cols - 1, 1)

    def left(x):
        return pltpu.roll(x, 1, 1)

    @pl.loop(0, rows // 8, unroll=2)
    def _(i):
        own = pl.ds(pl.multiple_of(i * 8, 8), 8)
        for l in range(layers):
            flux_sq = None
            for c in range(comps):
                centre = shifted(pot_ref, c * layers + l, i, 0)
                az = shifted(pot_ref, c * layers + l, i, 1) - centre
                rad = right(centre) - centre
                part = az * az + rad * rad
                flux_sq = part if flux_sq is None else flux_sq + part
            material = mat_ref[l, own, :]
            coef_ref[l, pl.ds(pl.multiple_of(i * 8 + 8, 8), 8), :] = half_reluct(
                lookup(material, nu_ref), lookup(material, sat_ref), flux_sq
            )

    def sweep(field_ref, store):
        @pl.loop(0, rows // 8, unroll=2)
        def _(i):
            own = pl.ds(pl.multiple_of(i * 8, 8), 8)
            coef = [shifted(coef_ref, l, i, 0) for l in range(layers)]
            field = [[shifted(field_ref, c * layers + l, i, 0) for l in range(layers)] for c in range(comps)]
            source = [[cur_ref[c * layers + l, own, :] for l in range(layers)] for c in range(comps)]
            moves = []
            for step in (1, -1):
                moves.append(
                    (
                        lambda l, step=step: shifted(coef_ref, l, i, step),
                        lambda c, l, step=step: shifted(field_ref, c * layers + l, i, step),
                    )
                )
            for turn in (right, left):
                moves.append((lambda l, turn=turn: turn(coef[l]), lambda c, l, turn=turn: turn(field[c][l])))
            new = sweep_cells(coef, field, source, moves)
            for c in range(comps):
                for l in range(layers):
                    store(c * layers + l, i, new[c][l])

    def store_one(j, i, x):
        one_ref[j, pl.ds(pl.multiple_of(i * 8 + 8, 8), 8), :] = x

    def store_two(j, i, x):
        out_ref[j, pl.ds(pl.multiple_of(i * 8, 8), 8), :] = x

    sweep(pot_ref, store_one)
    sweep(one_ref, store_two)


def tile(nu, sat, pot, cur, mat):
    fields, rows, cols = pot.shape
    layers = mat.shape[0]
    return pl.pallas_call(
        tile_kernel,
        out_shape=jax.ShapeDtypeStruct(pot.shape, f32),
        in_specs=[SMEM, SMEM, pl.BlockSpec(memory_space=pl.ANY), VMEM, VMEM],
        out_specs=VMEM,
        scratch_shapes=[
            pltpu.VMEM((fields, rows + 16, cols), f32),
            pltpu.VMEM((layers, rows + 16, cols), f32),
            pltpu.VMEM((fields, rows + 16, cols), f32),
            pltpu.SemaphoreType.DMA,
        ],
        compiler_params=params(),
        cost_estimate=pl.CostEstimate(flops=40_000_000, bytes_accessed=4_000_000, transcendentals=0),
        name="tile",
    )(nu, sat, pot, cur, mat)


def deposit(air_ref, vals_ref, blocks, fields, rows, base, cycle):
    lanes = vals_ref.shape[1]
    vals_ref[...] = jnp.zeros_like(vals_ref)
    for t, (ref, at) in enumerate(blocks):
        vals_ref[0 : fields + 1, t * 128 : (t + 1) * 128] = ref[at : at + fields + 1, :]
    values = vals_ref[...]
    local = vals_ref[fields : fields + 1, :].astype(jnp.int32) - base
    local = jnp.where(local < -1, local + cycle, local)
    local = jnp.where(local > rows, local - cycle, local)
    spot = lax.broadcasted_iota(jnp.int32, (rows, lanes), 0)
    onehot = jnp.where(spot == local, 1.0, 0.0).astype(jnp.bfloat16)
    high = values.astype(jnp.bfloat16)
    rest = values - high.astype(f32)
    mid = rest.astype(jnp.bfloat16)
    low = (rest - mid.astype(f32)).astype(jnp.bfloat16)
    parts = lax.dot_general(
        jnp.concatenate([high, mid, low], axis=0),
        onehot,
        (((1,), (1,)), ((), ())),
        preferred_element_type=f32,
    )
    air_ref[:, 0:rows] = parts[0:16] + parts[16:32] + parts[32:48]
    after = jnp.sum(jnp.where(local == rows, values, 0.0), axis=1, keepdims=True)
    before = jnp.sum(jnp.where((local == -1) | (local == cycle - 1), values, 0.0), axis=1, keepdims=True)
    lane = lax.broadcasted_iota(jnp.int32, (16, 128), 1)
    air_ref[:, rows : rows + 128] = jnp.where(lane == 0, after, jnp.where(lane == 127, before, 0.0))


def rim_kernel(
    cycle, nu_ref, sat_ref, main_ref, even_ref, odd_ref, two_ref, pans_ref, ext_ref, pt, pb, ct, cb, mt, mb,
    out_ref, rows_ref, cols_ref, vals_ref, air_ref, back_ref,
):
    fields, layers = pt.shape[0], mt.shape[0]
    comps = fields // layers
    rows, cols = main_ref.shape[1:]
    total = 2 * fields + layers
    scalars = halo * (fields + layers)
    r, a = lax.axis_index("rad"), lax.axis_index("az")
    size = lax.axis_size("rad")
    odd_a = lax.rem(a, 2) == 1
    send = round_up(rim_rows(fields, layers), 8)

    stator = (r == size // 2) | (r == size // 2 - 1)
    air_ref[...] = jnp.zeros_like(air_ref)

    @pl.when(stator)
    def _():
        n = pans_ref.shape[0]
        blocks = []
        for ref, at in ((pans_ref, 0), (even_ref, send + 16), (odd_ref, send + 16), (two_ref, 0)):
            blocks += [(ref, at + k * (fields + 1)) for k in range(n // (fields + 1))]
        deposit(air_ref, vals_ref, blocks, fields, rows, a * rows, cycle)

    def before(at, n):
        return jnp.where(odd_a, even_ref[at : at + n, :], odd_ref[at : at + n, :])

    def after(at, n):
        return jnp.where(odd_a, odd_ref[at : at + n, :], even_ref[at : at + n, :])

    rows_ref[...] = jnp.zeros_like(rows_ref)
    for j in range(total):
        if j < fields + layers:
            rows_ref[j, 8 - halo : 8, :] = before(halo * j, halo)
            rows_ref[j, 24 : 24 + halo, :] = after(halo * j, halo)
        else:
            s = scalars + j - fields - layers
            rows_ref[j, 7:8, :] = before(s, 1)
            rows_ref[j, 24:25, :] = after(s, 1)
        if j < fields:
            top, bottom = pt[j], pb[j]
        elif j < fields + layers:
            top, bottom = mt[j - fields].astype(f32), mb[j - fields].astype(f32)
        else:
            top, bottom = ct[j - fields - layers], cb[j - fields - layers]
        rows_ref[j, 8:16, :] = top
        rows_ref[j, 16:24, :] = bottom

    def solve(get, axis_az, axis_rad, inside, source):
        pot = [[get(c * layers + l) for l in range(layers)] for c in range(comps)]
        if inside is not None:
            pot = [[jnp.where(inside, x, 0.0) for x in part] for part in pot]
        shape = pot[0][0].shape

        def move(x, axis, step):
            return pltpu.roll(x, (-step) % shape[axis], axis)

        coef = []
        for l in range(layers):
            flux_sq = None
            for c in range(comps):
                az = move(pot[c][l], axis_az, 1) - pot[c][l]
                rad = move(pot[c][l], axis_rad, 1) - pot[c][l]
                part = az * az + rad * rad
                flux_sq = part if flux_sq is None else flux_sq + part
            material = get(fields + l).astype(jnp.int32)
            k = half_reluct(lookup(material, nu_ref), lookup(material, sat_ref), flux_sq)
            coef.append(k if inside is None else jnp.where(inside, k, 0.0))

        moved = {}

        def moves_of(field):
            table = []
            for axis in (axis_az, axis_rad):
                for step in (1, -1):
                    def coef_at(l, axis=axis, step=step):
                        key = (l, axis, step)
                        if key not in moved:
                            moved[key] = move(coef[l], axis, step)
                        return moved[key]

                    table.append((coef_at, lambda c, l, axis=axis, step=step: move(field[c][l], axis, step)))
            return table

        one = sweep_cells(coef, pot, source, moves_of(pot))
        if inside is not None:
            one = [[jnp.where(inside, x, 0.0) for x in part] for part in one]
        return sweep_cells(coef, one, source, moves_of(one))

    source = [[rows_ref[fields + layers + c * layers + l] for l in range(layers)] for c in range(comps)]
    fixed_rows = solve(lambda j: rows_ref[j], 0, 1, None, source)

    lane = lax.broadcasted_iota(jnp.int32, (16, 128), 1)
    corner_before, corner_after = before(send, 16), after(send, 16)
    for j in range(total):
        cols_ref[j, :, 0:rows] = ext_ref[j]
        cols_ref[j, :, rows : rows + 128] = jnp.where(
            lane < 64,
            pltpu.roll(corner_after, (-4 * j) % 128, 1),
            pltpu.roll(corner_before, (128 - halo - 4 * j) % 128, 1),
        )
    column = lax.broadcasted_iota(jnp.int32, (16, rows + 128), 0)
    inside = ((column >= 2) | (r > 0)) & ((column < 13) | (r < size - 1))
    target = jnp.where(r == size // 2, 2, jnp.where(r == size // 2 - 1, 13, -1))
    source = []
    for c in range(comps):
        source.append([])
        for l in range(layers):
            j = c * layers + l
            source[c].append(cols_ref[fields + layers + j] + jnp.where(column == target, air_ref[j : j + 1, :], 0.0))
    fixed_cols = solve(lambda j: cols_ref[j], 1, 0, inside, source)

    for c in range(comps):
        for l in range(layers):
            j = c * layers + l
            back_ref[8 * j : 8 * j + 3, :] = fixed_cols[c][l][10:13, 0:rows]
            back_ref[8 * j + 3 : 8 * j + 5, :] = fixed_cols[c][l][2:4, 0:rows]
    turned = back_ref[...].T

    lane = lax.broadcasted_iota(jnp.int32, (rows, cols), 1)
    edge = (lane < 2) | (lane >= cols - 3)
    for c in range(comps):
        for l in range(layers):
            j = c * layers + l
            main_ref[j, 0:2, :] = fixed_rows[c][l][8:10]
            main_ref[j, rows - 3 : rows, :] = fixed_rows[c][l][21:24]
            out_ref[j] = jnp.where(edge, pltpu.roll(turned, (cols - 3 - 8 * j) % cols, 1), main_ref[j])


def rims(nu, sat, main, even_got, odd_got, two_got, pans, ext, pot, cur, mat, cycle):
    fields, rows, cols = pot.shape
    layers = mat.shape[0]
    total = 2 * fields + layers
    panels = 4 * pans.shape[0] // (fields + 1) * 128
    arrays = (main, even_got, odd_got, two_got, pans, ext)
    return pl.pallas_call(
        functools.partial(rim_kernel, cycle),
        grid=(1,),
        out_shape=jax.ShapeDtypeStruct(pot.shape, f32),
        in_specs=[SMEM, SMEM]
        + [whole(x.shape) for x in arrays]
        + edge_specs(fields, rows, cols)
        + edge_specs(fields, rows, cols)
        + edge_specs(layers, rows, cols),
        out_specs=whole(pot.shape),
        scratch_shapes=[
            pltpu.VMEM((total, 32, cols), f32),
            pltpu.VMEM((total, 16, rows + 128), f32),
            pltpu.VMEM((16, panels), f32),
            pltpu.VMEM((16, rows + 128), f32),
            pltpu.VMEM((128, rows), f32),
        ],
        compiler_params=params(),
        name="rims",
    )(nu, sat, *arrays, pot, pot, cur, cur, mat, mat)


def local(potential, current, material, nu_table, sat_table, panel_flux, panel_jitter, rotor_offset):
    comps, layers, rows, cols = potential.shape
    fields = comps * layers
    az, rad = lax.axis_size("az"), lax.axis_size("rad")
    cycle = rows * az
    pot = potential.reshape(fields, rows, cols)
    cur = current.reshape(fields, rows, cols)

    def swap(x, az_of, rad_of):
        pairs = [(a * rad + r, az_of(a) * rad + rad_of(r)) for a in range(az) for r in range(rad)]
        return lax.ppermute(x, ("az", "rad"), pairs)

    def same(i):
        return i

    def even(i):
        return i ^ 1

    def odd(i, n):
        return (i + 1) % n if i % 2 else (i - 1) % n

    strips, re_send, ro_send, pan = pack(
        rotor_offset, pot, cur, material, panel_flux, panel_jitter.reshape(1, -1), cycle
    )
    re_got = swap(re_send, same, even)
    ro_got = swap(ro_send, same, lambda r: odd(r, rad))
    pans = [pan]
    bit = az // 2
    while bit >= 4:
        held = pans[0] if len(pans) == 1 else jnp.concatenate(pans, axis=0)
        pans = [held, swap(held, lambda a, bit=bit: a ^ bit, same)]
        bit //= 2
    ext, even_send, odd_send, held = middle(strips, re_got, ro_got, pot, cur, material, pans)
    two_got = swap(held, lambda a: a ^ 2, same)
    even_got = swap(even_send, even, same)
    odd_got = swap(odd_send, lambda a: odd(a, az), same)
    main = tile(nu_table, sat_table, pot, cur, material)
    out = rims(
        nu_table, sat_table, main, even_got, odd_got, two_got, held, ext, pot, cur, material, cycle
    )
    return out.reshape(potential.shape)


def solution(mesh):
    placed = (
        P(None, None, "az", "rad"),
        P(None, None, "az", "rad"),
        P(None, "az", "rad"),
        P(),
        P(),
        P(None, "az"),
        P("az"),
        P(),
    )
    return jax.shard_map(
        local, mesh=mesh, in_specs=placed, out_specs=P(None, None, "az", "rad"), check_vma=False
    )
```

time: 93.8 us -> 30.2 us (0.32)
  the two profiles are of different devices: /device:TPU:30 before, /device:TPU:0 now
where the time goes in v1:
time: 30.2 us; the launch traced here: 29.9 us
  Pallas kernels  11.3 us (37%)
  starting transfers between devices  10.9 us (36%)
  local copies, waits for them, and re-layouts  4.94 us (16%)
  waiting for transfers between devices  2.03 us (7%)
  between operations  0.74 us (2%)
    ppermute x6, starting transfers between devices, swap(): return lax.ppermute(x, ('az', 'rad'), pairs)  10.9 us
    pallas_call x1, Pallas kernels, tile(): pl.pallas_call(tile_kernel, out_shape=jax.ShapeDtypeStruct(pot.shape, f32...  6.31 us
    unnamed x16, local copies, waits for them, and re-layouts  4.94 us
    pallas_call x1, Pallas kernels, rims(): pl.pallas_call(functools.partial(rim_kernel, cycle), grid=(1,), out_shape...  2.79 us
    ppermute x6, waiting for transfers between devices, swap(): return lax.ppermute(x, ('az', 'rad'), pairs)  2.03 us
    pallas_call x1, Pallas kernels, pack(): pl.pallas_call(functools.partial(pack_kernel, cycle), out_shape=[jax.Shap...  1.96 us
  transfers between devices with their start and end apart: 6, of which 1 were waited for; matrix products, arithmetic and copies ran while one was open for 0% of the time, Pallas kernels for 21%

profile of v1, /device:TPU:0, one launch (start us, length us, event | category | flops | bytes accessed | tf_op | source)
XLA Modules:
  0.0 29.9 jit_solution(752930624074430018)
XLA Ops:
  0.7 0.0 copy-start
  0.7 1.3 %copy-done = f32[3,3,256,128]{3,2,1,0:T(8,128)S(1)} copy-done((f32[3,3,256,128]{3,2,1,0:T(8,128)S(1)}, f32[3,3,256,128]{3,2,1,0:T(8,128)}, u32[]{:S(2)}) %copy-start) | copy-done | bytes 1179672
  1.9 1.3 %copy-done.2 = f32[3,3,256,128]{3,2,1,0:T(8,128)S(1)} copy-done((f32[3,3,256,128]{3,2,1,0:T(8,128)S(1)}, f32[3,3,256,128]{3,2,1,0:T(8,128)}, u32[]{:S(2)}) %copy-start.2) | copy-done | bytes 1179672
  3.2 1.0 %copy-done.3 = s32[3,256,128]{2,1,0:T(8,128)S(1)} copy-done((s32[3,256,128]{2,1,0:T(8,128)S(1)}, s32[3,256,128]{2,1,0:T(8,128)}, u32[]{:S(2)}) %copy-start.3) | copy-done | bytes 393240
  4.2 0.7 %copy-done.4 = f32[9,256]{1,0:T(8,128)S(1)} copy-done((f32[9,256]{1,0:T(8,128)S(1)}, f32[9,256]{1,0:T(8,128)}, u32[]{:S(2)}) %copy-start.4) | copy-done | bytes 9240
  4.9 0.7 %copy-done.7 = s32[256]{0:T(256)S(1)} copy-done((s32[256]{0:T(256)S(1)}, s32[256]{0:T(256)}, u32[]{:S(2)}) %copy-start.7) | copy-done | bytes 1048
  5.6 2.0 %pack_columns.1 = (f32[256,256]{1,0:T(8,128)S(1)}, f32[48,256]{1,0:T(8,128)S(1)}, f32[48,256]{1,0:T(8,128)S(1)}, f32[20,128]{1,0:T(8,128)S(1)}) custom-call(s32[1]{0:T(128)S(6)} %copy.9.off_ref, f32[9,256,128]{2,1,0:T(8,128)S(1)} %bitcast.4, f32[9,256,128]{2,1,0:T(8,128)S(1)} %bitcast.10, s32[3,256,128]{2,1,0:T(8,128)S(1)} %copy-done.3, ...), custom_call_target="tpu_custom_call" | custom-call | flops 40000000 | bytes 3000000 | tf_op jit(solution)/shard_map/pack_columns/pallas_call | solution.py:133
  7.6 0.5 %collective-permute-start = (f32[48,256]{1,0:T(8,128)S(1)}, f32[48,256]{1,0:T(8,128)S(1)}, u32[]{:S(2)}, u32[]{:S(2)}) collective-permute-start(f32[48,256]{1,0:T(8,128)S(1)} %get-tuple-element.14), channel_id=1, source_target_pairs={{0,1},{1,0},{2,3},{3,2},{4,5},{5,4},{6,7},{7,6},{8,9},{9,8},{10,11... | collective-permute-start | bytes 147464 | tf_op jit(solution)/shard_map/ppermute | solution.py:534
  8.1 2.6 %collective-permute-start.1 = (f32[48,256]{1,0:T(8,128)S(1)}, f32[48,256]{1,0:T(8,128)S(1)}, u32[]{:S(2)}, u32[]{:S(2)}) collective-permute-start(f32[48,256]{1,0:T(8,128)S(1)} %get-tuple-element.15), channel_id=1, source_target_pairs={{0,3},{1,2},{2,1},{3,0},{4,7},{5,6},{6,5},{7,4},{8,11},{9,10},{10,... | collective-permute-start | bytes 147464 | tf_op jit(solution)/shard_map/ppermute | solution.py:534
  10.7 2.6 %collective-permute-start.2 = (f32[20,128]{1,0:T(8,128)S(1)}, f32[20,128]{1,0:T(8,128)S(1)}, u32[]{:S(2)}, u32[]{:S(2)}) collective-permute-start(f32[20,128]{1,0:T(8,128)S(1)} %get-tuple-element.16.refs_0_), channel_id=1, source_target_pairs={{0,16},{1,17},{2,18},{3,19},{4,20},{5,21},{6,22},{7,23},{8,24},{9,... | collective-permute-start | bytes 30728 | tf_op jit(solution)/shard_map/ppermute | solution.py:534
  13.3 2.0 %collective-permute-done.2.refs_1_ = f32[20,128]{1,0:T(8,128)S(1)} collective-permute-done((f32[20,128]{1,0:T(8,128)S(1)}, f32[20,128]{1,0:T(8,128)S(1)}, u32[]{:S(2)}, u32[]{:S(2)}) %collective-permute-start.2) | collective-permute-done | bytes 10272 | tf_op jit(solution)/shard_map/ppermute | solution.py:534
  15.3 0.0 collective-permute-done.re_ref
  15.3 0.0 collective-permute-done.1.ro_ref
  15.3 0.0 copy-start.5
  15.3 0.0 copy-start.6
  15.4 0.2 pack_rows.1
  15.6 1.6 %collective-permute-start.3 = (f32[104,128]{1,0:T(8,128)S(1)}, f32[104,128]{1,0:T(8,128)S(1)}, u32[]{:S(2)}, u32[]{:S(2)}) collective-permute-start(f32[104,128]{1,0:T(8,128)S(1)} %get-tuple-element.17), channel_id=1, source_target_pairs={{0,4},{1,5},{2,6},{3,7},{4,0},{5,1},{6,2},{7,3},{8,12},{9,13},{10,... | collective-permute-start | bytes 159752 | tf_op jit(solution)/shard_map/ppermute | solution.py:534
  17.1 3.6 %collective-permute-start.4 = (f32[104,128]{1,0:T(8,128)S(1)}, f32[104,128]{1,0:T(8,128)S(1)}, u32[]{:S(2)}, u32[]{:S(2)}) collective-permute-start(f32[104,128]{1,0:T(8,128)S(1)} %get-tuple-element.18), channel_id=1, source_target_pairs={{0,28},{1,29},{2,30},{3,31},{4,8},{5,9},{6,10},{7,11},{8,4},{9,5},... | collective-permute-start | bytes 159752 | tf_op jit(solution)/shard_map/ppermute | solution.py:534
  20.7 0.0 collective-permute-start.5
  20.7 6.3 %tile.1.main_ref = f32[9,256,128]{2,1,0:T(8,128)S(1)} custom-call(f32[8]{0:T(128)S(1)} %copy-done.5, f32[8]{0:T(128)S(1)} %copy-done.6, f32[9,256,128]{2,1,0:T(8,128)S(1)} %bitcast.7, f32[9,256,128]{2,1,0:T(8,128)S(1)} %bitcast.13, s32[3,256,128]{2,1,0:T(8,128)S(1)} %copy-done.3), custom_call_target="tpu_custom_call" | custom-call | flops 40000000 | bytes 4000000 | tf_op jit(solution)/shard_map/tile/pallas_call | solution.py:321
  27.0 0.0 collective-permute-done.5.two_ref
  27.1 0.0 collective-permute-done.3.even_ref
  27.1 0.0 collective-permute-done.4.odd_ref
  27.1 2.8 %rims.1 = f32[9,256,128]{2,1,0:T(8,128)} custom-call(f32[8]{0:T(128)S(1)} %copy-done.5, f32[8]{0:T(128)S(1)} %copy-done.6, f32[9,256,128]{2,1,0:T(8,128)S(1)} %tile.1.main_ref, f32[104,128]{1,0:T(8,128)S(1)} %collective-permute-done.3.even_ref, f32[104,128]{1,0:T(8,128)S(1)} %collective-permute-done.4.odd_ref, f32[40,128]{1,0:T(8,128)S(1)} %collective-permute-done.5.two_ref, ...), custom_call_target="tpu_custom_call" | custom-call | tf_op jit(solution)/shard_map/rims/pallas_call | solution.py:502
  (8 shorter events, 0.0 us)
Async XLA Ops:
  0.7 1.3 %copy-start = (f32[3,3,256,128]{3,2,1,0:T(8,128)S(1)}, f32[3,3,256,128]{3,2,1,0:T(8,128)}, u32[]{:S(2)}) copy-start(f32[3,3,256,128]{3,2,1,0:T(8,128)} %param.8) | copy-start | bytes 3538948
  1.9 1.3 %copy-start.2 = (f32[3,3,256,128]{3,2,1,0:T(8,128)S(1)}, f32[3,3,256,128]{3,2,1,0:T(8,128)}, u32[]{:S(2)}) copy-start(f32[3,3,256,128]{3,2,1,0:T(8,128)} %param.9) | copy-start | bytes 3538948
  3.2 1.0 %copy-start.3 = (s32[3,256,128]{2,1,0:T(8,128)S(1)}, s32[3,256,128]{2,1,0:T(8,128)}, u32[]{:S(2)}) copy-start(s32[3,256,128]{2,1,0:T(8,128)} %mb.3) | copy-start | bytes 1179652
  4.2 0.7 %copy-start.4 = (f32[9,256]{1,0:T(8,128)S(1)}, f32[9,256]{1,0:T(8,128)}, u32[]{:S(2)}) copy-start(f32[9,256]{1,0:T(8,128)} %flux_ref.1) | copy-start | bytes 27652
  4.9 0.7 %copy-start.7 = (s32[256]{0:T(256)S(1)}, s32[256]{0:T(256)}, u32[]{:S(2)}) copy-start(s32[256]{0:T(256)} %param.14) | copy-start | bytes 3076
  7.6 7.8 %collective-permute-start = (f32[48,256]{1,0:T(8,128)S(1)}, f32[48,256]{1,0:T(8,128)S(1)}, u32[]{:S(2)}, u32[]{:S(2)}) collective-permute-start(f32[48,256]{1,0:T(8,128)S(1)} %get-tuple-element.14), channel_id=1, source_target_pairs={{0,1},{1,0},{2,3},{3,2},{4,5},{5,4},{6,7},{7,6},{8,9},{9,8},{10,11... | collective-permute-start | bytes 147464 | tf_op jit(solution)/shard_map/ppermute | solution.py:534
  8.1 7.3 %collective-permute-start.1 = (f32[48,256]{1,0:T(8,128)S(1)}, f32[48,256]{1,0:T(8,128)S(1)}, u32[]{:S(2)}, u32[]{:S(2)}) collective-permute-start(f32[48,256]{1,0:T(8,128)S(1)} %get-tuple-element.15), channel_id=1, source_target_pairs={{0,3},{1,2},{2,1},{3,0},{4,7},{5,6},{6,5},{7,4},{8,11},{9,10},{10,... | collective-permute-start | bytes 147464 | tf_op jit(solution)/shard_map/ppermute | solution.py:534
  10.7 4.6 %collective-permute-start.2 = (f32[20,128]{1,0:T(8,128)S(1)}, f32[20,128]{1,0:T(8,128)S(1)}, u32[]{:S(2)}, u32[]{:S(2)}) collective-permute-start(f32[20,128]{1,0:T(8,128)S(1)} %get-tuple-element.16.refs_0_), channel_id=1, source_target_pairs={{0,16},{1,17},{2,18},{3,19},{4,20},{5,21},{6,22},{7,23},{8,24},{9,... | collective-permute-start | bytes 30728 | tf_op jit(solution)/shard_map/ppermute | solution.py:534
  15.3 5.4 %copy-start.1 = (f32[3,3,256,128]{3,2,1,0:T(8,128)S(1)}, f32[3,3,256,128]{3,2,1,0:T(8,128)}, u32[]{:S(2)}) copy-start(f32[3,3,256,128]{3,2,1,0:T(8,128)} %param.8) | copy-start | bytes 3538948
  15.3 5.4 %copy-start.5 = (f32[8]{0:T(128)S(1)}, f32[8]{0:T(128)}, u32[]{:S(2)}) copy-start(f32[8]{0:T(128)} %nu_ref.3) | copy-start | bytes 100
  15.3 5.4 %copy-start.6 = (f32[8]{0:T(128)S(1)}, f32[8]{0:T(128)}, u32[]{:S(2)}) copy-start(f32[8]{0:T(128)} %sat_ref.3) | copy-start | bytes 100
  15.6 11.5 %collective-permute-start.3 = (f32[104,128]{1,0:T(8,128)S(1)}, f32[104,128]{1,0:T(8,128)S(1)}, u32[]{:S(2)}, u32[]{:S(2)}) collective-permute-start(f32[104,128]{1,0:T(8,128)S(1)} %get-tuple-element.17), channel_id=1, source_target_pairs={{0,4},{1,5},{2,6},{3,7},{4,0},{5,1},{6,2},{7,3},{8,12},{9,13},{10,... | collective-permute-start | bytes 159752 | tf_op jit(solution)/shard_map/ppermute | solution.py:534
  17.1 9.9 %collective-permute-start.4 = (f32[104,128]{1,0:T(8,128)S(1)}, f32[104,128]{1,0:T(8,128)S(1)}, u32[]{:S(2)}, u32[]{:S(2)}) collective-permute-start(f32[104,128]{1,0:T(8,128)S(1)} %get-tuple-element.18), channel_id=1, source_target_pairs={{0,28},{1,29},{2,30},{3,31},{4,8},{5,9},{6,10},{7,11},{8,4},{9,5},... | collective-permute-start | bytes 159752 | tf_op jit(solution)/shard_map/ppermute | solution.py:534
  20.7 6.3 %collective-permute-start.5 = (f32[40,128]{1,0:T(8,128)S(1)}, f32[40,128]{1,0:T(8,128)S(1)}, u32[]{:S(2)}, u32[]{:S(2)}) collective-permute-start(f32[40,128]{1,0:T(8,128)S(1)} %get-tuple-element.19.pans_ref), channel_id=1, source_target_pairs={{0,8},{1,9},{2,10},{3,11},{4,12},{5,13},{6,14},{7,15},{8,0},{9,1},... | collective-permute-start | bytes 61448 | tf_op jit(solution)/shard_map/ppermute | solution.py:534

commit v2 on v0

v2 whole, which is shorter than its diff:
```python
import functools

import jax
import jax.numpy as jnp
from jax import lax
from jax.experimental import pallas as pl
from jax.experimental.pallas import tpu as pltpu
from jax.sharding import PartitionSpec as P

sigma_term = 1.0
LIMIT = 60
halo = 3
low_own, high_own = 6, 5
slot = low_own + high_own
f32 = jnp.float32
VMEM = pl.BlockSpec(memory_space=pltpu.VMEM)
SMEM = pl.BlockSpec(memory_space=pltpu.SMEM)
HBM = pl.BlockSpec(memory_space=pltpu.HBM)
ANY = pl.BlockSpec(memory_space=pl.ANY)


def params(mib=48):
    return pltpu.CompilerParams(vmem_limit_bytes=mib * 1024 * 1024)


def layout(fields, layers):
    depth = [halo] * fields + [halo - 1] * layers + [1] * fields
    return [(n, sum(depth[:j])) for j, n in enumerate(depth)]


def rim_rows(fields, layers):
    return halo * fields + (halo - 1) * layers + fields


def slot_base(j, cols):
    per = cols // slot
    return (j // per) * cols + (j % per) * slot


def lookup(material, table):
    values = [table[e] for e in range(table.shape[0])]
    bit = 1
    while len(values) > 1:
        take = (material & bit) != 0
        values = [jnp.where(take, values[i + 1], values[i]) for i in range(0, len(values), 2)]
        bit *= 2
    return values[0]


def half_reluct(base, saturation, flux_sq):
    return (0.5 * base) * (1.0 + saturation * flux_sq / (1.0 + flux_sq))


def sweep_cells(coef, field, source, moves):
    layers = len(coef)
    out = [[None] * layers for _ in field]
    for l in range(layers):
        centre = coef[l]
        total = jnp.full_like(centre, sigma_term)
        num = [source[c][l] for c in range(len(field))]
        for move_coef, move_field in moves:
            w = centre + move_coef(l)
            total = total + w
            for c in range(len(field)):
                num[c] = num[c] + w * move_field(c, l)
        for other in (l + 1, l - 1):
            if 0 <= other < layers:
                w = centre + coef[other]
                total = total + w
                for c in range(len(field)):
                    num[c] = num[c] + w * field[c][other]
            else:
                total = total + centre
        inverse = 1.0 / total
        for c in range(len(field)):
            out[c][l] = num[c] * inverse
    return out


def divisor(n, most):
    return max(d for d in range(1, most + 1) if n % d == 0)


def half_strength(centres, az_next, rad_next):
    total = None
    for centre, az, rad in zip(centres, az_next, rad_next):
        az, rad = az - centre, rad - centre
        part = az * az + rad * rad
        total = part if total is None else total + part
    return total


def edges_kernel(
    cycle, off_ref, pot_hbm, cur_hbm, mat_hbm, flux_hbm, jit_hbm, odd_ref, even_ref, pan_ref,
    up_ref, down_ref, pot_ref, cur_ref, mat_ref, flux_ref, jit_ref, sems
):
    fields, layers = pot_ref.shape[1], mat_ref.shape[1]
    rows = pot_hbm.shape[1]
    pairs = [(flux_hbm, flux_ref), (jit_hbm, jit_ref)]
    for hbm, ref in ((pot_hbm, pot_ref), (cur_hbm, cur_ref), (mat_hbm, mat_ref)):
        pairs += [(hbm.at[:, 0:8, :], ref.at[0]), (hbm.at[:, rows - 8 : rows, :], ref.at[1])]
    copies = [pltpu.make_async_copy(src, dst, sems.at[n]) for n, (src, dst) in enumerate(pairs)]
    for copy in copies:
        copy.start()
    for copy in copies:
        copy.wait()

    odd_a = lax.rem(lax.axis_index("az"), 2) == 1
    panels = flux_ref.shape[1]
    where = jit_ref[...] + off_ref[0]
    where = jnp.where(where >= cycle, where - cycle, where).astype(f32)
    for h in range(panels // 128):
        at = h * (fields + 1)
        pan_ref[at : at + fields, :] = flux_ref[:, h * 128 : (h + 1) * 128]
        pan_ref[at + fields : at + fields + 1, :] = where[:, h * 128 : (h + 1) * 128]
    for j, (n, at) in enumerate(layout(fields, layers)):
        if j < fields:
            ref, k = pot_ref, j
        elif j < fields + layers:
            ref, k = mat_ref, j - fields
        else:
            ref, k = cur_ref, j - fields - layers
        up_ref[at : at + n, :] = ref[0, k, 0:n, :].astype(f32)
        down_ref[at : at + n, :] = ref[1, k, 8 - n : 8, :].astype(f32)
    n = up_ref.shape[0]
    even_ref[0:n, :] = jnp.where(odd_a, up_ref[...], down_ref[...])
    odd_ref[0:n, :] = jnp.where(odd_a, down_ref[...], up_ref[...])
    even_ref[n:, :] = pan_ref[...]
    odd_ref[n:, :] = pan_ref[...]


def edges(offset, pot, cur, mat, flux, jitter, cycle):
    fields, rows, cols = pot.shape
    layers = mat.shape[0]
    send = rim_rows(fields, layers)
    pan_rows = flux.shape[1] // 128 * (fields + 1)
    return pl.pallas_call(
        functools.partial(edges_kernel, cycle),
        out_shape=[
            jax.ShapeDtypeStruct((send + pan_rows, cols), f32),
            jax.ShapeDtypeStruct((send + pan_rows, cols), f32),
            jax.ShapeDtypeStruct((pan_rows, 128), f32),
        ],
        in_specs=[SMEM] + [HBM] * 5,
        out_specs=[VMEM] * 3,
        scratch_shapes=[
            pltpu.VMEM((send, cols), f32),
            pltpu.VMEM((send, cols), f32),
            pltpu.VMEM((2, fields, 8, cols), f32),
            pltpu.VMEM((2, fields, 8, cols), f32),
            pltpu.VMEM((2, layers, 8, cols), jnp.int32),
            pltpu.VMEM(flux.shape, f32),
            pltpu.VMEM(jitter.shape, jnp.int32),
            pltpu.SemaphoreType.DMA((8,)),
        ],
        compiler_params=params(LIMIT),
        cost_estimate=pl.CostEstimate(flops=1_000_000, bytes_accessed=400_000, transcendentals=0),
        name="pack_rows",
    )(offset, pot, cur, mat, flux, jitter)


def columns_kernel(pot_ref, cur_ref, mat_ref, strips_ref, slots_ref):
    fields, layers = pot_ref.shape[0], mat_ref.shape[0]
    rows, cols = mat_ref.shape[1:]
    total = 2 * fields + layers
    per = cols // slot
    groups = -(-total // per)
    lane = lax.broadcasted_iota(jnp.int32, (8, cols), 1)

    @pl.loop(0, rows // 8, unroll=8)
    def _(i):
        at = pl.ds(pl.multiple_of(i * 8, 8), 8)
        for g in range(groups):
            acc = None
            for k in range(min(per, total - g * per)):
                j = g * per + k
                if j < fields:
                    x = pot_ref[j, at, :]
                elif j < fields + layers:
                    x = mat_ref[j - fields, at, :].astype(f32)
                else:
                    x = cur_ref[j - fields - layers, at, :]
                x = pltpu.roll(x, (k * slot + high_own) % cols, 1)
                acc = x if acc is None else jnp.where(lane >= k * slot, x, acc)
            slots_ref[g, at, :] = acc

    for g in range(groups):
        strips_ref[g * cols : (g + 1) * cols, :] = slots_ref[g].T


def columns(pot, cur, mat):
    fields, rows, cols = pot.shape
    total = 2 * fields + mat.shape[0]
    groups = -(-total // (cols // slot))
    return pl.pallas_call(
        columns_kernel,
        out_shape=jax.ShapeDtypeStruct((groups * cols, rows), f32),
        in_specs=[VMEM] * 3,
        out_specs=VMEM,
        scratch_shapes=[pltpu.VMEM((groups, rows, cols), f32)],
        compiler_params=params(),
        cost_estimate=pl.CostEstimate(flops=8_000_000, bytes_accessed=3_000_000, transcendentals=0),
        name="turn_columns",
    )(pot, cur, mat)


def middle_kernel(fields, layers, odd_ref, even_ref, strips_ref, _coef, _air, ro_ref, re_ref, turned_ref, rim_ref):
    cols = even_ref.shape[1]
    send = rim_rows(fields, layers)
    odd_r = lax.rem(lax.axis_index("rad"), 2) == 1
    odd_a = lax.rem(lax.axis_index("az"), 2) == 1

    rim_ref[0:send, :] = jnp.where(odd_a, odd_ref[0:send, :], even_ref[0:send, :])
    rim_ref[64 : 64 + send, :] = jnp.where(odd_a, even_ref[0:send, :], odd_ref[0:send, :])
    turned_ref[...] = rim_ref[...].T

    for j, (n, at) in enumerate(layout(fields, layers)):
        b = slot_base(j, cols) + high_own
        lo, hi = strips_ref[b : b + n, :], strips_ref[b - n : b, :]
        re_ref[at : at + n, :] = jnp.where(odd_r, lo, hi)
        ro_ref[at : at + n, :] = jnp.where(odd_r, hi, lo)
    lo, hi = turned_ref[0:halo, :], turned_ref[cols - halo : cols, :]
    re_ref[send : send + halo, 0:128] = jnp.where(odd_r, lo, hi)
    ro_ref[send : send + halo, 0:128] = jnp.where(odd_r, hi, lo)


def middle(strips, odd_got, even_got, coef, air, fields, layers):
    cols = even_got.shape[1]
    rows = strips.shape[1]
    send = rim_rows(fields, layers)
    arrays = (odd_got, even_got, strips, coef, air)
    return pl.pallas_call(
        functools.partial(middle_kernel, fields, layers),
        out_shape=[
            jax.ShapeDtypeStruct((send + halo, rows), f32),
            jax.ShapeDtypeStruct((send + halo, rows), f32),
            jax.ShapeDtypeStruct((cols, 128), f32),
        ],
        in_specs=[VMEM] * 3 + [ANY] * 2,
        out_specs=[VMEM] * 3,
        scratch_shapes=[pltpu.VMEM((128, cols), f32)],
        compiler_params=params(),
        cost_estimate=pl.CostEstimate(flops=1_000_000, bytes_accessed=600_000, transcendentals=0),
        name="pack_columns",
    )(*arrays)


def block(i):
    return pl.ds(pl.multiple_of(i * 8, 8), 8)


def right(x):
    return pltpu.roll(x, x.shape[1] - 1, 1)


def left(x):
    return pltpu.roll(x, 1, 1)


def reluct_block(nu_ref, sat_ref, coef_ref, load, material, i):
    layers = coef_ref.shape[0]
    comps = 3
    for l in range(layers):
        centres = [load(c * layers + l, 0) for c in range(comps)]
        nexts = [load(c * layers + l, 1) for c in range(comps)]
        flux_sq = half_strength(centres, nexts, [right(x) for x in centres])
        which = material(l)
        coef_ref[l, block(i + 2), :] = half_reluct(lookup(which, nu_ref), lookup(which, sat_ref), flux_sq)


def sweep_block(coef_ref, load, source_at, i, store):
    layers = coef_ref.shape[0]
    comps = 3
    coef = [coef_ref[l, block(i + 2), :] for l in range(layers)]
    field = [[load(c * layers + l, 0) for l in range(layers)] for c in range(comps)]
    source = [[source_at(c * layers + l) for l in range(layers)] for c in range(comps)]
    moves = []
    for step in (1, -1):
        moves.append(
            (
                lambda l, step=step: coef_ref[l, pl.ds(i * 8 + 16 + step, 8), :],
                lambda c, l, step=step: load(c * layers + l, step),
            )
        )
    for turn in (right, left):
        moves.append((lambda l, turn=turn: turn(coef[l]), lambda c, l, turn=turn: turn(field[c][l])))
    new = sweep_cells(coef, field, source, moves)
    for c in range(comps):
        for l in range(layers):
            store(c * layers + l, new[c][l])


def keep(one_ref, i):
    def store(j, x):
        one_ref[j, block(i + 1), :] = x

    return store


def inner_kernel(nu_ref, sat_ref, pot_ref, cur_ref, mat_ref, coef_ref, one_ref):
    rows, cols = mat_ref.shape[1:]
    count = rows // 8
    inner = count - 2
    step = divisor(inner, 10)

    def load_at(i):
        return lambda j, step: pot_ref[j, pl.ds(i * 8 + step, 8), :]

    def reluct_at(i, load):
        reluct_block(nu_ref, sat_ref, coef_ref, load, lambda l: mat_ref[l, block(i), :], i)

    def last_load(j, step):
        x = pot_ref[j, rows - 8 : rows, :]
        return x if step == 0 else pltpu.roll(x, 7, 0)

    reluct_at(0, load_at(0))
    reluct_at(count - 1, last_load)

    @pl.loop(1, count - 1, unroll=step)
    def _(i):
        reluct_at(i, load_at(i))

    @pl.loop(1, count - 1, unroll=step)
    def _(i):
        sweep_block(coef_ref, load_at(i), lambda j: cur_ref[j, block(i), :], i, keep(one_ref, i))


def inner(nu, sat, pot, cur, mat):
    fields, rows, cols = pot.shape
    layers = mat.shape[0]
    return pl.pallas_call(
        inner_kernel,
        out_shape=[
            jax.ShapeDtypeStruct((layers, rows + 32, cols), f32),
            jax.ShapeDtypeStruct((fields, rows + 16, cols), f32),
        ],
        in_specs=[SMEM, SMEM] + [VMEM] * 3,
        out_specs=[VMEM, VMEM],
        compiler_params=params(),
        cost_estimate=pl.CostEstimate(flops=20_000_000, bytes_accessed=4_000_000, transcendentals=0),
        name="inner_rows",
    )(nu, sat, pot, cur, mat)


def outer_kernel(
    nu_ref, sat_ref, pot_ref, cur_ref, mat_ref, odd_ref, even_ref, coef_in, one_in, out_ref, coef_ref, one_ref, edge_ref
):
    fields, rows, cols = out_ref.shape
    layers = mat_ref.shape[0]
    odd_a = lax.rem(lax.axis_index("az"), 2) == 1
    count = rows // 8

    blank = jnp.zeros((8, cols), f32)
    for j, (n, at) in enumerate(layout(fields, layers)):
        if j < fields:
            ref, k = pot_ref, j
        elif j < fields + layers:
            ref, k = mat_ref, j - fields
        else:
            ref, k = cur_ref, j - fields - layers
        edge_ref[0, j, 0:8, :] = blank
        edge_ref[0, j, 8:16, :] = blank
        edge_ref[1, j, 16:24, :] = blank
        edge_ref[1, j, 24:32, :] = blank
        edge_ref[0, j, 16:32, :] = ref[k, 0:16, :].astype(f32)
        edge_ref[1, j, 0:16, :] = ref[k, rows - 16 : rows, :].astype(f32)
        even, odd = even_ref[at : at + n, :], odd_ref[at : at + n, :]
        edge_ref[0, j, 16 - n : 16, :] = jnp.where(odd_a, even, odd)
        edge_ref[1, j, 16 : 16 + n, :] = jnp.where(odd_a, odd, even)
    for l in range(layers):
        coef_ref[l, 0:8, :] = blank
        coef_ref[l, 24 + rows : 32 + rows, :] = blank

    def edge_load(k):
        side, at = k // 2, 8 + 8 * (k % 2)
        return (
            lambda j, step: edge_ref[side, j, at + step : at + step + 8, :],
            (-1, 0, count - 1, count)[k],
        )

    for k in (0, 2, 3):
        load, i = edge_load(k)
        reluct_block(nu_ref, sat_ref, coef_ref, load, lambda l: load(fields + l, 0).astype(jnp.int32), i)
    for k in range(4):
        load, i = edge_load(k)
        sweep_block(coef_ref, load, lambda j: load(fields + layers + j, 0), i, keep(one_ref, i))

    @pl.loop(0, count, unroll=divisor(count, 8))
    def _(i):
        def store(j, x):
            out_ref[j, block(i), :] = x

        sweep_block(
            coef_ref,
            lambda j, step: one_ref[j, pl.ds(i * 8 + 8 + step, 8), :],
            lambda j: cur_ref[j, block(i), :],
            i,
            store,
        )


def outer(nu, sat, pot, cur, mat, odd_got, even_got, coef, one):
    fields, rows, cols = pot.shape
    layers = mat.shape[0]
    total = 2 * fields + layers
    return pl.pallas_call(
        outer_kernel,
        out_shape=[
            jax.ShapeDtypeStruct(pot.shape, f32),
            jax.ShapeDtypeStruct(coef.shape, f32),
            jax.ShapeDtypeStruct(one.shape, f32),
        ],
        in_specs=[SMEM, SMEM] + [VMEM] * 7,
        out_specs=[VMEM] * 3,
        input_output_aliases={7: 1, 8: 2},
        scratch_shapes=[pltpu.VMEM((2, total, 32, cols), f32)],
        compiler_params=params(),
        cost_estimate=pl.CostEstimate(flops=20_000_000, bytes_accessed=4_000_000, transcendentals=0),
        name="outer_rows",
    )(nu, sat, pot, cur, mat, odd_got, even_got, coef, one)[0]


def deposit_kernel(cycle, starts, bases, fields, rows, *refs):
    n = len(starts)
    pan_refs, air_refs, vals_ref = refs[:n], refs[n + 1 : -1], refs[-1]
    r, a = lax.axis_index("rad"), lax.axis_index("az")
    size = lax.axis_size("rad")
    stator = (r == size // 2) | (r == size // 2 - 1)

    @pl.when(stator)
    def _():
        lanes = vals_ref.shape[1]
        vals_ref[...] = jnp.zeros_like(vals_ref)
        t = 0
        for ref, first in zip(pan_refs, starts):
            for at in range(first, ref.shape[0], fields + 1):
                vals_ref[0 : fields + 1, t * 128 : (t + 1) * 128] = ref[at : at + fields + 1, :]
                t += 1
        values = vals_ref[...]
        position = vals_ref[fields : fields + 1, :].astype(jnp.int32)
        high = values.astype(jnp.bfloat16)
        rest = values - high.astype(f32)
        mid = rest.astype(jnp.bfloat16)
        low = (rest - mid.astype(f32)).astype(jnp.bfloat16)
        split = jnp.concatenate([high, mid, low], axis=0)
        spot = lax.broadcasted_iota(jnp.int32, (rows, lanes), 0)
        lane = lax.broadcasted_iota(jnp.int32, (16, 128), 1)
        for air_ref, bit in zip(air_refs, bases):
            local = position - (a ^ bit) * rows
            onehot = jnp.where(spot == local, 1.0, 0.0).astype(jnp.bfloat16)
            parts = lax.dot_general(split, onehot, (((1,), (1,)), ((), ())), preferred_element_type=f32)
            air_ref[0:16, 0:rows] = parts[0:16] + parts[16:32] + parts[32:48]
            after = (local == rows) | (local == rows - cycle)
            before = (local == -1) | (local == cycle - 1)
            after = jnp.sum(jnp.where(after, values, 0.0), axis=1, keepdims=True)
            before = jnp.sum(jnp.where(before, values, 0.0), axis=1, keepdims=True)
            air_ref[16:32, 0:128] = jnp.where(lane == 0, after, jnp.where(lane == 127, before, 0.0))

    @pl.when(jnp.logical_not(stator))
    def _():
        for air_ref in air_refs:
            air_ref[...] = jnp.zeros_like(air_ref)


def deposit(pans, starts, coef, bases, fields, rows, cycle):
    layers = coef.shape[0]
    panels = sum(p.shape[0] - first for p, first in zip(pans, starts)) // (fields + 1) * 128
    return pl.pallas_call(
        functools.partial(deposit_kernel, cycle, starts, bases, fields, rows),
        out_shape=[jax.ShapeDtypeStruct((rim_rows(fields, layers) + halo, rows), f32) for _ in bases],
        in_specs=[VMEM] * len(pans) + [ANY],
        out_specs=[VMEM] * len(bases),
        scratch_shapes=[pltpu.VMEM((16, panels), f32)],
        compiler_params=params(),
        cost_estimate=pl.CostEstimate(flops=4_000_000, bytes_accessed=500_000, transcendentals=0),
        name="airgap",
    )(*pans, coef)


def rim_kernel(n_airs, nu_ref, sat_ref, main_ref, *refs):
    air_refs, (strips_ref, turned_ref, ro_ref, re_ref) = refs[:n_airs], refs[n_airs:-6]
    out_hbm, merged_ref, cols_ref, corner_ref, back_ref, sem = refs[-6:]
    fields, rows, cols = main_ref.shape
    total = cols_ref.shape[0]
    layers = total - 2 * fields
    comps = fields // layers
    send = rim_rows(fields, layers)
    r = lax.axis_index("rad")
    size = lax.axis_size("rad")
    odd_r = lax.rem(r, 2) == 1

    def left(at, n):
        return jnp.where(odd_r, re_ref[at : at + n, :], ro_ref[at : at + n, :])

    def right(at, n):
        return jnp.where(odd_r, ro_ref[at : at + n, :], re_ref[at : at + n, :])

    corner_ref[0:2, :] = left(send + 1, 2)[:, 0:128]
    corner_ref[2:8, :] = turned_ref[0:low_own, :]
    corner_ref[8:13, :] = turned_ref[cols - high_own : cols, :]
    corner_ref[13:16, :] = right(send, halo)[:, 0:128]
    corner = corner_ref[...]
    lane = lax.broadcasted_iota(jnp.int32, (16, 128), 1)
    for j, (n, at) in enumerate(layout(fields, layers)):
        b = slot_base(j, cols)
        cols_ref[j, 0:8, 0:rows] = strips_ref[b + high_own - 2 : b + high_own + 6, :]
        cols_ref[j, 8:16, 0:rows] = strips_ref[b : b + 8, :]
        m = min(n, 2)
        cols_ref[j, 2 - m : 2, 0:rows] = left(at + n - m, m)
        cols_ref[j, 13 : 13 + n, 0:rows] = right(at, n)
        cols_ref[j, :, rows : rows + 128] = jnp.where(
            lane < 64, pltpu.roll(corner, (-at) % 128, 1), pltpu.roll(corner, (64 - n - at) % 128, 1)
        )

    column = lax.broadcasted_iota(jnp.int32, (16, rows + 128), 0)
    inside = ((column >= 2) | (r > 0)) & ((column < 13) | (r < size - 1))
    target = jnp.where(r == size // 2, 2, jnp.where(r == size // 2 - 1, 13, -1))

    def move(x, axis, step):
        return pltpu.roll(x, (-step) % x.shape[axis], axis)

    pot = [[jnp.where(inside, cols_ref[c * layers + l], 0.0) for l in range(layers)] for c in range(comps)]
    source = []
    for c in range(comps):
        source.append([])
        for l in range(layers):
            j = c * layers + l
            air = sum(ref[j : j + 1, :] for ref in air_refs)
            outside = sum(ref[16 + j : 17 + j, 0:128] for ref in air_refs)
            air = jnp.concatenate([air, outside], axis=1)
            source[c].append(cols_ref[fields + layers + j] + jnp.where(column == target, air, 0.0))
    coef = []
    for l in range(layers):
        centres = [pot[c][l] for c in range(comps)]
        flux_sq = half_strength(centres, [move(x, 1, 1) for x in centres], [move(x, 0, 1) for x in centres])
        which = cols_ref[fields + l].astype(jnp.int32)
        k = half_reluct(lookup(which, nu_ref), lookup(which, sat_ref), flux_sq)
        coef.append(jnp.where(inside, k, 0.0))
    moves = [(axis, step) for axis in (1, 0) for step in (1, -1)]
    moved = {(l, m): move(coef[l], *m) for l in range(layers) for m in moves}

    def sweep(field):
        table = [
            (lambda l, m=m: moved[l, m], lambda c, l, m=m: move(field[c][l], *m)) for m in moves
        ]
        return sweep_cells(coef, field, source, table)

    one = [[jnp.where(inside, x, 0.0) for x in part] for part in sweep(pot)]
    fixed = sweep(one)
    for c in range(comps):
        for l in range(layers):
            j = c * layers + l
            back_ref[8 * j : 8 * j + 3, :] = fixed[c][l][10:13, 0:rows]
            back_ref[8 * j + 3 : 8 * j + 5, :] = fixed[c][l][2:4, 0:rows]
    turned = back_ref[...].T

    lane = lax.broadcasted_iota(jnp.int32, (rows, cols), 1)
    edge = (lane < 2) | (lane >= cols - 3)
    for j in range(fields):
        merged_ref[j] = jnp.where(edge, pltpu.roll(turned, (cols - 3 - 8 * j) % cols, 1), main_ref[j])
        pltpu.make_async_copy(merged_ref.at[j], out_hbm.at[j], sem.at[j]).start()
    for j in range(fields):
        pltpu.make_async_copy(merged_ref.at[j], out_hbm.at[j], sem.at[j]).wait()


def rims(nu, sat, main, strips, turned, ro_got, re_got, airs, layers):
    fields, rows, cols = main.shape
    total = 2 * fields + layers
    arrays = (main, *airs, strips, turned, ro_got, re_got)
    return pl.pallas_call(
        functools.partial(rim_kernel, len(airs)),
        out_shape=jax.ShapeDtypeStruct(main.shape, f32),
        in_specs=[SMEM, SMEM] + [VMEM] * len(arrays),
        out_specs=ANY,
        scratch_shapes=[
            pltpu.VMEM(main.shape, f32),
            pltpu.VMEM((total, 16, rows + 128), f32),
            pltpu.VMEM((16, 128), f32),
            pltpu.VMEM((128, rows), f32),
            pltpu.SemaphoreType.DMA((fields,)),
        ],
        compiler_params=params(),
        name="rims",
    )(nu, sat, *arrays)


def local(potential, current, material, nu_table, sat_table, panel_flux, panel_jitter, rotor_offset):
    comps, layers, rows, cols = potential.shape
    fields = comps * layers
    az, rad = lax.axis_size("az"), lax.axis_size("rad")
    cycle = rows * az
    pot = potential.reshape(fields, rows, cols)
    cur = current.reshape(fields, rows, cols)

    def swap(x, az_of, rad_of):
        pairs = [(a * rad + r, az_of(a) * rad + rad_of(r)) for a in range(az) for r in range(rad)]
        return lax.ppermute(x, ("az", "rad"), pairs)

    def same(i):
        return i

    def even(i):
        return i ^ 1

    def odd(i, n):
        return (i + 1) % n if i % 2 else (i - 1) % n

    odd_send, even_send, pan = edges(
        rotor_offset, pot, cur, material, panel_flux, panel_jitter.reshape(1, -1), cycle
    )
    odd_got = swap(odd_send, lambda a: odd(a, az), same)
    even_got = swap(even_send, even, same)
    two_got = swap(pan, lambda a: a ^ 2, same)
    strips = columns(pot, cur, material)
    coef, one = inner(nu_table, sat_table, pot, cur, material)
    at = rim_rows(fields, layers)
    pans, starts = [pan, odd_got, even_got, two_got], [0, at, at, 0]
    if az > 8:
        held, bit = jnp.concatenate([p[first:] for p, first in zip(pans, starts)], axis=0), 8
        while bit < az:
            held = jnp.concatenate([held, swap(held, lambda a, bit=bit: a ^ bit, same)], axis=0)
            bit *= 2
        pans, starts = [held], [0]
    if az > 4:
        air, air_send = deposit(pans, starts, coef, [0, 4], fields, rows, cycle)
        airs = [air, swap(air_send, lambda a: a ^ 4, same)]
    else:
        airs = deposit(pans, starts, coef, [0], fields, rows, cycle)
    ro_send, re_send, turned = middle(strips, odd_got, even_got, coef, airs[0], fields, layers)
    ro_got = swap(ro_send, same, lambda r: odd(r, rad))
    re_got = swap(re_send, same, even)
    main = outer(nu_table, sat_table, pot, cur, material, odd_got, even_got, coef, one)
    out = rims(nu_table, sat_table, main, strips, turned, ro_got, re_got, airs, layers)
    return out.reshape(potential.shape)


def solution(mesh):
    placed = (
        P(None, None, "az", "rad"),
        P(None, None, "az", "rad"),
        P(None, "az", "rad"),
        P(),
        P(),
        P(None, "az"),
        P("az"),
        P(),
    )
    return jax.shard_map(
        local, mesh=mesh, in_specs=placed, out_specs=P(None, None, "az", "rad"), check_vma=False
    )
```

time: 93.8 us -> 20.3 us (0.22)
  the two profiles are of different devices: /device:TPU:30 before, /device:TPU:0 now
where the time goes in v2:
time: 20.3 us; the launch traced here: 20.2 us
  Pallas kernels  9.55 us (47%)
  starting transfers between devices  9.17 us (45%)
  between operations  0.77 us (4%)
  waiting for transfers between devices  0.64 us (3%)
    ppermute x6, starting transfers between devices, swap(): return lax.ppermute(x, ('az', 'rad'), pairs)  9.17 us
    pallas_call x1, Pallas kernels, rims(): pl.pallas_call(functools.partial(rim_kernel, len(airs)), out_shape=jax.Sh...  2.45 us
    pallas_call x1, Pallas kernels, inner(): pl.pallas_call(inner_kernel, out_shape=[jax.ShapeDtypeStruct((layers, row...  2.24 us
    pallas_call x1, Pallas kernels, outer(): pl.pallas_call(outer_kernel, out_shape=[jax.ShapeDtypeStruct(pot.shape, f...  1.89 us
    pallas_call x1, Pallas kernels, edges(): pl.pallas_call(functools.partial(edges_kernel, cycle), out_shape=[jax.Sha...  1.73 us
    pallas_call x1, Pallas kernels, columns(): pl.pallas_call(columns_kernel, out_shape=jax.ShapeDtypeStruct((groups * c...  1.11 us
    ppermute x6, waiting for transfers between devices, swap(): return lax.ppermute(x, ('az', 'rad'), pairs)  0.64 us
  transfers between devices with their start and end apart: 6, of which 2 were waited for; matrix products, arithmetic and copies ran while one was open for 0% of the time, Pallas kernels for 27%

profile of v2, /device:TPU:0, one launch (start us, length us, event | category | flops | bytes accessed | tf_op | source)
XLA Modules:
  0.0 20.2 jit_solution(17918769902618349176)
XLA Ops:
  0.7 0.0 copy-start
  0.7 0.0 copy-start.1
  0.7 0.0 copy-start.2
  0.7 1.7 %pack_rows.1 = (f32[62,128]{1,0:T(8,128)}, f32[62,128]{1,0:T(8,128)}, f32[20,128]{1,0:T(8,128)}) custom-call(s32[1]{0:T(128)S(6)} %copy.13.off_ref, f32[9,256,128]{2,1,0:T(8,128)} %bitcast.4, f32[9,256,128]{2,1,0:T(8,128)} %bitcast.8, s32[3,256,128]{2,1,0:T(8,128)} %mat_ref.5, f32[9,256]{1,0:T(8,128)} %flux_hbm.1, s32[1,256]{1,0:T(1,128)} %bitcast.12), custom_call_target="tpu_custom_call" | custom-call | flops 1000000 | bytes 400000 | tf_op jit(solution)/shard_map/pack_rows/pallas_call | solution.py:137
  2.4 6.0 %collective-permute-start = (f32[62,128]{1,0:T(8,128)}, f32[62,128]{1,0:T(8,128)S(1)}, u32[]{:S(2)}, u32[]{:S(2)}) collective-permute-start(f32[62,128]{1,0:T(8,128)} %get-tuple-element.16), channel_id=1, source_target_pairs={{0,28},{1,29},{2,30},{3,31},{4,8},{5,9},{6,10},{7,11},{8,4},{9,5},... | collective-permute-start | bytes 95240 | tf_op jit(solution)/shard_map/ppermute | solution.py:597
  8.5 0.0 collective-permute-start.1
  8.5 0.1 collective-permute-start.2
  8.6 0.0 copy-done
  8.6 0.0 copy-done.1
  8.6 0.0 copy-done.2
  8.6 1.1 %turn_columns.1.strips_ref.refs_2_ = f32[256,256]{1,0:T(8,128)S(1)} custom-call(f32[9,256,128]{2,1,0:T(8,128)S(1)} %bitcast.5, f32[9,256,128]{2,1,0:T(8,128)S(1)} %bitcast.9, s32[3,256,128]{2,1,0:T(8,128)S(1)} %copy-done.2), custom_call_target="tpu_custom_call" | custom-call | flops 8000000 | bytes 3000000 | tf_op jit(solution)/shard_map/turn_columns/pallas_call | solution.py:195
  9.7 2.2 %inner_rows.1 = (f32[3,288,128]{2,1,0:T(8,128)S(1)}, f32[9,272,128]{2,1,0:T(8,128)S(1)}) custom-call(f32[8]{0:T(128)S(1)} %copy-done.4, f32[8]{0:T(128)S(1)} %copy-done.5, f32[9,256,128]{2,1,0:T(8,128)S(1)} %bitcast.6, f32[9,256,128]{2,1,0:T(8,128)S(1)} %bitcast.10, s32[3,256,128]{2,1,0:T(8,128)S(1)} %copy-done.2), custom_call_target="tpu_custom_call" | custom-call | flops 20000000 | bytes 4000000 | tf_op jit(solution)/shard_map/inner_rows/pallas_call | solution.py:331
  12.0 0.4 %collective-permute-done.2.refs_3_ = f32[20,128]{1,0:T(8,128)S(1)} collective-permute-done((f32[20,128]{1,0:T(8,128)}, f32[20,128]{1,0:T(8,128)S(1)}, u32[]{:S(2)}, u32[]{:S(2)}) %collective-permute-start.2) | collective-permute-done | bytes 10272 | tf_op jit(solution)/shard_map/ppermute | solution.py:597
  12.4 0.0 collective-permute-done.odd_ref.refs_1_
  12.4 0.2 %collective-permute-done.1.even_ref.refs_2_ = f32[62,128]{1,0:T(8,128)S(1)} collective-permute-done((f32[62,128]{1,0:T(8,128)}, f32[62,128]{1,0:T(8,128)S(1)}, u32[]{:S(2)}, u32[]{:S(2)}) %collective-permute-start.1) | collective-permute-done | bytes 31776 | tf_op jit(solution)/shard_map/ppermute | solution.py:597
  12.6 1.0 %collective-permute-start.3 = (f32[45,256]{1,0:T(8,128)S(1)}, f32[45,256]{1,0:T(8,128)S(1)}, u32[]{:S(2)}, u32[]{:S(2)}) collective-permute-start(f32[45,256]{1,0:T(8,128)S(1)} %get-tuple-element.23), channel_id=1, source_target_pairs={{0,16},{1,17},{2,18},{3,19},{4,20},{5,21},{6,22},{7,23},{8,24},{9,... | collective-permute-start | bytes 138248 | tf_op jit(solution)/shard_map/ppermute | solution.py:597
  13.6 0.1 pack_columns.1
  13.7 0.1 collective-permute-start.4
  13.8 2.0 %collective-permute-start.5 = (f32[45,256]{1,0:T(8,128)S(1)}, f32[45,256]{1,0:T(8,128)S(1)}, u32[]{:S(2)}, u32[]{:S(2)}) collective-permute-start(f32[45,256]{1,0:T(8,128)S(1)} %get-tuple-element.26), channel_id=1, source_target_pairs={{0,1},{1,0},{2,3},{3,2},{4,5},{5,4},{6,7},{7,6},{8,9},{9,8},{10,11... | collective-permute-start | bytes 138248 | tf_op jit(solution)/shard_map/ppermute | solution.py:597
  15.8 1.9 %outer_rows.1 = (f32[9,256,128]{2,1,0:T(8,128)S(1)}, f32[3,288,128]{2,1,0:T(8,128)S(1)}, f32[9,272,128]{2,1,0:T(8,128)S(1)}) custom-call(f32[8]{0:T(128)S(1)} %copy-done.4, f32[8]{0:T(128)S(1)} %copy-done.5, f32[9,256,128]{2,1,0:T(8,128)S(1)} %bitcast.7, f32[9,256,128]{2,1,0:T(8,128)S(1)} %bitcast.11, ...), custom_call_target="tpu_custom_call", output_to_operand_aliasing={{1}: (7, {}), {2}: (8, {})} | custom-call | flops 20000000 | bytes 4000000 | tf_op jit(solution)/shard_map/outer_rows/pallas_call | solution.py:406
  17.7 0.0 collective-permute-done.3.refs_1_
  17.7 0.0 collective-permute-done.4.refs_4_
  17.7 0.0 collective-permute-done.5.refs_5_
  17.7 2.5 %rims.1 = f32[9,256,128]{2,1,0:T(8,128)} custom-call(f32[8]{0:T(128)S(1)} %copy-done.4, f32[8]{0:T(128)S(1)} %copy-done.5, f32[9,256,128]{2,1,0:T(8,128)S(1)} %get-tuple-element.20.main_ref, f32[45,256]{1,0:T(8,128)S(1)} %get-tuple-element.22._air.refs_0_, f32[45,256]{1,0:T(8,128)S(1)} %collective-permute-done.3.refs_1_, ...), custom_call_target="tpu_custom_call" | custom-call | tf_op jit(solution)/shard_map/rims/pallas_call | solution.py:570
  (7 shorter events, 0.0 us)
Async XLA Ops:
  0.7 7.9 %copy-start = (f32[3,3,256,128]{3,2,1,0:T(8,128)S(1)}, f32[3,3,256,128]{3,2,1,0:T(8,128)}, u32[]{:S(2)}) copy-start(f32[3,3,256,128]{3,2,1,0:T(8,128)} %param.8) | copy-start | bytes 3538948
  0.7 7.9 %copy-start.1 = (f32[3,3,256,128]{3,2,1,0:T(8,128)S(1)}, f32[3,3,256,128]{3,2,1,0:T(8,128)}, u32[]{:S(2)}) copy-start(f32[3,3,256,128]{3,2,1,0:T(8,128)} %param.9) | copy-start | bytes 3538948
  0.7 7.9 %copy-start.2 = (s32[3,256,128]{2,1,0:T(8,128)S(1)}, s32[3,256,128]{2,1,0:T(8,128)}, u32[]{:S(2)}) copy-start(s32[3,256,128]{2,1,0:T(8,128)} %mat_ref.5) | copy-start | bytes 1179652
  2.4 10.0 %collective-permute-start = (f32[62,128]{1,0:T(8,128)}, f32[62,128]{1,0:T(8,128)S(1)}, u32[]{:S(2)}, u32[]{:S(2)}) collective-permute-start(f32[62,128]{1,0:T(8,128)} %get-tuple-element.16), channel_id=1, source_target_pairs={{0,28},{1,29},{2,30},{3,31},{4,8},{5,9},{6,10},{7,11},{8,4},{9,5},... | collective-permute-start | bytes 95240 | tf_op jit(solution)/shard_map/ppermute | solution.py:597
  8.5 4.1 %collective-permute-start.1 = (f32[62,128]{1,0:T(8,128)}, f32[62,128]{1,0:T(8,128)S(1)}, u32[]{:S(2)}, u32[]{:S(2)}) collective-permute-start(f32[62,128]{1,0:T(8,128)} %get-tuple-element.17), channel_id=1, source_target_pairs={{0,4},{1,5},{2,6},{3,7},{4,0},{5,1},{6,2},{7,3},{8,12},{9,13},{10,... | collective-permute-start | bytes 95240 | tf_op jit(solution)/shard_map/ppermute | solution.py:597
  8.5 1.2 %copy-start.4 = (f32[8]{0:T(128)S(1)}, f32[8]{0:T(128)}, u32[]{:S(2)}) copy-start(f32[8]{0:T(128)} %nu_ref.5) | copy-start | bytes 100
  8.5 1.2 %copy-start.5 = (f32[8]{0:T(128)S(1)}, f32[8]{0:T(128)}, u32[]{:S(2)}) copy-start(f32[8]{0:T(128)} %sat_ref.5) | copy-start | bytes 100
  8.5 3.9 %collective-permute-start.2 = (f32[20,128]{1,0:T(8,128)}, f32[20,128]{1,0:T(8,128)S(1)}, u32[]{:S(2)}, u32[]{:S(2)}) collective-permute-start(f32[20,128]{1,0:T(8,128)} %get-tuple-element.21.refs_0_), channel_id=1, source_target_pairs={{0,8},{1,9},{2,10},{3,11},{4,12},{5,13},{6,14},{7,15},{8,0},{9,1},... | collective-permute-start | bytes 30728 | tf_op jit(solution)/shard_map/ppermute | solution.py:597
  9.7 2.9 %copy-start.3 = (f32[20,128]{1,0:T(8,128)S(1)}, f32[20,128]{1,0:T(8,128)}, u32[]{:S(2)}) copy-start(f32[20,128]{1,0:T(8,128)} %get-tuple-element.21.refs_0_) | copy-start | bytes 30724
  12.6 5.1 %collective-permute-start.3 = (f32[45,256]{1,0:T(8,128)S(1)}, f32[45,256]{1,0:T(8,128)S(1)}, u32[]{:S(2)}, u32[]{:S(2)}) collective-permute-start(f32[45,256]{1,0:T(8,128)S(1)} %get-tuple-element.23), channel_id=1, source_target_pairs={{0,16},{1,17},{2,18},{3,19},{4,20},{5,21},{6,22},{7,23},{8,24},{9,... | collective-permute-start | bytes 138248 | tf_op jit(solution)/shard_map/ppermute | solution.py:597
  13.7 4.0 %collective-permute-start.4 = (f32[45,256]{1,0:T(8,128)S(1)}, f32[45,256]{1,0:T(8,128)S(1)}, u32[]{:S(2)}, u32[]{:S(2)}) collective-permute-start(f32[45,256]{1,0:T(8,128)S(1)} %get-tuple-element.25), channel_id=1, source_target_pairs={{0,3},{1,2},{2,1},{3,0},{4,7},{5,6},{6,5},{7,4},{8,11},{9,10},{10,... | collective-permute-start | bytes 138248 | tf_op jit(solution)/shard_map/ppermute | solution.py:597
  13.8 3.9 %collective-permute-start.5 = (f32[45,256]{1,0:T(8,128)S(1)}, f32[45,256]{1,0:T(8,128)S(1)}, u32[]{:S(2)}, u32[]{:S(2)}) collective-permute-start(f32[45,256]{1,0:T(8,128)S(1)} %get-tuple-element.26), channel_id=1, source_target_pairs={{0,1},{1,0},{2,3},{3,2},{4,5},{5,4},{6,7},{7,6},{8,9},{9,8},{10,11... | collective-permute-start | bytes 138248 | tf_op jit(solution)/shard_map/ppermute | solution.py:597

commit v3 on v2

--- a/solution.py
+++ b/solution.py
@@ -9,12 +9,12 @@
 
 sigma_term = 1.0
 LIMIT = 60
+EXPAND = 20_000_000_000
 halo = 3
 low_own, high_own = 6, 5
 slot = low_own + high_own
 f32 = jnp.float32
 VMEM = pl.BlockSpec(memory_space=pltpu.VMEM)
-SMEM = pl.BlockSpec(memory_space=pltpu.SMEM)
 HBM = pl.BlockSpec(memory_space=pltpu.HBM)
 ANY = pl.BlockSpec(memory_space=pl.ANY)
 
@@ -37,8 +37,12 @@
     return (j // per) * cols + (j % per) * slot
 
 
-def lookup(material, table):
-    values = [table[e] for e in range(table.shape[0])]
+def lookup(material, table_ref, first):
+    rows, lanes = material.shape
+    values = []
+    for e in range(first, first + table_ref.shape[0] // 2):
+        row = jnp.broadcast_to(table_ref[e : e + 1, :], (rows, 128))
+        values.append(jnp.concatenate([row] * (lanes // 128), axis=1))
     bit = 1
     while len(values) > 1:
         take = (material & bit) != 0
@@ -47,7 +51,9 @@
     return values[0]
 
 
-def half_reluct(base, saturation, flux_sq):
+def half_reluct(table_ref, material, flux_sq):
+    base = lookup(material, table_ref, 0)
+    saturation = lookup(material, table_ref, table_ref.shape[0] // 2)
     return (0.5 * base) * (1.0 + saturation * flux_sq / (1.0 + flux_sq))
 
 
@@ -91,12 +97,12 @@
 
 
 def edges_kernel(
-    cycle, off_ref, pot_hbm, cur_hbm, mat_hbm, flux_hbm, jit_hbm, odd_ref, even_ref, pan_ref,
-    up_ref, down_ref, pot_ref, cur_ref, mat_ref, flux_ref, jit_ref, sems
+    cycle, off_hbm, nu_hbm, sat_hbm, pot_hbm, cur_hbm, mat_hbm, flux_hbm, jit_hbm, odd_ref, even_ref, pan_ref, table_ref,
+    up_ref, down_ref, pot_ref, cur_ref, mat_ref, flux_ref, jit_ref, off_ref, nu_ref, sat_ref, sems
 ):
     fields, layers = pot_ref.shape[1], mat_ref.shape[1]
     rows = pot_hbm.shape[1]
-    pairs = [(flux_hbm, flux_ref), (jit_hbm, jit_ref)]
+    pairs = [(flux_hbm, flux_ref), (jit_hbm, jit_ref), (off_hbm, off_ref), (nu_hbm, nu_ref), (sat_hbm, sat_ref)]
     for hbm, ref in ((pot_hbm, pot_ref), (cur_hbm, cur_ref), (mat_hbm, mat_ref)):
         pairs += [(hbm.at[:, 0:8, :], ref.at[0]), (hbm.at[:, rows - 8 : rows, :], ref.at[1])]
     copies = [pltpu.make_async_copy(src, dst, sems.at[n]) for n, (src, dst) in enumerate(pairs)]
@@ -127,9 +133,13 @@
     odd_ref[0:n, :] = jnp.where(odd_a, down_ref[...], up_ref[...])
     even_ref[n:, :] = pan_ref[...]
     odd_ref[n:, :] = pan_ref[...]
-
-
-def edges(offset, pot, cur, mat, flux, jitter, cycle):
+    entries = nu_ref.shape[0]
+    for e in range(entries):
+        table_ref[e : e + 1, :] = jnp.full((1, 128), nu_ref[e], f32)
+        table_ref[entries + e : entries + e + 1, :] = jnp.full((1, 128), sat_ref[e], f32)
+
+
+def edges(offset, nu, sat, pot, cur, mat, flux, jitter, cycle):
     fields, rows, cols = pot.shape
     layers = mat.shape[0]
     send = rim_rows(fields, layers)
@@ -140,9 +150,10 @@
             jax.ShapeDtypeStruct((send + pan_rows, cols), f32),
             jax.ShapeDtypeStruct((send + pan_rows, cols), f32),
             jax.ShapeDtypeStruct((pan_rows, 128), f32),
+            jax.ShapeDtypeStruct((2 * nu.shape[0], 128), f32),
         ],
-        in_specs=[SMEM] + [HBM] * 5,
-        out_specs=[VMEM] * 3,
+        in_specs=[HBM] * 8,
+        out_specs=[VMEM] * 4,
         scratch_shapes=[
             pltpu.VMEM((send, cols), f32),
             pltpu.VMEM((send, cols), f32),
@@ -151,12 +162,15 @@
             pltpu.VMEM((2, layers, 8, cols), jnp.int32),
             pltpu.VMEM(flux.shape, f32),
             pltpu.VMEM(jitter.shape, jnp.int32),
-            pltpu.SemaphoreType.DMA((8,)),
+            pltpu.SMEM(offset.shape, jnp.int32),
+            pltpu.SMEM(nu.shape, f32),
+            pltpu.SMEM(sat.shape, f32),
+            pltpu.SemaphoreType.DMA((11,)),
         ],
         compiler_params=params(LIMIT),
         cost_estimate=pl.CostEstimate(flops=1_000_000, bytes_accessed=400_000, transcendentals=0),
         name="pack_rows",
-    )(offset, pot, cur, mat, flux, jitter)
+    )(offset, nu, sat, pot, cur, mat, flux, jitter)
 
 
 def columns_kernel(pot_ref, cur_ref, mat_ref, strips_ref, slots_ref):
@@ -257,7 +271,7 @@
     return pltpu.roll(x, 1, 1)
 
 
-def reluct_block(nu_ref, sat_ref, coef_ref, load, material, i):
+def reluct_block(table_ref, coef_ref, load, material, i):
     layers = coef_ref.shape[0]
     comps = 3
     for l in range(layers):
@@ -265,7 +279,7 @@
         nexts = [load(c * layers + l, 1) for c in range(comps)]
         flux_sq = half_strength(centres, nexts, [right(x) for x in centres])
         which = material(l)
-        coef_ref[l, block(i + 2), :] = half_reluct(lookup(which, nu_ref), lookup(which, sat_ref), flux_sq)
+        coef_ref[l, block(i + 2), :] = half_reluct(table_ref, which, flux_sq)
 
 
 def sweep_block(coef_ref, load, source_at, i, store):
@@ -297,7 +311,7 @@
     return store
 
 
-def inner_kernel(nu_ref, sat_ref, pot_ref, cur_ref, mat_ref, coef_ref, one_ref):
+def inner_kernel(table_ref, pot_ref, cur_ref, mat_ref, coef_ref, one_ref):
     rows, cols = mat_ref.shape[1:]
     count = rows // 8
     inner = count - 2
@@ -307,7 +321,7 @@
         return lambda j, step: pot_ref[j, pl.ds(i * 8 + step, 8), :]
 
     def reluct_at(i, load):
-        reluct_block(nu_ref, sat_ref, coef_ref, load, lambda l: mat_ref[l, block(i), :], i)
+        reluct_block(table_ref, coef_ref, load, lambda l: mat_ref[l, block(i), :], i)
 
     def last_load(j, step):
         x = pot_ref[j, rows - 8 : rows, :]
@@ -325,7 +339,7 @@
         sweep_block(coef_ref, load_at(i), lambda j: cur_ref[j, block(i), :], i, keep(one_ref, i))
 
 
-def inner(nu, sat, pot, cur, mat):
+def inner(table, pot, cur, mat):
     fields, rows, cols = pot.shape
     layers = mat.shape[0]
     return pl.pallas_call(
@@ -334,16 +348,16 @@
             jax.ShapeDtypeStruct((layers, rows + 32, cols), f32),
             jax.ShapeDtypeStruct((fields, rows + 16, cols), f32),
         ],
-        in_specs=[SMEM, SMEM] + [VMEM] * 3,
+        in_specs=[VMEM] * 4,
         out_specs=[VMEM, VMEM],
         compiler_params=params(),
         cost_estimate=pl.CostEstimate(flops=20_000_000, bytes_accessed=4_000_000, transcendentals=0),
         name="inner_rows",
-    )(nu, sat, pot, cur, mat)
+    )(table, pot, cur, mat)
 
 
 def outer_kernel(
-    nu_ref, sat_ref, pot_ref, cur_ref, mat_ref, odd_ref, even_ref, coef_in, one_in, out_ref, coef_ref, one_ref, edge_ref
+    table_ref, pot_ref, cur_ref, mat_ref, odd_ref, even_ref, coef_in, one_in, out_ref, coef_ref, one_ref, edge_ref
 ):
     fields, rows, cols = out_ref.shape
     layers = mat_ref.shape[0]
@@ -380,7 +394,7 @@
 
     for k in (0, 2, 3):
         load, i = edge_load(k)
-        reluct_block(nu_ref, sat_ref, coef_ref, load, lambda l: load(fields + l, 0).astype(jnp.int32), i)
+        reluct_block(table_ref, coef_ref, load, lambda l: load(fields + l, 0).astype(jnp.int32), i)
     for k in range(4):
         load, i = edge_load(k)
         sweep_block(coef_ref, load, lambda j: load(fields + layers + j, 0), i, keep(one_ref, i))
@@ -399,7 +413,7 @@
         )
 
 
-def outer(nu, sat, pot, cur, mat, odd_got, even_got, coef, one):
+def outer(table, pot, cur, mat, odd_got, even_got, coef, one):
     fields, rows, cols = pot.shape
     layers = mat.shape[0]
     total = 2 * fields + layers
@@ -410,19 +424,19 @@
             jax.ShapeDtypeStruct(coef.shape, f32),
             jax.ShapeDtypeStruct(one.shape, f32),
         ],
-        in_specs=[SMEM, SMEM] + [VMEM] * 7,
+        in_specs=[VMEM] * 8,
         out_specs=[VMEM] * 3,
-        input_output_aliases={7: 1, 8: 2},
+        input_output_aliases={6: 1, 7: 2},
         scratch_shapes=[pltpu.VMEM((2, total, 32, cols), f32)],
         compiler_params=params(),
         cost_estimate=pl.CostEstimate(flops=20_000_000, bytes_accessed=4_000_000, transcendentals=0),
         name="outer_rows",
-    )(nu, sat, pot, cur, mat, odd_got, even_got, coef, one)[0]
+    )(table, pot, cur, mat, odd_got, even_got, coef, one)[0]
 
 
 def deposit_kernel(cycle, starts, bases, fields, rows, *refs):
     n = len(starts)
-    pan_refs, air_refs, vals_ref = refs[:n], refs[n + 1 : -1], refs[-1]
+    pan_refs, air_refs, vals_ref = refs[:n], refs[n + 2 : -1], refs[-1]
     r, a = lax.axis_index("rad"), lax.axis_index("az")
     size = lax.axis_size("rad")
     stator = (r == size // 2) | (r == size // 2 - 1)
@@ -445,16 +459,18 @@
         split = jnp.concatenate([high, mid, low], axis=0)
         spot = lax.broadcasted_iota(jnp.int32, (rows, lanes), 0)
         lane = lax.broadcasted_iota(jnp.int32, (16, 128), 1)
+        channel = lax.broadcasted_iota(jnp.int32, (16, 128), 0)
         for air_ref, bit in zip(air_refs, bases):
             local = position - (a ^ bit) * rows
             onehot = jnp.where(spot == local, 1.0, 0.0).astype(jnp.bfloat16)
             parts = lax.dot_general(split, onehot, (((1,), (1,)), ((), ())), preferred_element_type=f32)
-            air_ref[0:16, 0:rows] = parts[0:16] + parts[16:32] + parts[32:48]
+            air_ref[...] = parts[0:16] + parts[16:32] + parts[32:48]
             after = (local == rows) | (local == rows - cycle)
             before = (local == -1) | (local == cycle - 1)
             after = jnp.sum(jnp.where(after, values, 0.0), axis=1, keepdims=True)
             before = jnp.sum(jnp.where(before, values, 0.0), axis=1, keepdims=True)
-            air_ref[16:32, 0:128] = jnp.where(lane == 0, after, jnp.where(lane == 127, before, 0.0))
+            outside = jnp.where(lane == channel, after, jnp.where(lane == channel + 16, before, 0.0))
+            air_ref[fields : fields + 1, 0:128] = jnp.sum(outside, axis=0, keepdims=True)
 
     @pl.when(jnp.logical_not(stator))
     def _():
@@ -462,24 +478,50 @@
             air_ref[...] = jnp.zeros_like(air_ref)
 
 
-def deposit(pans, starts, coef, bases, fields, rows, cycle):
-    layers = coef.shape[0]
+def deposit(pans, starts, order, bases, fields, rows, cycle):
     panels = sum(p.shape[0] - first for p, first in zip(pans, starts)) // (fields + 1) * 128
     return pl.pallas_call(
         functools.partial(deposit_kernel, cycle, starts, bases, fields, rows),
-        out_shape=[jax.ShapeDtypeStruct((rim_rows(fields, layers) + halo, rows), f32) for _ in bases],
-        in_specs=[VMEM] * len(pans) + [ANY],
+        out_shape=[jax.ShapeDtypeStruct((16, rows), f32) for _ in bases],
+        in_specs=[VMEM] * len(pans) + [ANY] * len(order),
         out_specs=[VMEM] * len(bases),
         scratch_shapes=[pltpu.VMEM((16, panels), f32)],
         compiler_params=params(),
         cost_estimate=pl.CostEstimate(flops=4_000_000, bytes_accessed=500_000, transcendentals=0),
         name="airgap",
-    )(*pans, coef)
-
-
-def rim_kernel(n_airs, nu_ref, sat_ref, main_ref, *refs):
-    air_refs, (strips_ref, turned_ref, ro_ref, re_ref) = refs[:n_airs], refs[n_airs:-6]
-    out_hbm, merged_ref, cols_ref, corner_ref, back_ref, sem = refs[-6:]
+    )(*pans, *order)
+
+
+def air_kernel(n, fields, *refs):
+    air_ref = refs[-1]
+    rows = refs[0].shape[1]
+    airgap = sum(ref[...] for ref in refs[:n])
+    lane = lax.broadcasted_iota(jnp.int32, (16, 128), 1)
+    channel = lax.broadcasted_iota(jnp.int32, (16, 128), 0)
+    spread = airgap[fields : fields + 1, 0:128]
+    after = jnp.sum(jnp.where(lane == channel, spread, 0.0), axis=1, keepdims=True)
+    before = jnp.sum(jnp.where(lane == channel + 16, spread, 0.0), axis=1, keepdims=True)
+    air_ref[:, 0:rows] = airgap
+    air_ref[:, rows : rows + 128] = jnp.where(lane == 0, after, jnp.where(lane == 127, before, 0.0))
+
+
+def gather_air(airs, main):
+    fields, rows, _ = main.shape
+    return pl.pallas_call(
+        functools.partial(air_kernel, len(airs), fields),
+        out_shape=jax.ShapeDtypeStruct((16, rows + 128), f32),
+        in_specs=[VMEM] * len(airs) + [ANY],
+        out_specs=VMEM,
+        compiler_params=params(),
+        cost_estimate=pl.CostEstimate(flops=EXPAND, bytes_accessed=0, transcendentals=0),
+        name="airgap_sum",
+    )(*airs, main)
+
+
+def rim_kernel(
+    table_ref, main_ref, air_ref, strips_ref, turned_ref, ro_ref, re_ref,
+    out_hbm, merged_ref, cols_ref, corner_ref, back_ref, sem,
+):
     fields, rows, cols = main_ref.shape
     total = cols_ref.shape[0]
     layers = total - 2 * fields
@@ -525,16 +567,14 @@
         source.append([])
         for l in range(layers):
             j = c * layers + l
-            air = sum(ref[j : j + 1, :] for ref in air_refs)
-            outside = sum(ref[16 + j : 17 + j, 0:128] for ref in air_refs)
-            air = jnp.concatenate([air, outside], axis=1)
+            air = air_ref[j : j + 1, :]
             source[c].append(cols_ref[fields + layers + j] + jnp.where(column == target, air, 0.0))
     coef = []
     for l in range(layers):
         centres = [pot[c][l] for c in range(comps)]
         flux_sq = half_strength(centres, [move(x, 1, 1) for x in centres], [move(x, 0, 1) for x in centres])
         which = cols_ref[fields + l].astype(jnp.int32)
-        k = half_reluct(lookup(which, nu_ref), lookup(which, sat_ref), flux_sq)
+        k = half_reluct(table_ref, which, flux_sq)
         coef.append(jnp.where(inside, k, 0.0))
     moves = [(axis, step) for axis in (1, 0) for step in (1, -1)]
     moved = {(l, m): move(coef[l], *m) for l in range(layers) for m in moves}
@@ -563,14 +603,14 @@
         pltpu.make_async_copy(merged_ref.at[j], out_hbm.at[j], sem.at[j]).wait()
 
 
-def rims(nu, sat, main, strips, turned, ro_got, re_got, airs, layers):
+def rims(table, main, air, strips, turned, ro_got, re_got, layers):
     fields, rows, cols = main.shape
     total = 2 * fields + layers
-    arrays = (main, *airs, strips, turned, ro_got, re_got)
-    return pl.pallas_call(
-        functools.partial(rim_kernel, len(airs)),
+    arrays = (main, air, strips, turned, ro_got, re_got)
+    return pl.pallas_call(
+        rim_kernel,
         out_shape=jax.ShapeDtypeStruct(main.shape, f32),
-        in_specs=[SMEM, SMEM] + [VMEM] * len(arrays),
+        in_specs=[VMEM] * (1 + len(arrays)),
         out_specs=ANY,
         scratch_shapes=[
             pltpu.VMEM(main.shape, f32),
@@ -581,7 +621,7 @@
         ],
         compiler_params=params(),
         name="rims",
-    )(nu, sat, *arrays)
+    )(table, *arrays)
 
 
 def local(potential, current, material, nu_table, sat_table, panel_flux, panel_jitter, rotor_offset):
@@ -605,14 +645,14 @@
     def odd(i, n):
         return (i + 1) % n if i % 2 else (i - 1) % n
 
-    odd_send, even_send, pan = edges(
-        rotor_offset, pot, cur, material, panel_flux, panel_jitter.reshape(1, -1), cycle
+    odd_send, even_send, pan, table = edges(
+        rotor_offset, nu_table, sat_table, pot, cur, material, panel_flux, panel_jitter.reshape(1, -1), cycle
     )
     odd_got = swap(odd_send, lambda a: odd(a, az), same)
     even_got = swap(even_send, even, same)
     two_got = swap(pan, lambda a: a ^ 2, same)
     strips = columns(pot, cur, material)
-    coef, one = inner(nu_table, sat_table, pot, cur, material)
+    coef, one = inner(table, pot, cur, material)
     at = rim_rows(fields, layers)
     pans, starts = [pan, odd_got, even_got, two_got], [0, at, at, 0]
     if az > 8:
@@ -622,15 +662,16 @@
             bit *= 2
         pans, starts = [held], [0]
     if az > 4:
-        air, air_send = deposit(pans, starts, coef, [0, 4], fields, rows, cycle)
+        air, air_send = deposit(pans, starts, (coef, strips), [0, 4], fields, rows, cycle)
         airs = [air, swap(air_send, lambda a: a ^ 4, same)]
     else:
-        airs = deposit(pans, starts, coef, [0], fields, rows, cycle)
+        airs = deposit(pans, starts, (coef, strips), [0], fields, rows, cycle)
     ro_send, re_send, turned = middle(strips, odd_got, even_got, coef, airs[0], fields, layers)
     ro_got = swap(ro_send, same, lambda r: odd(r, rad))
     re_got = swap(re_send, same, even)
-    main = outer(nu_table, sat_table, pot, cur, material, odd_got, even_got, coef, one)
-    out = rims(nu_table, sat_table, main, strips, turned, ro_got, re_got, airs, layers)
+    main = outer(table, pot, cur, material, odd_got, even_got, coef, one)
+    air = gather_air(airs, main)
+    out = rims(table, main, air, strips, turned, ro_got, re_got, layers)
     return out.reshape(potential.shape)
 
 

time: 20.3 us -> 19.5 us (0.961)
  Pallas kernels: 9.55 us -> 8.1 us
  waiting for transfers between devices: 0.64 us -> 1.28 us
    ppermute x6, waiting for transfers between devices: 0.64 us -> 1.28 us  [swap(): return lax.ppermute(x, ('az', 'rad'), pairs)]
    pallas_call x1, Pallas kernels: 2.24 us -> 1.69 us  [inner(): pl.pallas_call(inner_kernel, out_shape=[jax.ShapeDtypeStruct((layers, row...]
    pallas_call x1 -> x2, Pallas kernels: 2.45 us -> 1.97 us  [the longest x1 1.88 us: rims(): pl.pallas_call(rim_kernel, out_shape=jax.ShapeDtypeStruct(main.shape, f32...]
    pallas_call x1, Pallas kernels: 1.89 us -> 1.45 us  [outer(): pl.pallas_call(outer_kernel, out_shape=[jax.ShapeDtypeStruct(pot.shape, f...]
  transfers between devices with their start and end apart: 6 -> 6, of which waited for: 2 -> 3; matrix products, arithmetic and copies ran while one was open for 0% -> 0% of each run, Pallas kernels for 27% -> 23%
where the time goes in v3:
time: 19.5 us; the launch traced here: 19.3 us
  starting transfers between devices  9.18 us (47%)
  Pallas kernels  8.1 us (42%)
  waiting for transfers between devices  1.28 us (7%)
  between operations  0.75 us (4%)
    ppermute x6, starting transfers between devices, swap(): return lax.ppermute(x, ('az', 'rad'), pairs)  9.18 us
    pallas_call x1, Pallas kernels, rims(): pl.pallas_call(rim_kernel, out_shape=jax.ShapeDtypeStruct(main.shape, f32...  1.88 us
    pallas_call x1, Pallas kernels, edges(): pl.pallas_call(functools.partial(edges_kernel, cycle), out_shape=[jax.Sha...  1.77 us
    pallas_call x1, Pallas kernels, inner(): pl.pallas_call(inner_kernel, out_shape=[jax.ShapeDtypeStruct((layers, row...  1.69 us
    pallas_call x1, Pallas kernels, outer(): pl.pallas_call(outer_kernel, out_shape=[jax.ShapeDtypeStruct(pot.shape, f...  1.45 us
    ppermute x6, waiting for transfers between devices, swap(): return lax.ppermute(x, ('az', 'rad'), pairs)  1.28 us
    pallas_call x1, Pallas kernels, columns(): pl.pallas_call(columns_kernel, out_shape=jax.ShapeDtypeStruct((groups * c...  1.11 us
  transfers between devices with their start and end apart: 6, of which 3 were waited for; matrix products, arithmetic and copies ran while one was open for 0% of the time, Pallas kernels for 23%

profile of v3, /device:TPU:0, one launch (start us, length us, event | category | flops | bytes accessed | tf_op | source)
XLA Modules:
  0.0 19.3 jit_solution(9234928034817174231)
XLA Ops:
  0.7 0.0 copy-start
  0.7 0.0 copy-start.1
  0.7 0.0 copy-start.2
  0.7 1.8 %pack_rows.1 = (f32[62,128]{1,0:T(8,128)}, f32[62,128]{1,0:T(8,128)}, f32[20,128]{1,0:T(8,128)}, f32[16,128]{1,0:T(8,128)}) custom-call(s32[1]{0:T(128)S(6)} %copy.13.off_hbm, f32[8]{0:T(128)} %nu_hbm.1, f32[8]{0:T(128)} %sat_hbm.1, f32[9,256,128]{2,1,0:T(8,128)} %bitcast.4, f32[9,256,128]{2,1,0:T(8,128)} %bitcast.8, s32[3,256,128]{2,1,0:T(8,128)} %mat_ref.5, ...), custom_call_target="tpu_custom_call" | custom-call | flops 1000000 | bytes 400000 | tf_op jit(solution)/shard_map/pack_rows/pallas_call | solution.py:147
  2.5 6.0 %collective-permute-start = (f32[62,128]{1,0:T(8,128)}, f32[62,128]{1,0:T(8,128)S(1)}, u32[]{:S(2)}, u32[]{:S(2)}) collective-permute-start(f32[62,128]{1,0:T(8,128)} %get-tuple-element.18), channel_id=1, source_target_pairs={{0,28},{1,29},{2,30},{3,31},{4,8},{5,9},{6,10},{7,11},{8,4},{9,5},... | collective-permute-start | bytes 95240 | tf_op jit(solution)/shard_map/ppermute | solution.py:637
  8.5 0.0 collective-permute-start.1
  8.5 0.1 collective-permute-start.2
  8.6 0.0 copy-done
  8.6 0.0 copy-done.1
  8.6 1.1 %turn_columns.1.refs_5_.strips_ref = f32[256,256]{1,0:T(8,128)S(1)} custom-call(f32[9,256,128]{2,1,0:T(8,128)S(1)} %bitcast.5, f32[9,256,128]{2,1,0:T(8,128)S(1)} %bitcast.9, s32[3,256,128]{2,1,0:T(8,128)S(1)} %copy-done.2), custom_call_target="tpu_custom_call" | custom-call | flops 8000000 | bytes 3000000 | tf_op jit(solution)/shard_map/turn_columns/pallas_call | solution.py:209
  9.7 1.7 %inner_rows.1 = (f32[3,288,128]{2,1,0:T(8,128)S(1)}, f32[9,272,128]{2,1,0:T(8,128)S(1)}) custom-call(f32[16,128]{1,0:T(8,128)S(1)} %copy-done.3, f32[9,256,128]{2,1,0:T(8,128)S(1)} %bitcast.6, f32[9,256,128]{2,1,0:T(8,128)S(1)} %bitcast.10, s32[3,256,128]{2,1,0:T(8,128)S(1)} %copy-done.2), custom_call_target="tpu_custom_call" | custom-call | flops 20000000 | bytes 4000000 | tf_op jit(solution)/shard_map/inner_rows/pallas_call | solution.py:345
  11.4 1.0 %collective-permute-done.2.refs_3_ = f32[20,128]{1,0:T(8,128)S(1)} collective-permute-done((f32[20,128]{1,0:T(8,128)}, f32[20,128]{1,0:T(8,128)S(1)}, u32[]{:S(2)}, u32[]{:S(2)}) %collective-permute-start.2) | collective-permute-done | bytes 10272 | tf_op jit(solution)/shard_map/ppermute | solution.py:637
  12.4 0.0 collective-permute-done.odd_ref.refs_1_
  12.4 0.2 %collective-permute-done.1.even_ref.refs_2_ = f32[62,128]{1,0:T(8,128)S(1)} collective-permute-done((f32[62,128]{1,0:T(8,128)}, f32[62,128]{1,0:T(8,128)S(1)}, u32[]{:S(2)}, u32[]{:S(2)}) %collective-permute-start.1) | collective-permute-done | bytes 31776 | tf_op jit(solution)/shard_map/ppermute | solution.py:637
  12.6 1.0 %collective-permute-start.3 = (f32[16,256]{1,0:T(8,128)S(1)}, f32[16,256]{1,0:T(8,128)S(1)}, u32[]{:S(2)}, u32[]{:S(2)}) collective-permute-start(f32[16,256]{1,0:T(8,128)S(1)} %get-tuple-element.25), channel_id=1, source_target_pairs={{0,16},{1,17},{2,18},{3,19},{4,20},{5,21},{6,22},{7,23},{8,24},{9,... | collective-permute-start | bytes 49160 | tf_op jit(solution)/shard_map/ppermute | solution.py:637
  13.6 0.1 pack_columns.1
  13.7 0.1 collective-permute-start.4
  13.8 2.0 %collective-permute-start.5 = (f32[45,256]{1,0:T(8,128)S(1)}, f32[45,256]{1,0:T(8,128)S(1)}, u32[]{:S(2)}, u32[]{:S(2)}) collective-permute-start(f32[45,256]{1,0:T(8,128)S(1)} %get-tuple-element.28), channel_id=1, source_target_pairs={{0,1},{1,0},{2,3},{3,2},{4,5},{5,4},{6,7},{7,6},{8,9},{9,8},{10,11... | collective-permute-start | bytes 138248 | tf_op jit(solution)/shard_map/ppermute | solution.py:637
  15.8 1.4 %outer_rows.1 = (f32[9,256,128]{2,1,0:T(8,128)S(1)}, f32[3,288,128]{2,1,0:T(8,128)S(1)}, f32[9,272,128]{2,1,0:T(8,128)S(1)}) custom-call(f32[16,128]{1,0:T(8,128)S(1)} %copy-done.3, f32[9,256,128]{2,1,0:T(8,128)S(1)} %bitcast.7, f32[9,256,128]{2,1,0:T(8,128)S(1)} %bitcast.11, ...), custom_call_target="tpu_custom_call", output_to_operand_aliasing={{1}: (6, {}), {2}: (7, {})} | custom-call | flops 20000000 | bytes 4000000 | tf_op jit(solution)/shard_map/outer_rows/pallas_call | solution.py:420
  17.3 0.0 collective-permute-done.3.refs_1_
  17.3 0.1 airgap_sum.1.air_ref
  17.4 0.1 collective-permute-done.4.ro_ref
  17.4 0.0 collective-permute-done.5.re_ref
  17.4 1.9 %rims.1 = f32[9,256,128]{2,1,0:T(8,128)} custom-call(f32[16,128]{1,0:T(8,128)S(1)} %copy-done.3, f32[9,256,128]{2,1,0:T(8,128)S(1)} %get-tuple-element.22.refs_2_.main_ref, f32[16,384]{1,0:T(8,128)S(1)} %airgap_sum.1.air_ref, f32[256,256]{1,0:T(8,128)S(1)} %turn_columns.1.refs_5_.strips_ref, f32[128,128]{1,0:T(8,128)S(1)} %get-tuple-element.26.turned_ref, ...), custom_call_target="tpu_custom_call" | custom-call | tf_op jit(solution)/shard_map/rims/pallas_call | solution.py:610
  (6 shorter events, 0.0 us)
Async XLA Ops:
  0.7 7.9 %copy-start = (f32[3,3,256,128]{3,2,1,0:T(8,128)S(1)}, f32[3,3,256,128]{3,2,1,0:T(8,128)}, u32[]{:S(2)}) copy-start(f32[3,3,256,128]{3,2,1,0:T(8,128)} %param.8) | copy-start | bytes 3538948
  0.7 7.9 %copy-start.1 = (f32[3,3,256,128]{3,2,1,0:T(8,128)S(1)}, f32[3,3,256,128]{3,2,1,0:T(8,128)}, u32[]{:S(2)}) copy-start(f32[3,3,256,128]{3,2,1,0:T(8,128)} %param.9) | copy-start | bytes 3538948
  0.7 7.9 %copy-start.2 = (s32[3,256,128]{2,1,0:T(8,128)S(1)}, s32[3,256,128]{2,1,0:T(8,128)}, u32[]{:S(2)}) copy-start(s32[3,256,128]{2,1,0:T(8,128)} %mat_ref.5) | copy-start | bytes 1179652
  2.5 10.0 %collective-permute-start = (f32[62,128]{1,0:T(8,128)}, f32[62,128]{1,0:T(8,128)S(1)}, u32[]{:S(2)}, u32[]{:S(2)}) collective-permute-start(f32[62,128]{1,0:T(8,128)} %get-tuple-element.18), channel_id=1, source_target_pairs={{0,28},{1,29},{2,30},{3,31},{4,8},{5,9},{6,10},{7,11},{8,4},{9,5},... | collective-permute-start | bytes 95240 | tf_op jit(solution)/shard_map/ppermute | solution.py:637
  8.5 4.1 %collective-permute-start.1 = (f32[62,128]{1,0:T(8,128)}, f32[62,128]{1,0:T(8,128)S(1)}, u32[]{:S(2)}, u32[]{:S(2)}) collective-permute-start(f32[62,128]{1,0:T(8,128)} %get-tuple-element.19), channel_id=1, source_target_pairs={{0,4},{1,5},{2,6},{3,7},{4,0},{5,1},{6,2},{7,3},{8,12},{9,13},{10,... | collective-permute-start | bytes 95240 | tf_op jit(solution)/shard_map/ppermute | solution.py:637
  8.5 1.2 %copy-start.3 = (f32[16,128]{1,0:T(8,128)S(1)}, f32[16,128]{1,0:T(8,128)}, u32[]{:S(2)}) copy-start(f32[16,128]{1,0:T(8,128)} %get-tuple-element.17.table_ref) | copy-start | bytes 24580
  8.5 3.9 %collective-permute-start.2 = (f32[20,128]{1,0:T(8,128)}, f32[20,128]{1,0:T(8,128)S(1)}, u32[]{:S(2)}, u32[]{:S(2)}) collective-permute-start(f32[20,128]{1,0:T(8,128)} %get-tuple-element.23.refs_0_), channel_id=1, source_target_pairs={{0,8},{1,9},{2,10},{3,11},{4,12},{5,13},{6,14},{7,15},{8,0},{9,1},... | collective-permute-start | bytes 30728 | tf_op jit(solution)/shard_map/ppermute | solution.py:637
  9.7 2.9 %copy-start.4 = (f32[20,128]{1,0:T(8,128)S(1)}, f32[20,128]{1,0:T(8,128)}, u32[]{:S(2)}) copy-start(f32[20,128]{1,0:T(8,128)} %get-tuple-element.23.refs_0_) | copy-start | bytes 30724
  12.6 4.6 %collective-permute-start.3 = (f32[16,256]{1,0:T(8,128)S(1)}, f32[16,256]{1,0:T(8,128)S(1)}, u32[]{:S(2)}, u32[]{:S(2)}) collective-permute-start(f32[16,256]{1,0:T(8,128)S(1)} %get-tuple-element.25), channel_id=1, source_target_pairs={{0,16},{1,17},{2,18},{3,19},{4,20},{5,21},{6,22},{7,23},{8,24},{9,... | collective-permute-start | bytes 49160 | tf_op jit(solution)/shard_map/ppermute | solution.py:637
  13.7 3.7 %collective-permute-start.4 = (f32[45,256]{1,0:T(8,128)S(1)}, f32[45,256]{1,0:T(8,128)S(1)}, u32[]{:S(2)}, u32[]{:S(2)}) collective-permute-start(f32[45,256]{1,0:T(8,128)S(1)} %get-tuple-element.27), channel_id=1, source_target_pairs={{0,3},{1,2},{2,1},{3,0},{4,7},{5,6},{6,5},{7,4},{8,11},{9,10},{10,... | collective-permute-start | bytes 138248 | tf_op jit(solution)/shard_map/ppermute | solution.py:637
  13.8 3.6 %collective-permute-start.5 = (f32[45,256]{1,0:T(8,128)S(1)}, f32[45,256]{1,0:T(8,128)S(1)}, u32[]{:S(2)}, u32[]{:S(2)}) collective-permute-start(f32[45,256]{1,0:T(8,128)S(1)} %get-tuple-element.28), channel_id=1, source_target_pairs={{0,1},{1,0},{2,3},{3,2},{4,5},{5,4},{6,7},{7,6},{8,9},{9,8},{10,11... | collective-permute-start | bytes 138248 | tf_op jit(solution)/shard_map/ppermute | solution.py:637

commit v4 on v3

--- a/solution.py
+++ b/solution.py
@@ -8,7 +8,7 @@
 from jax.sharding import PartitionSpec as P
 
 sigma_term = 1.0
-LIMIT = 60
+
 EXPAND = 20_000_000_000
 halo = 3
 low_own, high_own = 6, 5
@@ -97,12 +97,12 @@
 
 
 def edges_kernel(
-    cycle, off_hbm, nu_hbm, sat_hbm, pot_hbm, cur_hbm, mat_hbm, flux_hbm, jit_hbm, odd_ref, even_ref, pan_ref, table_ref,
-    up_ref, down_ref, pot_ref, cur_ref, mat_ref, flux_ref, jit_ref, off_ref, nu_ref, sat_ref, sems
+    cycle, off_ref, nu_hbm, sat_hbm, pot_hbm, cur_hbm, mat_hbm, flux_hbm, jit_hbm, odd_ref, even_ref, pan_ref, table_ref,
+    up_ref, down_ref, pot_ref, cur_ref, mat_ref, flux_ref, jit_ref, nu_ref, sat_ref, sems
 ):
     fields, layers = pot_ref.shape[1], mat_ref.shape[1]
     rows = pot_hbm.shape[1]
-    pairs = [(flux_hbm, flux_ref), (jit_hbm, jit_ref), (off_hbm, off_ref), (nu_hbm, nu_ref), (sat_hbm, sat_ref)]
+    pairs = [(flux_hbm, flux_ref), (jit_hbm, jit_ref), (nu_hbm, nu_ref), (sat_hbm, sat_ref)]
     for hbm, ref in ((pot_hbm, pot_ref), (cur_hbm, cur_ref), (mat_hbm, mat_ref)):
         pairs += [(hbm.at[:, 0:8, :], ref.at[0]), (hbm.at[:, rows - 8 : rows, :], ref.at[1])]
     copies = [pltpu.make_async_copy(src, dst, sems.at[n]) for n, (src, dst) in enumerate(pairs)]
@@ -152,7 +152,7 @@
             jax.ShapeDtypeStruct((pan_rows, 128), f32),
             jax.ShapeDtypeStruct((2 * nu.shape[0], 128), f32),
         ],
-        in_specs=[HBM] * 8,
+        in_specs=[pl.BlockSpec(memory_space=pltpu.SMEM)] + [HBM] * 7,
         out_specs=[VMEM] * 4,
         scratch_shapes=[
             pltpu.VMEM((send, cols), f32),
@@ -162,15 +162,14 @@
             pltpu.VMEM((2, layers, 8, cols), jnp.int32),
             pltpu.VMEM(flux.shape, f32),
             pltpu.VMEM(jitter.shape, jnp.int32),
-            pltpu.SMEM(offset.shape, jnp.int32),
             pltpu.SMEM(nu.shape, f32),
             pltpu.SMEM(sat.shape, f32),
-            pltpu.SemaphoreType.DMA((11,)),
+            pltpu.SemaphoreType.DMA((10,)),
         ],
-        compiler_params=params(LIMIT),
+        compiler_params=params(),
         cost_estimate=pl.CostEstimate(flops=1_000_000, bytes_accessed=400_000, transcendentals=0),
         name="pack_rows",
-    )(offset, nu, sat, pot, cur, mat, flux, jitter)
+    )(offset, *(pltpu.with_memory_space_constraint(x, pltpu.HBM) for x in (nu, sat, pot, cur, mat, flux, jitter)))
 
 
 def columns_kernel(pot_ref, cur_ref, mat_ref, strips_ref, slots_ref):

time: 19.5 us -> 18.6 us (0.954)
  Pallas kernels: 8.1 us -> 7.47 us
  waiting for transfers between devices: 1.28 us -> 1.07 us
    pallas_call x1, Pallas kernels: 1.77 us -> 1.13 us  [edges(): pl.pallas_call(functools.partial(edges_kernel, cycle), out_shape=[jax.Sha...]
    ppermute x6, waiting for transfers between devices: 1.28 us -> 1.07 us  [swap(): return lax.ppermute(x, ('az', 'rad'), pairs)]
  transfers between devices with their start and end apart: 6 -> 6, of which waited for: 3 -> 3; matrix products, arithmetic and copies ran while one was open for 0% -> 0% of each run, Pallas kernels for 23% -> 24%
where the time goes in v4:
time: 18.6 us; the launch traced here: 18.4 us
  starting transfers between devices  9.17 us (49%)
  Pallas kernels  7.47 us (40%)
  waiting for transfers between devices  1.07 us (6%)
  between operations  0.72 us (4%)
    ppermute x6, starting transfers between devices, swap(): return lax.ppermute(x, ('az', 'rad'), pairs)  9.17 us
    pallas_call x1, Pallas kernels, rims(): pl.pallas_call(rim_kernel, out_shape=jax.ShapeDtypeStruct(main.shape, f32...  1.89 us
    pallas_call x1, Pallas kernels, inner(): pl.pallas_call(inner_kernel, out_shape=[jax.ShapeDtypeStruct((layers, row...  1.69 us
    pallas_call x1, Pallas kernels, outer(): pl.pallas_call(outer_kernel, out_shape=[jax.ShapeDtypeStruct(pot.shape, f...  1.45 us
    pallas_call x1, Pallas kernels, edges(): pl.pallas_call(functools.partial(edges_kernel, cycle), out_shape=[jax.Sha...  1.13 us
    pallas_call x1, Pallas kernels, columns(): pl.pallas_call(columns_kernel, out_shape=jax.ShapeDtypeStruct((groups * c...  1.11 us
    ppermute x6, waiting for transfers between devices, swap(): return lax.ppermute(x, ('az', 'rad'), pairs)  1.07 us
  transfers between devices with their start and end apart: 6, of which 3 were waited for; matrix products, arithmetic and copies ran while one was open for 0% of the time, Pallas kernels for 24%

profile of v4, /device:TPU:0, one launch (start us, length us, event | category | flops | bytes accessed | tf_op | source)
XLA Modules:
  0.0 18.4 jit_solution(1147743309849508209)
XLA Ops:
  0.7 0.0 copy-start
  0.7 0.0 copy-start.1
  0.7 0.0 copy-start.2
  0.7 1.1 %pack_rows.1 = (f32[62,128]{1,0:T(8,128)S(1)}, f32[62,128]{1,0:T(8,128)S(1)}, f32[20,128]{1,0:T(8,128)S(1)}, f32[16,128]{1,0:T(8,128)S(1)}) custom-call(s32[1]{0:T(128)S(6)} %copy.13.off_ref, f32[8]{0:T(128)} %nu_hbm.1, f32[8]{0:T(128)} %sat_hbm.1, f32[9,256,128]{2,1,0:T(8,128)} %bitcast.4, f32[9,256,128]{2,1,0:T(8,128)} %bitcast.8, s32[3,256,128]{2,1,0:T(8,128)} %mat_ref.5, ...), custom_call_target="tpu_custom_call" | custom-call | flops 1000000 | bytes 400000 | tf_op jit(solution)/shard_map/pack_rows/pallas_call | solution.py:147
  1.8 6.0 %collective-permute-start = (f32[62,128]{1,0:T(8,128)S(1)}, f32[62,128]{1,0:T(8,128)S(1)}, u32[]{:S(2)}, u32[]{:S(2)}) collective-permute-start(f32[62,128]{1,0:T(8,128)S(1)} %get-tuple-element.18), channel_id=1, source_target_pairs={{0,28},{1,29},{2,30},{3,31},{4,8},{5,9},{6,10},{7,11},{8,4},{9,5},... | collective-permute-start | bytes 95240 | tf_op jit(solution)/shard_map/ppermute | solution.py:636
  7.9 0.0 collective-permute-start.1
  7.9 0.1 collective-permute-start.2
  7.9 0.0 copy-done
  7.9 0.0 copy-done.1
  8.0 1.1 %turn_columns.1.refs_5_.strips_ref = f32[256,256]{1,0:T(8,128)S(1)} custom-call(f32[9,256,128]{2,1,0:T(8,128)S(1)} %bitcast.5, f32[9,256,128]{2,1,0:T(8,128)S(1)} %bitcast.9, s32[3,256,128]{2,1,0:T(8,128)S(1)} %copy-done.2), custom_call_target="tpu_custom_call" | custom-call | flops 8000000 | bytes 3000000 | tf_op jit(solution)/shard_map/turn_columns/pallas_call | solution.py:208
  9.1 1.7 %inner_rows.1 = (f32[3,288,128]{2,1,0:T(8,128)S(1)}, f32[9,272,128]{2,1,0:T(8,128)S(1)}) custom-call(f32[16,128]{1,0:T(8,128)S(1)} %get-tuple-element.17.table_ref, f32[9,256,128]{2,1,0:T(8,128)S(1)} %bitcast.6, f32[9,256,128]{2,1,0:T(8,128)S(1)} %bitcast.10, s32[3,256,128]{2,1,0:T(8,128)S(1)} %copy-done.2), custom_call_target="tpu_custom_call" | custom-call | flops 20000000 | bytes 4000000 | tf_op jit(solution)/shard_map/inner_rows/pallas_call | solution.py:344
  10.8 0.8 %collective-permute-done.2.refs_3_ = f32[20,128]{1,0:T(8,128)S(1)} collective-permute-done((f32[20,128]{1,0:T(8,128)S(1)}, f32[20,128]{1,0:T(8,128)S(1)}, u32[]{:S(2)}, u32[]{:S(2)}) %collective-permute-start.2) | collective-permute-done | bytes 10272 | tf_op jit(solution)/shard_map/ppermute | solution.py:636
  11.6 0.0 collective-permute-done.odd_ref.refs_1_
  11.6 0.2 %collective-permute-done.1.even_ref.refs_2_ = f32[62,128]{1,0:T(8,128)S(1)} collective-permute-done((f32[62,128]{1,0:T(8,128)S(1)}, f32[62,128]{1,0:T(8,128)S(1)}, u32[]{:S(2)}, u32[]{:S(2)}) %collective-permute-start.1) | collective-permute-done | bytes 31776 | tf_op jit(solution)/shard_map/ppermute | solution.py:636
  11.8 1.0 %collective-permute-start.3 = (f32[16,256]{1,0:T(8,128)S(1)}, f32[16,256]{1,0:T(8,128)S(1)}, u32[]{:S(2)}, u32[]{:S(2)}) collective-permute-start(f32[16,256]{1,0:T(8,128)S(1)} %get-tuple-element.25), channel_id=1, source_target_pairs={{0,16},{1,17},{2,18},{3,19},{4,20},{5,21},{6,22},{7,23},{8,24},{9,... | collective-permute-start | bytes 49160 | tf_op jit(solution)/shard_map/ppermute | solution.py:636
  12.7 0.1 pack_columns.1
  12.9 0.1 collective-permute-start.4
  12.9 2.0 %collective-permute-start.5 = (f32[45,256]{1,0:T(8,128)S(1)}, f32[45,256]{1,0:T(8,128)S(1)}, u32[]{:S(2)}, u32[]{:S(2)}) collective-permute-start(f32[45,256]{1,0:T(8,128)S(1)} %get-tuple-element.28), channel_id=1, source_target_pairs={{0,1},{1,0},{2,3},{3,2},{4,5},{5,4},{6,7},{7,6},{8,9},{9,8},{10,11... | collective-permute-start | bytes 138248 | tf_op jit(solution)/shard_map/ppermute | solution.py:636
  14.9 1.4 %outer_rows.1 = (f32[9,256,128]{2,1,0:T(8,128)S(1)}, f32[3,288,128]{2,1,0:T(8,128)S(1)}, f32[9,272,128]{2,1,0:T(8,128)S(1)}) custom-call(f32[16,128]{1,0:T(8,128)S(1)} %get-tuple-element.17.table_ref, f32[9,256,128]{2,1,0:T(8,128)S(1)} %bitcast.7, f32[9,256,128]{2,1,0:T(8,128)S(1)} %bitcast.11, ...), custom_call_target="tpu_custom_call", output_to_operand_aliasing={{1}: (6, {}), {2}: (7, {})} | custom-call | flops 20000000 | bytes 4000000 | tf_op jit(solution)/shard_map/outer_rows/pallas_call | solution.py:419
  16.4 0.0 collective-permute-done.3.refs_1_
  16.4 0.1 airgap_sum.1.air_ref
  16.5 0.1 collective-permute-done.4.ro_ref
  16.6 0.0 collective-permute-done.5.re_ref
  16.6 1.9 %rims.1 = f32[9,256,128]{2,1,0:T(8,128)} custom-call(f32[16,128]{1,0:T(8,128)S(1)} %get-tuple-element.17.table_ref, f32[9,256,128]{2,1,0:T(8,128)S(1)} %get-tuple-element.22.refs_2_.main_ref, f32[16,384]{1,0:T(8,128)S(1)} %airgap_sum.1.air_ref, f32[256,256]{1,0:T(8,128)S(1)} %turn_columns.1.refs_5_.strips_ref, f32[128,128]{1,0:T(8,128)S(1)} %get-tuple-element.26.turned_ref, ...), custom_call_target="tpu_custom_call" | custom-call | tf_op jit(solution)/shard_map/rims/pallas_call | solution.py:609
  (2 shorter events, 0.0 us)
Async XLA Ops:
  0.7 7.3 %copy-start = (f32[3,3,256,128]{3,2,1,0:T(8,128)S(1)}, f32[3,3,256,128]{3,2,1,0:T(8,128)}, u32[]{:S(2)}) copy-start(f32[3,3,256,128]{3,2,1,0:T(8,128)} %param.8) | copy-start | bytes 3538948
  0.7 7.3 %copy-start.1 = (f32[3,3,256,128]{3,2,1,0:T(8,128)S(1)}, f32[3,3,256,128]{3,2,1,0:T(8,128)}, u32[]{:S(2)}) copy-start(f32[3,3,256,128]{3,2,1,0:T(8,128)} %param.9) | copy-start | bytes 3538948
  0.7 7.3 %copy-start.2 = (s32[3,256,128]{2,1,0:T(8,128)S(1)}, s32[3,256,128]{2,1,0:T(8,128)}, u32[]{:S(2)}) copy-start(s32[3,256,128]{2,1,0:T(8,128)} %mat_ref.5) | copy-start | bytes 1179652
  1.8 9.7 %collective-permute-start = (f32[62,128]{1,0:T(8,128)S(1)}, f32[62,128]{1,0:T(8,128)S(1)}, u32[]{:S(2)}, u32[]{:S(2)}) collective-permute-start(f32[62,128]{1,0:T(8,128)S(1)} %get-tuple-element.18), channel_id=1, source_target_pairs={{0,28},{1,29},{2,30},{3,31},{4,8},{5,9},{6,10},{7,11},{8,4},{9,5},... | collective-permute-start | bytes 95240 | tf_op jit(solution)/shard_map/ppermute | solution.py:636
  7.9 3.9 %collective-permute-start.1 = (f32[62,128]{1,0:T(8,128)S(1)}, f32[62,128]{1,0:T(8,128)S(1)}, u32[]{:S(2)}, u32[]{:S(2)}) collective-permute-start(f32[62,128]{1,0:T(8,128)S(1)} %get-tuple-element.19), channel_id=1, source_target_pairs={{0,4},{1,5},{2,6},{3,7},{4,0},{5,1},{6,2},{7,3},{8,12},{9,13},{10,... | collective-permute-start | bytes 95240 | tf_op jit(solution)/shard_map/ppermute | solution.py:636
  7.9 3.7 %collective-permute-start.2 = (f32[20,128]{1,0:T(8,128)S(1)}, f32[20,128]{1,0:T(8,128)S(1)}, u32[]{:S(2)}, u32[]{:S(2)}) collective-permute-start(f32[20,128]{1,0:T(8,128)S(1)} %get-tuple-element.23.refs_0_), channel_id=1, source_target_pairs={{0,8},{1,9},{2,10},{3,11},{4,12},{5,13},{6,14},{7,15},{8,0},{9,1},... | collective-permute-start | bytes 30728 | tf_op jit(solution)/shard_map/ppermute | solution.py:636
  11.8 4.6 %collective-permute-start.3 = (f32[16,256]{1,0:T(8,128)S(1)}, f32[16,256]{1,0:T(8,128)S(1)}, u32[]{:S(2)}, u32[]{:S(2)}) collective-permute-start(f32[16,256]{1,0:T(8,128)S(1)} %get-tuple-element.25), channel_id=1, source_target_pairs={{0,16},{1,17},{2,18},{3,19},{4,20},{5,21},{6,22},{7,23},{8,24},{9,... | collective-permute-start | bytes 49160 | tf_op jit(solution)/shard_map/ppermute | solution.py:636
  12.9 3.7 %collective-permute-start.4 = (f32[45,256]{1,0:T(8,128)S(1)}, f32[45,256]{1,0:T(8,128)S(1)}, u32[]{:S(2)}, u32[]{:S(2)}) collective-permute-start(f32[45,256]{1,0:T(8,128)S(1)} %get-tuple-element.27), channel_id=1, source_target_pairs={{0,3},{1,2},{2,1},{3,0},{4,7},{5,6},{6,5},{7,4},{8,11},{9,10},{10,... | collective-permute-start | bytes 138248 | tf_op jit(solution)/shard_map/ppermute | solution.py:636
  12.9 3.6 %collective-permute-start.5 = (f32[45,256]{1,0:T(8,128)S(1)}, f32[45,256]{1,0:T(8,128)S(1)}, u32[]{:S(2)}, u32[]{:S(2)}) collective-permute-start(f32[45,256]{1,0:T(8,128)S(1)} %get-tuple-element.28), channel_id=1, source_target_pairs={{0,1},{1,0},{2,3},{3,2},{4,5},{5,4},{6,7},{7,6},{8,9},{9,8},{10,11... | collective-permute-start | bytes 138248 | tf_op jit(solution)/shard_map/ppermute | solution.py:636

commit v5 on v4

--- a/solution.py
+++ b/solution.py
@@ -10,11 +10,13 @@
 sigma_term = 1.0
 
 EXPAND = 20_000_000_000
+AHEAD = 0
 halo = 3
 low_own, high_own = 6, 5
 slot = low_own + high_own
 f32 = jnp.float32
 VMEM = pl.BlockSpec(memory_space=pltpu.VMEM)
+SMEM = pl.BlockSpec(memory_space=pltpu.SMEM)
 HBM = pl.BlockSpec(memory_space=pltpu.HBM)
 ANY = pl.BlockSpec(memory_space=pl.ANY)
 
@@ -97,7 +99,7 @@
 
 
 def edges_kernel(
-    cycle, off_ref, nu_hbm, sat_hbm, pot_hbm, cur_hbm, mat_hbm, flux_hbm, jit_hbm, odd_ref, even_ref, pan_ref, table_ref,
+    nu_hbm, sat_hbm, pot_hbm, cur_hbm, mat_hbm, flux_hbm, jit_hbm, odd_ref, even_ref, pan_ref, table_ref,
     up_ref, down_ref, pot_ref, cur_ref, mat_ref, flux_ref, jit_ref, nu_ref, sat_ref, sems
 ):
     fields, layers = pot_ref.shape[1], mat_ref.shape[1]
@@ -113,8 +115,7 @@
 
     odd_a = lax.rem(lax.axis_index("az"), 2) == 1
     panels = flux_ref.shape[1]
-    where = jit_ref[...] + off_ref[0]
-    where = jnp.where(where >= cycle, where - cycle, where).astype(f32)
+    where = jit_ref[...].astype(f32)
     for h in range(panels // 128):
         at = h * (fields + 1)
         pan_ref[at : at + fields, :] = flux_ref[:, h * 128 : (h + 1) * 128]
@@ -139,20 +140,20 @@
         table_ref[entries + e : entries + e + 1, :] = jnp.full((1, 128), sat_ref[e], f32)
 
 
-def edges(offset, nu, sat, pot, cur, mat, flux, jitter, cycle):
+def edges(nu, sat, pot, cur, mat, flux, jitter):
     fields, rows, cols = pot.shape
     layers = mat.shape[0]
     send = rim_rows(fields, layers)
     pan_rows = flux.shape[1] // 128 * (fields + 1)
     return pl.pallas_call(
-        functools.partial(edges_kernel, cycle),
+        edges_kernel,
         out_shape=[
             jax.ShapeDtypeStruct((send + pan_rows, cols), f32),
             jax.ShapeDtypeStruct((send + pan_rows, cols), f32),
             jax.ShapeDtypeStruct((pan_rows, 128), f32),
             jax.ShapeDtypeStruct((2 * nu.shape[0], 128), f32),
         ],
-        in_specs=[pl.BlockSpec(memory_space=pltpu.SMEM)] + [HBM] * 7,
+        in_specs=[HBM] * 7,
         out_specs=[VMEM] * 4,
         scratch_shapes=[
             pltpu.VMEM((send, cols), f32),
@@ -169,10 +170,10 @@
         compiler_params=params(),
         cost_estimate=pl.CostEstimate(flops=1_000_000, bytes_accessed=400_000, transcendentals=0),
         name="pack_rows",
-    )(offset, *(pltpu.with_memory_space_constraint(x, pltpu.HBM) for x in (nu, sat, pot, cur, mat, flux, jitter)))
-
-
-def columns_kernel(pot_ref, cur_ref, mat_ref, strips_ref, slots_ref):
+    )(*(pltpu.with_memory_space_constraint(x, pltpu.HBM) for x in (nu, sat, pot, cur, mat, flux, jitter)))
+
+
+def columns_kernel(_offset, pot_ref, cur_ref, mat_ref, strips_ref, slots_ref):
     fields, layers = pot_ref.shape[0], mat_ref.shape[0]
     rows, cols = mat_ref.shape[1:]
     total = 2 * fields + layers
@@ -180,7 +181,7 @@
     groups = -(-total // per)
     lane = lax.broadcasted_iota(jnp.int32, (8, cols), 1)
 
-    @pl.loop(0, rows // 8, unroll=8)
+    @pl.loop(0, rows // 8, unroll=32)
     def _(i):
         at = pl.ds(pl.multiple_of(i * 8, 8), 8)
         for g in range(groups):
@@ -201,20 +202,20 @@
         strips_ref[g * cols : (g + 1) * cols, :] = slots_ref[g].T
 
 
-def columns(pot, cur, mat):
+def columns(offset, pot, cur, mat):
     fields, rows, cols = pot.shape
     total = 2 * fields + mat.shape[0]
     groups = -(-total // (cols // slot))
     return pl.pallas_call(
         columns_kernel,
         out_shape=jax.ShapeDtypeStruct((groups * cols, rows), f32),
-        in_specs=[VMEM] * 3,
+        in_specs=[SMEM] + [VMEM] * 3,
         out_specs=VMEM,
         scratch_shapes=[pltpu.VMEM((groups, rows, cols), f32)],
         compiler_params=params(),
         cost_estimate=pl.CostEstimate(flops=8_000_000, bytes_accessed=3_000_000, transcendentals=0),
         name="turn_columns",
-    )(pot, cur, mat)
+    )(offset, pot, cur, mat)
 
 
 def middle_kernel(fields, layers, odd_ref, even_ref, strips_ref, _coef, _air, ro_ref, re_ref, turned_ref, rim_ref):
@@ -310,11 +311,11 @@
     return store
 
 
-def inner_kernel(table_ref, pot_ref, cur_ref, mat_ref, coef_ref, one_ref):
+def inner_kernel(table_ref, pot_ref, cur_ref, mat_ref, coef_ref, one_ref, out_ref):
     rows, cols = mat_ref.shape[1:]
     count = rows // 8
     inner = count - 2
-    step = divisor(inner, 10)
+    step = divisor(inner, 30)
 
     def load_at(i):
         return lambda j, step: pot_ref[j, pl.ds(i * 8 + step, 8), :]
@@ -336,6 +337,26 @@
     @pl.loop(1, count - 1, unroll=step)
     def _(i):
         sweep_block(coef_ref, load_at(i), lambda j: cur_ref[j, block(i), :], i, keep(one_ref, i))
+
+    ahead = AHEAD * (count - 4) // 4
+    if ahead:
+
+        @pl.loop(2, 2 + ahead, unroll=divisor(ahead, 10))
+        def _(i):
+            second_block(coef_ref, one_ref, cur_ref, out_ref, i)
+
+
+def second_block(coef_ref, one_ref, cur_ref, out_ref, i):
+    def store(j, x):
+        out_ref[j, block(i), :] = x
+
+    sweep_block(
+        coef_ref,
+        lambda j, step: one_ref[j, pl.ds(i * 8 + 8 + step, 8), :],
+        lambda j: cur_ref[j, block(i), :],
+        i,
+        store,
+    )
 
 
 def inner(table, pot, cur, mat):
@@ -346,9 +367,10 @@
         out_shape=[
             jax.ShapeDtypeStruct((layers, rows + 32, cols), f32),
             jax.ShapeDtypeStruct((fields, rows + 16, cols), f32),
+            jax.ShapeDtypeStruct(pot.shape, f32),
         ],
         in_specs=[VMEM] * 4,
-        out_specs=[VMEM, VMEM],
+        out_specs=[VMEM] * 3,
         compiler_params=params(),
         cost_estimate=pl.CostEstimate(flops=20_000_000, bytes_accessed=4_000_000, transcendentals=0),
         name="inner_rows",
@@ -356,7 +378,7 @@
 
 
 def outer_kernel(
-    table_ref, pot_ref, cur_ref, mat_ref, odd_ref, even_ref, coef_in, one_in, out_ref, coef_ref, one_ref, edge_ref
+    table_ref, pot_ref, cur_ref, mat_ref, odd_ref, even_ref, coef_in, one_in, out_in, coef_ref, one_ref, out_ref, edge_ref
 ):
     fields, rows, cols = out_ref.shape
     layers = mat_ref.shape[0]
@@ -398,44 +420,40 @@
         load, i = edge_load(k)
         sweep_block(coef_ref, load, lambda j: load(fields + layers + j, 0), i, keep(one_ref, i))
 
-    @pl.loop(0, count, unroll=divisor(count, 8))
-    def _(i):
-        def store(j, x):
-            out_ref[j, block(i), :] = x
-
-        sweep_block(
-            coef_ref,
-            lambda j, step: one_ref[j, pl.ds(i * 8 + 8 + step, 8), :],
-            lambda j: cur_ref[j, block(i), :],
-            i,
-            store,
-        )
-
-
-def outer(table, pot, cur, mat, odd_got, even_got, coef, one):
+    for i in (0, 1, count - 2, count - 1):
+        second_block(coef_ref, one_ref, cur_ref, out_ref, i)
+    ahead = AHEAD * (count - 4) // 4
+    if ahead < count - 4:
+
+        @pl.loop(2 + ahead, count - 2, unroll=divisor(count - 4 - ahead, 30))
+        def _(i):
+            second_block(coef_ref, one_ref, cur_ref, out_ref, i)
+
+
+def outer(table, pot, cur, mat, odd_got, even_got, coef, one, main):
     fields, rows, cols = pot.shape
     layers = mat.shape[0]
     total = 2 * fields + layers
     return pl.pallas_call(
         outer_kernel,
         out_shape=[
-            jax.ShapeDtypeStruct(pot.shape, f32),
             jax.ShapeDtypeStruct(coef.shape, f32),
             jax.ShapeDtypeStruct(one.shape, f32),
+            jax.ShapeDtypeStruct(main.shape, f32),
         ],
-        in_specs=[VMEM] * 8,
+        in_specs=[VMEM] * 9,
         out_specs=[VMEM] * 3,
-        input_output_aliases={6: 1, 7: 2},
+        input_output_aliases={6: 0, 7: 1, 8: 2},
         scratch_shapes=[pltpu.VMEM((2, total, 32, cols), f32)],
         compiler_params=params(),
         cost_estimate=pl.CostEstimate(flops=20_000_000, bytes_accessed=4_000_000, transcendentals=0),
         name="outer_rows",
-    )(table, pot, cur, mat, odd_got, even_got, coef, one)[0]
-
-
-def deposit_kernel(cycle, starts, bases, fields, rows, *refs):
+    )(table, pot, cur, mat, odd_got, even_got, coef, one, main)[2]
+
+
+def deposit_kernel(cycle, starts, bases, fields, rows, n_order, off_ref, *refs):
     n = len(starts)
-    pan_refs, air_refs, vals_ref = refs[:n], refs[n + 2 : -1], refs[-1]
+    pan_refs, air_refs, vals_ref = refs[:n], refs[n + n_order : -1], refs[-1]
     r, a = lax.axis_index("rad"), lax.axis_index("az")
     size = lax.axis_size("rad")
     stator = (r == size // 2) | (r == size // 2 - 1)
@@ -450,7 +468,8 @@
                 vals_ref[0 : fields + 1, t * 128 : (t + 1) * 128] = ref[at : at + fields + 1, :]
                 t += 1
         values = vals_ref[...]
-        position = vals_ref[fields : fields + 1, :].astype(jnp.int32)
+        position = vals_ref[fields : fields + 1, :].astype(jnp.int32) + off_ref[0]
+        position = jnp.where(position >= cycle, position - cycle, position)
         high = values.astype(jnp.bfloat16)
         rest = values - high.astype(f32)
         mid = rest.astype(jnp.bfloat16)
@@ -477,18 +496,18 @@
             air_ref[...] = jnp.zeros_like(air_ref)
 
 
-def deposit(pans, starts, order, bases, fields, rows, cycle):
+def deposit(name, offset, pans, starts, order, bases, fields, rows, cycle):
     panels = sum(p.shape[0] - first for p, first in zip(pans, starts)) // (fields + 1) * 128
     return pl.pallas_call(
-        functools.partial(deposit_kernel, cycle, starts, bases, fields, rows),
+        functools.partial(deposit_kernel, cycle, starts, bases, fields, rows, len(order)),
         out_shape=[jax.ShapeDtypeStruct((16, rows), f32) for _ in bases],
-        in_specs=[VMEM] * len(pans) + [ANY] * len(order),
+        in_specs=[SMEM] + [VMEM] * len(pans) + [ANY] * len(order),
         out_specs=[VMEM] * len(bases),
         scratch_shapes=[pltpu.VMEM((16, panels), f32)],
         compiler_params=params(),
         cost_estimate=pl.CostEstimate(flops=4_000_000, bytes_accessed=500_000, transcendentals=0),
-        name="airgap",
-    )(*pans, *order)
+        name=name,
+    )(offset, *pans, *order)
 
 
 def air_kernel(n, fields, *refs):
@@ -602,7 +621,7 @@
         pltpu.make_async_copy(merged_ref.at[j], out_hbm.at[j], sem.at[j]).wait()
 
 
-def rims(table, main, air, strips, turned, ro_got, re_got, layers):
+def rims(table, main, air, strips, turned, re_got, ro_got, layers):
     fields, rows, cols = main.shape
     total = 2 * fields + layers
     arrays = (main, air, strips, turned, ro_got, re_got)
@@ -632,10 +651,10 @@
     cur = current.reshape(fields, rows, cols)
 
     def swap(x, az_of, rad_of):
-        pairs = [(a * rad + r, az_of(a) * rad + rad_of(r)) for a in range(az) for r in range(rad)]
+        pairs = [(a * rad + r, az_of(a, r) * rad + rad_of(r)) for a in range(az) for r in range(rad)]
         return lax.ppermute(x, ("az", "rad"), pairs)
 
-    def same(i):
+    def same(i, r=None):
         return i
 
     def even(i):
@@ -645,32 +664,32 @@
         return (i + 1) % n if i % 2 else (i - 1) % n
 
     odd_send, even_send, pan, table = edges(
-        rotor_offset, nu_table, sat_table, pot, cur, material, panel_flux, panel_jitter.reshape(1, -1), cycle
+        nu_table, sat_table, pot, cur, material, panel_flux, panel_jitter.reshape(1, -1)
     )
-    odd_got = swap(odd_send, lambda a: odd(a, az), same)
-    even_got = swap(even_send, even, same)
-    two_got = swap(pan, lambda a: a ^ 2, same)
-    strips = columns(pot, cur, material)
-    coef, one = inner(table, pot, cur, material)
+    odd_got = swap(odd_send, lambda a, r: odd(a, az), same)
+    even_got = swap(even_send, lambda a, r: a ^ 1, same)
+    two_got = swap(pan, lambda a, r: a ^ 2, same)
+    strips = columns(rotor_offset, pot, cur, material)
+    coef, one, main = inner(table, pot, cur, material)
     at = rim_rows(fields, layers)
     pans, starts = [pan, odd_got, even_got, two_got], [0, at, at, 0]
     if az > 8:
         held, bit = jnp.concatenate([p[first:] for p, first in zip(pans, starts)], axis=0), 8
         while bit < az:
-            held = jnp.concatenate([held, swap(held, lambda a, bit=bit: a ^ bit, same)], axis=0)
+            held = jnp.concatenate([held, swap(held, lambda a, r, bit=bit: a ^ bit, same)], axis=0)
             bit *= 2
         pans, starts = [held], [0]
+    airs = []
     if az > 4:
-        air, air_send = deposit(pans, starts, (coef, strips), [0, 4], fields, rows, cycle)
-        airs = [air, swap(air_send, lambda a: a ^ 4, same)]
-    else:
-        airs = deposit(pans, starts, (coef, strips), [0], fields, rows, cycle)
-    ro_send, re_send, turned = middle(strips, odd_got, even_got, coef, airs[0], fields, layers)
+        send = deposit("airgap_far", rotor_offset, pans, starts, (coef, strips), [4], fields, rows, cycle)[0]
+        airs.append(swap(send, lambda a, r: a ^ 4, same))
+    ro_send, re_send, turned = middle(strips, odd_got, even_got, coef, send if airs else table, fields, layers)
     ro_got = swap(ro_send, same, lambda r: odd(r, rad))
     re_got = swap(re_send, same, even)
-    main = outer(table, pot, cur, material, odd_got, even_got, coef, one)
+    main = outer(table, pot, cur, material, odd_got, even_got, coef, one, main)
+    airs += deposit("airgap_own", rotor_offset, pans, starts, (main,), [0], fields, rows, cycle)
     air = gather_air(airs, main)
-    out = rims(table, main, air, strips, turned, ro_got, re_got, layers)
+    out = rims(table, main, air, strips, turned, re_got, ro_got, layers)
     return out.reshape(potential.shape)
 
 

time: 18.6 us -> 18 us (0.968)
  Pallas kernels: 7.47 us -> 6.55 us
  waiting for transfers between devices: 1.07 us -> 1.53 us
    ppermute x6, waiting for transfers between devices: 1.07 us -> 1.53 us  [swap(): return lax.ppermute(x, ('az', 'rad'), pairs)]
    pallas_call x1, Pallas kernels: 1.69 us -> 1.3 us  [inner(): pl.pallas_call(inner_kernel, out_shape=[jax.ShapeDtypeStruct((layers, row...]
    pallas_call x2, Pallas kernels: 2.58 us -> 2.28 us  [the longest x1 1.15 us: outer(): pl.pallas_call(outer_kernel, out_shape=[jax.ShapeDtypeStruct(coef.shape,...]
    pallas_call x1, Pallas kernels: 1.11 us -> 0.87 us  [columns(): pl.pallas_call(columns_kernel, out_shape=jax.ShapeDtypeStruct((groups * c...]
  transfers between devices with their start and end apart: 6 -> 6, of which waited for: 3 -> 4; matrix products, arithmetic and copies ran while one was open for 0% -> 0% of each run, Pallas kernels for 24% -> 20%
where the time goes in v5:
time: 18 us; the launch traced here: 17.8 us
  starting transfers between devices  9.02 us (50%)
  Pallas kernels  6.55 us (36%)
  waiting for transfers between devices  1.53 us (8%)
  between operations  0.73 us (4%)
    ppermute x6, starting transfers between devices, swap(): return lax.ppermute(x, ('az', 'rad'), pairs)  9.02 us
    pallas_call x1, Pallas kernels, rims(): pl.pallas_call(rim_kernel, out_shape=jax.ShapeDtypeStruct(main.shape, f32...  1.88 us
    ppermute x6, waiting for transfers between devices, swap(): return lax.ppermute(x, ('az', 'rad'), pairs)  1.53 us
    pallas_call x1, Pallas kernels, inner(): pl.pallas_call(inner_kernel, out_shape=[jax.ShapeDtypeStruct((layers, row...  1.3 us
    pallas_call x1, Pallas kernels, outer(): pl.pallas_call(outer_kernel, out_shape=[jax.ShapeDtypeStruct(coef.shape,...  1.15 us
    pallas_call x1, Pallas kernels, edges(): pl.pallas_call(edges_kernel, out_shape=[jax.ShapeDtypeStruct((send + pan_...  1.12 us
    pallas_call x1, Pallas kernels, columns(): pl.pallas_call(columns_kernel, out_shape=jax.ShapeDtypeStruct((groups * c...  0.87 us
  transfers between devices with their start and end apart: 6, of which 4 were waited for; matrix products, arithmetic and copies ran while one was open for 0% of the time, Pallas kernels for 20%

profile of v5, /device:TPU:0, one launch (start us, length us, event | category | flops | bytes accessed | tf_op | source)
XLA Modules:
  0.0 17.8 jit_solution(6439783498673836189)
XLA Ops:
  0.0 0.0 copy-start.1
  0.0 0.0 copy-start.2
  0.0 1.1 %pack_rows.1 = (f32[62,128]{1,0:T(8,128)S(1)}, f32[62,128]{1,0:T(8,128)S(1)}, f32[20,128]{1,0:T(8,128)S(1)}, f32[16,128]{1,0:T(8,128)S(1)}) custom-call(f32[8]{0:T(128)} %nu_hbm.1, f32[8]{0:T(128)} %sat_hbm.1, f32[9,256,128]{2,1,0:T(8,128)} %bitcast.4, f32[9,256,128]{2,1,0:T(8,128)} %bitcast.8, s32[3,256,128]{2,1,0:T(8,128)} %mat_ref.5, f32[9,256]{1,0:T(8,128)} %flux_hbm.1, ...), custom_call_target="tpu_custom_call" | custom-call | flops 1000000 | bytes 400000 | tf_op jit(solution)/shard_map/pack_rows/pallas_call | solution.py:148
  1.1 6.0 %collective-permute-start = (f32[62,128]{1,0:T(8,128)S(1)}, f32[62,128]{1,0:T(8,128)S(1)}, u32[]{:S(2)}, u32[]{:S(2)}) collective-permute-start(f32[62,128]{1,0:T(8,128)S(1)} %get-tuple-element.17), channel_id=1, source_target_pairs={{0,28},{1,29},{2,30},{3,31},{4,8},{5,9},{6,10},{7,11},{8,4},{9,5},... | collective-permute-start | bytes 95240 | tf_op jit(solution)/shard_map/ppermute | solution.py:655
  7.2 0.0 collective-permute-start.1
  7.2 0.1 collective-permute-start.2
  7.9 0.0 copy-done
  7.9 0.0 copy-done.1
  7.9 0.0 copy-done.2
  8.0 0.9 %turn_columns.1.refs_5_.strips_ref = f32[256,256]{1,0:T(8,128)S(1)} custom-call(s32[1]{0:T(128)S(6)} %copy.15._offset.off_ref, f32[9,256,128]{2,1,0:T(8,128)S(1)} %bitcast.5, f32[9,256,128]{2,1,0:T(8,128)S(1)} %bitcast.9, s32[3,256,128]{2,1,0:T(8,128)S(1)} %copy-done.2), custom_call_target="tpu_custom_call" | custom-call | flops 8000000 | bytes 3000000 | tf_op jit(solution)/shard_map/turn_columns/pallas_call | solution.py:209
  8.8 1.3 %inner_rows.1 = (f32[3,288,128]{2,1,0:T(8,128)S(1)}, f32[9,272,128]{2,1,0:T(8,128)S(1)}, f32[9,256,128]{2,1,0:T(8,128)S(1)}) custom-call(f32[16,128]{1,0:T(8,128)S(1)} %get-tuple-element.16.table_ref, f32[9,256,128]{2,1,0:T(8,128)S(1)} %bitcast.6, f32[9,256,128]{2,1,0:T(8,128)S(1)} %bitcast.10, s32[3,256,128]{2,1,0:T(8,128)S(1)} %copy-done.2), custom_call_target="tpu_custom_call" | custom-call | flops 20000000 | bytes 4000000 | tf_op jit(solution)/shard_map/inner_rows/pallas_call | solution.py:365
  10.1 0.7 %collective-permute-done.2.refs_3_ = f32[20,128]{1,0:T(8,128)S(1)} collective-permute-done((f32[20,128]{1,0:T(8,128)S(1)}, f32[20,128]{1,0:T(8,128)S(1)}, u32[]{:S(2)}, u32[]{:S(2)}) %collective-permute-start.2) | collective-permute-done | bytes 10272 | tf_op jit(solution)/shard_map/ppermute | solution.py:655
  10.9 0.0 collective-permute-done.odd_ref.refs_1_
  10.9 0.2 %collective-permute-done.1.even_ref.refs_2_ = f32[62,128]{1,0:T(8,128)S(1)} collective-permute-done((f32[62,128]{1,0:T(8,128)S(1)}, f32[62,128]{1,0:T(8,128)S(1)}, u32[]{:S(2)}, u32[]{:S(2)}) %collective-permute-start.1) | collective-permute-done | bytes 31776 | tf_op jit(solution)/shard_map/ppermute | solution.py:655
  11.1 1.0 %collective-permute-start.3 = (f32[16,256]{1,0:T(8,128)S(1)}, f32[16,256]{1,0:T(8,128)S(1)}, u32[]{:S(2)}, u32[]{:S(2)}) collective-permute-start(f32[16,256]{1,0:T(8,128)S(1)} %airgap_far.1._air), channel_id=1, source_target_pairs={{0,16},{1,17},{2,18},{3,19},{4,20},{5,21},{6,22},{7,23},{8,24},{9,... | collective-permute-start | bytes 49160 | tf_op jit(solution)/shard_map/ppermute | solution.py:655
  12.1 0.1 pack_columns.1
  12.2 0.1 collective-permute-start.4
  12.3 1.9 %collective-permute-start.5 = (f32[45,256]{1,0:T(8,128)S(1)}, f32[45,256]{1,0:T(8,128)S(1)}, u32[]{:S(2)}, u32[]{:S(2)}) collective-permute-start(f32[45,256]{1,0:T(8,128)S(1)} %get-tuple-element.26), channel_id=1, source_target_pairs={{0,1},{1,0},{2,3},{3,2},{4,5},{5,4},{6,7},{7,6},{8,9},{9,8},{10,11... | collective-permute-start | bytes 138248 | tf_op jit(solution)/shard_map/ppermute | solution.py:655
  14.1 1.2 %outer_rows.1 = (f32[3,288,128]{2,1,0:T(8,128)S(1)}, f32[9,272,128]{2,1,0:T(8,128)S(1)}, f32[9,256,128]{2,1,0:T(8,128)S(1)}) custom-call(f32[16,128]{1,0:T(8,128)S(1)} %get-tuple-element.16.table_ref, f32[9,256,128]{2,1,0:T(8,128)S(1)} %bitcast.7, f32[9,256,128]{2,1,0:T(8,128)S(1)} %bitcast.11, ...), custom_call_target="tpu_custom_call", output_to_operand_aliasing={{0}: (6, {}), {1}: (7, {}), {2}: (8, {})} | custom-call | flops 20000000 | bytes 4000000 | tf_op jit(solution)/shard_map/outer_rows/pallas_call | solution.py:437
  15.3 0.4 %collective-permute-done.3.refs_0_ = f32[16,256]{1,0:T(8,128)S(1)} collective-permute-done((f32[16,256]{1,0:T(8,128)S(1)}, f32[16,256]{1,0:T(8,128)S(1)}, u32[]{:S(2)}, u32[]{:S(2)}) %collective-permute-start.3) | collective-permute-done | bytes 16416 | tf_op jit(solution)/shard_map/ppermute | solution.py:655
  15.7 0.1 airgap_sum.1.air_ref
  15.8 0.1 collective-permute-done.4.ro_ref
  16.0 0.0 collective-permute-done.5.re_ref
  16.0 1.9 %rims.1 = f32[9,256,128]{2,1,0:T(8,128)} custom-call(f32[16,128]{1,0:T(8,128)S(1)} %get-tuple-element.16.table_ref, f32[9,256,128]{2,1,0:T(8,128)S(1)} %get-tuple-element.22.refs_4_.refs_2_.main_ref, f32[16,384]{1,0:T(8,128)S(1)} %airgap_sum.1.air_ref, f32[256,256]{1,0:T(8,128)S(1)} %turn_columns.1.refs_5_.strips_ref, ...), custom_call_target="tpu_custom_call" | custom-call | tf_op jit(solution)/shard_map/rims/pallas_call | solution.py:628
  (3 shorter events, 0.0 us)
Async XLA Ops:
  0.0 7.9 %copy-start = (f32[3,3,256,128]{3,2,1,0:T(8,128)S(1)}, f32[3,3,256,128]{3,2,1,0:T(8,128)}, u32[]{:S(2)}) copy-start(f32[3,3,256,128]{3,2,1,0:T(8,128)} %param.8) | copy-start | bytes 3538948
  0.0 7.9 %copy-start.1 = (f32[3,3,256,128]{3,2,1,0:T(8,128)S(1)}, f32[3,3,256,128]{3,2,1,0:T(8,128)}, u32[]{:S(2)}) copy-start(f32[3,3,256,128]{3,2,1,0:T(8,128)} %param.9) | copy-start | bytes 3538948
  0.0 7.9 %copy-start.2 = (s32[3,256,128]{2,1,0:T(8,128)S(1)}, s32[3,256,128]{2,1,0:T(8,128)}, u32[]{:S(2)}) copy-start(s32[3,256,128]{2,1,0:T(8,128)} %mat_ref.5) | copy-start | bytes 1179652
  1.1 9.7 %collective-permute-start = (f32[62,128]{1,0:T(8,128)S(1)}, f32[62,128]{1,0:T(8,128)S(1)}, u32[]{:S(2)}, u32[]{:S(2)}) collective-permute-start(f32[62,128]{1,0:T(8,128)S(1)} %get-tuple-element.17), channel_id=1, source_target_pairs={{0,28},{1,29},{2,30},{3,31},{4,8},{5,9},{6,10},{7,11},{8,4},{9,5},... | collective-permute-start | bytes 95240 | tf_op jit(solution)/shard_map/ppermute | solution.py:655
  7.2 3.9 %collective-permute-start.1 = (f32[62,128]{1,0:T(8,128)S(1)}, f32[62,128]{1,0:T(8,128)S(1)}, u32[]{:S(2)}, u32[]{:S(2)}) collective-permute-start(f32[62,128]{1,0:T(8,128)S(1)} %get-tuple-element.18), channel_id=1, source_target_pairs={{0,4},{1,5},{2,6},{3,7},{4,0},{5,1},{6,2},{7,3},{8,12},{9,13},{10,... | collective-permute-start | bytes 95240 | tf_op jit(solution)/shard_map/ppermute | solution.py:655
  7.2 3.7 %collective-permute-start.2 = (f32[20,128]{1,0:T(8,128)S(1)}, f32[20,128]{1,0:T(8,128)S(1)}, u32[]{:S(2)}, u32[]{:S(2)}) collective-permute-start(f32[20,128]{1,0:T(8,128)S(1)} %get-tuple-element.23.refs_0_), channel_id=1, source_target_pairs={{0,8},{1,9},{2,10},{3,11},{4,12},{5,13},{6,14},{7,15},{8,0},{9,1},... | collective-permute-start | bytes 30728 | tf_op jit(solution)/shard_map/ppermute | solution.py:655
  11.1 4.6 %collective-permute-start.3 = (f32[16,256]{1,0:T(8,128)S(1)}, f32[16,256]{1,0:T(8,128)S(1)}, u32[]{:S(2)}, u32[]{:S(2)}) collective-permute-start(f32[16,256]{1,0:T(8,128)S(1)} %airgap_far.1._air), channel_id=1, source_target_pairs={{0,16},{1,17},{2,18},{3,19},{4,20},{5,21},{6,22},{7,23},{8,24},{9,... | collective-permute-start | bytes 49160 | tf_op jit(solution)/shard_map/ppermute | solution.py:655
  12.2 3.8 %collective-permute-start.4 = (f32[45,256]{1,0:T(8,128)S(1)}, f32[45,256]{1,0:T(8,128)S(1)}, u32[]{:S(2)}, u32[]{:S(2)}) collective-permute-start(f32[45,256]{1,0:T(8,128)S(1)} %get-tuple-element.25), channel_id=1, source_target_pairs={{0,3},{1,2},{2,1},{3,0},{4,7},{5,6},{6,5},{7,4},{8,11},{9,10},{10,... | collective-permute-start | bytes 138248 | tf_op jit(solution)/shard_map/ppermute | solution.py:655
  12.3 3.7 %collective-permute-start.5 = (f32[45,256]{1,0:T(8,128)S(1)}, f32[45,256]{1,0:T(8,128)S(1)}, u32[]{:S(2)}, u32[]{:S(2)}) collective-permute-start(f32[45,256]{1,0:T(8,128)S(1)} %get-tuple-element.26), channel_id=1, source_target_pairs={{0,1},{1,0},{2,3},{3,2},{4,5},{5,4},{6,7},{7,6},{8,9},{9,8},{10,11... | collective-permute-start | bytes 138248 | tf_op jit(solution)/shard_map/ppermute | solution.py:655

commit v6 on v5

--- a/solution.py
+++ b/solution.py
@@ -218,7 +218,7 @@
     )(offset, pot, cur, mat)
 
 
-def middle_kernel(fields, layers, odd_ref, even_ref, strips_ref, _coef, _air, ro_ref, re_ref, turned_ref, rim_ref):
+def middle_kernel(fields, layers, odd_ref, even_ref, strips_ref, _coef, ro_ref, re_ref, turned_ref, rim_ref):
     cols = even_ref.shape[1]
     send = rim_rows(fields, layers)
     odd_r = lax.rem(lax.axis_index("rad"), 2) == 1
@@ -238,11 +238,11 @@
     ro_ref[send : send + halo, 0:128] = jnp.where(odd_r, hi, lo)
 
 
-def middle(strips, odd_got, even_got, coef, air, fields, layers):
+def middle(strips, odd_got, even_got, coef, fields, layers):
     cols = even_got.shape[1]
     rows = strips.shape[1]
     send = rim_rows(fields, layers)
-    arrays = (odd_got, even_got, strips, coef, air)
+    arrays = (odd_got, even_got, strips, coef)
     return pl.pallas_call(
         functools.partial(middle_kernel, fields, layers),
         out_shape=[
@@ -250,7 +250,7 @@
             jax.ShapeDtypeStruct((send + halo, rows), f32),
             jax.ShapeDtypeStruct((cols, 128), f32),
         ],
-        in_specs=[VMEM] * 3 + [ANY] * 2,
+        in_specs=[VMEM] * 3 + [ANY],
         out_specs=[VMEM] * 3,
         scratch_shapes=[pltpu.VMEM((128, cols), f32)],
         compiler_params=params(),
@@ -572,39 +572,44 @@
             lane < 64, pltpu.roll(corner, (-at) % 128, 1), pltpu.roll(corner, (64 - n - at) % 128, 1)
         )
 
-    column = lax.broadcasted_iota(jnp.int32, (16, rows + 128), 0)
+    def apart(x):
+        return x.reshape(2, 8, x.shape[1])
+
+    column = apart(lax.broadcasted_iota(jnp.int32, (16, rows + 128), 0))
     inside = ((column >= 2) | (r > 0)) & ((column < 13) | (r < size - 1))
     target = jnp.where(r == size // 2, 2, jnp.where(r == size // 2 - 1, 13, -1))
 
     def move(x, axis, step):
         return pltpu.roll(x, (-step) % x.shape[axis], axis)
 
-    pot = [[jnp.where(inside, cols_ref[c * layers + l], 0.0) for l in range(layers)] for c in range(comps)]
+    pot = [[jnp.where(inside, apart(cols_ref[c * layers + l]), 0.0) for l in range(layers)] for c in range(comps)]
     source = []
     for c in range(comps):
         source.append([])
         for l in range(layers):
             j = c * layers + l
-            air = air_ref[j : j + 1, :]
-            source[c].append(cols_ref[fields + layers + j] + jnp.where(column == target, air, 0.0))
+            air = air_ref[j : j + 1, :].reshape(1, 1, rows + 128)
+            source[c].append(apart(cols_ref[fields + layers + j]) + jnp.where(column == target, air, 0.0))
     coef = []
     for l in range(layers):
         centres = [pot[c][l] for c in range(comps)]
-        flux_sq = half_strength(centres, [move(x, 1, 1) for x in centres], [move(x, 0, 1) for x in centres])
+        flux_sq = half_strength(centres, [move(x, 2, 1) for x in centres], [move(x, 1, 1) for x in centres])
         which = cols_ref[fields + l].astype(jnp.int32)
-        k = half_reluct(table_ref, which, flux_sq)
+        k = apart(half_reluct(table_ref, which, flux_sq.reshape(16, rows + 128)))
         coef.append(jnp.where(inside, k, 0.0))
-    moves = [(axis, step) for axis in (1, 0) for step in (1, -1)]
+    moves = [(axis, step) for axis in (2, 1) for step in (1, -1)]
     moved = {(l, m): move(coef[l], *m) for l in range(layers) for m in moves}
 
-    def sweep(field):
+    def sweep(field, lanes):
         table = [
-            (lambda l, m=m: moved[l, m], lambda c, l, m=m: move(field[c][l], *m)) for m in moves
+            (lambda l, m=m: moved[l, m][..., :lanes], lambda c, l, m=m: move(field[c][l], *m)[..., :lanes])
+            for m in moves
         ]
-        return sweep_cells(coef, field, source, table)
-
-    one = [[jnp.where(inside, x, 0.0) for x in part] for part in sweep(pot)]
-    fixed = sweep(one)
+        cut = lambda part: [x[..., :lanes] for x in part]
+        return sweep_cells(cut(coef), [cut(part) for part in field], [cut(part) for part in source], table)
+
+    one = [[jnp.where(inside, x, 0.0) for x in part] for part in sweep(pot, rows + 128)]
+    fixed = [[x.reshape(16, rows) for x in part] for part in sweep(one, rows)]
     for c in range(comps):
         for l in range(layers):
             j = c * layers + l
@@ -663,6 +668,9 @@
     def odd(i, n):
         return (i + 1) % n if i % 2 else (i - 1) % n
 
+    def beside(r):
+        return r in (rad // 2 - 1, rad // 2)
+
     odd_send, even_send, pan, table = edges(
         nu_table, sat_table, pot, cur, material, panel_flux, panel_jitter.reshape(1, -1)
     )
@@ -679,11 +687,13 @@
             held = jnp.concatenate([held, swap(held, lambda a, r, bit=bit: a ^ bit, same)], axis=0)
             bit *= 2
         pans, starts = [held], [0]
+    ro_send, re_send, turned = middle(strips, odd_got, even_got, coef, fields, layers)
     airs = []
     if az > 4:
-        send = deposit("airgap_far", rotor_offset, pans, starts, (coef, strips), [4], fields, rows, cycle)[0]
-        airs.append(swap(send, lambda a, r: a ^ 4, same))
-    ro_send, re_send, turned = middle(strips, odd_got, even_got, coef, send if airs else table, fields, layers)
+        send = deposit("airgap_far", rotor_offset, pans, starts, (turned,), [4], fields, rows, cycle)[0]
+        airs.append(
+            swap(send, lambda a, r: a ^ 4 if beside(r) else a, lambda r: r if beside(r) else rad - 1 - r)
+        )
     ro_got = swap(ro_send, same, lambda r: odd(r, rad))
     re_got = swap(re_send, same, even)
     main = outer(table, pot, cur, material, odd_got, even_got, coef, one, main)

time: 18 us -> 17.3 us (0.961)
  waiting for transfers between devices: 1.53 us -> 0.83 us
  starting transfers between devices: 9.02 us -> 8.81 us
    ppermute x6, waiting for transfers between devices: 1.53 us -> 0.83 us  [swap(): return lax.ppermute(x, ('az', 'rad'), pairs)]
    ppermute x6, starting transfers between devices: 9.02 us -> 8.81 us  [swap(): return lax.ppermute(x, ('az', 'rad'), pairs)]
  transfers between devices with their start and end apart: 6 -> 6, of which waited for: 4 -> 1; matrix products, arithmetic and copies ran while one was open for 0% -> 0% of each run, Pallas kernels for 20% -> 21%
where the time goes in v6:
time: 17.3 us; the launch traced here: 17 us
  starting transfers between devices  8.81 us (51%)
  Pallas kernels  6.65 us (38%)
  waiting for transfers between devices  0.83 us (5%)
  between operations  0.75 us (4%)
    ppermute x6, starting transfers between devices, swap(): return lax.ppermute(x, ('az', 'rad'), pairs)  8.81 us
    pallas_call x1, Pallas kernels, rims(): pl.pallas_call(rim_kernel, out_shape=jax.ShapeDtypeStruct(main.shape, f32...  1.85 us
    pallas_call x1, Pallas kernels, inner(): pl.pallas_call(inner_kernel, out_shape=[jax.ShapeDtypeStruct((layers, row...  1.44 us
    pallas_call x1, Pallas kernels, edges(): pl.pallas_call(edges_kernel, out_shape=[jax.ShapeDtypeStruct((send + pan_...  1.12 us
    pallas_call x1, Pallas kernels, outer(): pl.pallas_call(outer_kernel, out_shape=[jax.ShapeDtypeStruct(coef.shape,...  1.12 us
    pallas_call x1, Pallas kernels, columns(): pl.pallas_call(columns_kernel, out_shape=jax.ShapeDtypeStruct((groups * c...  0.87 us
    ppermute x6, waiting for transfers between devices, swap(): return lax.ppermute(x, ('az', 'rad'), pairs)  0.83 us
  transfers between devices with their start and end apart: 6, of which 1 were waited for; matrix products, arithmetic and copies ran while one was open for 0% of the time, Pallas kernels for 21%

profile of v6, /device:TPU:0, one launch (start us, length us, event | category | flops | bytes accessed | tf_op | source)
XLA Modules:
  0.0 17.0 jit_solution(14728315347236326025)
XLA Ops:
  0.0 0.0 copy-start
  0.0 0.0 copy-start.1
  0.0 1.1 %pack_rows.1 = (f32[62,128]{1,0:T(8,128)S(1)}, f32[62,128]{1,0:T(8,128)S(1)}, f32[20,128]{1,0:T(8,128)S(1)}, f32[16,128]{1,0:T(8,128)S(1)}) custom-call(f32[8]{0:T(128)} %nu_hbm.1, f32[8]{0:T(128)} %sat_hbm.1, f32[9,256,128]{2,1,0:T(8,128)} %bitcast.4, f32[9,256,128]{2,1,0:T(8,128)} %bitcast.8, s32[3,256,128]{2,1,0:T(8,128)} %mat_ref.5, f32[9,256]{1,0:T(8,128)} %flux_hbm.1, ...), custom_call_target="tpu_custom_call" | custom-call | flops 1000000 | bytes 400000 | tf_op jit(solution)/shard_map/pack_rows/pallas_call | solution.py:148
  1.1 6.0 %collective-permute-start = (f32[62,128]{1,0:T(8,128)S(1)}, f32[62,128]{1,0:T(8,128)S(1)}, u32[]{:S(2)}, u32[]{:S(2)}) collective-permute-start(f32[62,128]{1,0:T(8,128)S(1)} %get-tuple-element.17), channel_id=1, source_target_pairs={{0,28},{1,29},{2,30},{3,31},{4,8},{5,9},{6,10},{7,11},{8,4},{9,5},... | collective-permute-start | bytes 95240 | tf_op jit(solution)/shard_map/ppermute | solution.py:660
  7.2 0.0 collective-permute-start.1
  7.2 0.1 collective-permute-start.2
  7.9 0.0 copy-done
  7.9 0.0 copy-done.1
  7.9 0.0 copy-done.2
  8.0 0.9 %turn_columns.1.strips_ref = f32[256,256]{1,0:T(8,128)S(1)} custom-call(s32[1]{0:T(128)S(6)} %copy.15._offset.off_ref, f32[9,256,128]{2,1,0:T(8,128)S(1)} %bitcast.5, f32[9,256,128]{2,1,0:T(8,128)S(1)} %bitcast.9, s32[3,256,128]{2,1,0:T(8,128)S(1)} %copy-done.2), custom_call_target="tpu_custom_call" | custom-call | flops 8000000 | bytes 3000000 | tf_op jit(solution)/shard_map/turn_columns/pallas_call | solution.py:209
  8.8 1.4 %inner_rows.1 = (f32[3,288,128]{2,1,0:T(8,128)S(1)}, f32[9,272,128]{2,1,0:T(8,128)S(1)}, f32[9,256,128]{2,1,0:T(8,128)S(1)}) custom-call(f32[16,128]{1,0:T(8,128)S(1)} %get-tuple-element.16.table_ref, f32[9,256,128]{2,1,0:T(8,128)S(1)} %bitcast.6, f32[9,256,128]{2,1,0:T(8,128)S(1)} %bitcast.10, s32[3,256,128]{2,1,0:T(8,128)S(1)} %copy-done.2), custom_call_target="tpu_custom_call" | custom-call | flops 20000000 | bytes 4000000 | tf_op jit(solution)/shard_map/inner_rows/pallas_call | solution.py:365
  10.3 0.0 collective-permute-done.odd_ref.refs_1_
  10.3 0.8 %collective-permute-done.1.even_ref.refs_2_ = f32[62,128]{1,0:T(8,128)S(1)} collective-permute-done((f32[62,128]{1,0:T(8,128)S(1)}, f32[62,128]{1,0:T(8,128)S(1)}, u32[]{:S(2)}, u32[]{:S(2)}) %collective-permute-start.1) | collective-permute-done | bytes 31776 | tf_op jit(solution)/shard_map/ppermute | solution.py:660
  11.1 0.1 pack_columns.1
  11.2 0.0 collective-permute-done.2.refs_3_
  11.2 0.1 collective-permute-start.3
  11.3 1.7 %collective-permute-start.4 = (f32[45,256]{1,0:T(8,128)S(1)}, f32[45,256]{1,0:T(8,128)S(1)}, u32[]{:S(2)}, u32[]{:S(2)}) collective-permute-start(f32[45,256]{1,0:T(8,128)S(1)} %get-tuple-element.25), channel_id=1, source_target_pairs={{0,3},{1,2},{2,1},{3,0},{4,7},{5,6},{6,5},{7,4},{8,11},{9,10},{10,... | collective-permute-start | bytes 138248 | tf_op jit(solution)/shard_map/ppermute | solution.py:660
  13.1 0.9 %collective-permute-start.5 = (f32[45,256]{1,0:T(8,128)S(1)}, f32[45,256]{1,0:T(8,128)S(1)}, u32[]{:S(2)}, u32[]{:S(2)}) collective-permute-start(f32[45,256]{1,0:T(8,128)S(1)} %get-tuple-element.26), channel_id=1, source_target_pairs={{0,1},{1,0},{2,3},{3,2},{4,5},{5,4},{6,7},{7,6},{8,9},{9,8},{10,11... | collective-permute-start | bytes 138248 | tf_op jit(solution)/shard_map/ppermute | solution.py:660
  13.9 1.1 %outer_rows.1 = (f32[3,288,128]{2,1,0:T(8,128)S(1)}, f32[9,272,128]{2,1,0:T(8,128)S(1)}, f32[9,256,128]{2,1,0:T(8,128)S(1)}) custom-call(f32[16,128]{1,0:T(8,128)S(1)} %get-tuple-element.16.table_ref, f32[9,256,128]{2,1,0:T(8,128)S(1)} %bitcast.7, f32[9,256,128]{2,1,0:T(8,128)S(1)} %bitcast.11, ...), custom_call_target="tpu_custom_call", output_to_operand_aliasing={{0}: (6, {}), {1}: (7, {}), {2}: (8, {})} | custom-call | flops 20000000 | bytes 4000000 | tf_op jit(solution)/shard_map/outer_rows/pallas_call | solution.py:437
  15.1 0.0 collective-permute-done.3.refs_0_
  15.1 0.1 airgap_sum.1.air_ref
  15.2 0.0 collective-permute-done.4.ro_ref
  15.2 0.0 collective-permute-done.5.re_ref
  15.2 1.8 %rims.1 = f32[9,256,128]{2,1,0:T(8,128)} custom-call(f32[16,128]{1,0:T(8,128)S(1)} %get-tuple-element.16.table_ref, f32[9,256,128]{2,1,0:T(8,128)S(1)} %get-tuple-element.22.refs_4_.refs_2_.main_ref, f32[16,384]{1,0:T(8,128)S(1)} %airgap_sum.1.air_ref, f32[256,256]{1,0:T(8,128)S(1)} %turn_columns.1.strips_ref, ...), custom_call_target="tpu_custom_call" | custom-call | tf_op jit(solution)/shard_map/rims/pallas_call | solution.py:633
  (3 shorter events, 0.0 us)
Async XLA Ops:
  0.0 7.9 %copy-start = (f32[3,3,256,128]{3,2,1,0:T(8,128)S(1)}, f32[3,3,256,128]{3,2,1,0:T(8,128)}, u32[]{:S(2)}) copy-start(f32[3,3,256,128]{3,2,1,0:T(8,128)} %param.8) | copy-start | bytes 3538948
  0.0 7.9 %copy-start.1 = (f32[3,3,256,128]{3,2,1,0:T(8,128)S(1)}, f32[3,3,256,128]{3,2,1,0:T(8,128)}, u32[]{:S(2)}) copy-start(f32[3,3,256,128]{3,2,1,0:T(8,128)} %param.9) | copy-start | bytes 3538948
  0.0 7.9 %copy-start.2 = (s32[3,256,128]{2,1,0:T(8,128)S(1)}, s32[3,256,128]{2,1,0:T(8,128)}, u32[]{:S(2)}) copy-start(s32[3,256,128]{2,1,0:T(8,128)} %mat_ref.5) | copy-start | bytes 1179652
  1.1 9.1 %collective-permute-start = (f32[62,128]{1,0:T(8,128)S(1)}, f32[62,128]{1,0:T(8,128)S(1)}, u32[]{:S(2)}, u32[]{:S(2)}) collective-permute-start(f32[62,128]{1,0:T(8,128)S(1)} %get-tuple-element.17), channel_id=1, source_target_pairs={{0,28},{1,29},{2,30},{3,31},{4,8},{5,9},{6,10},{7,11},{8,4},{9,5},... | collective-permute-start | bytes 95240 | tf_op jit(solution)/shard_map/ppermute | solution.py:660
  7.2 3.9 %collective-permute-start.1 = (f32[62,128]{1,0:T(8,128)S(1)}, f32[62,128]{1,0:T(8,128)S(1)}, u32[]{:S(2)}, u32[]{:S(2)}) collective-permute-start(f32[62,128]{1,0:T(8,128)S(1)} %get-tuple-element.18), channel_id=1, source_target_pairs={{0,4},{1,5},{2,6},{3,7},{4,0},{5,1},{6,2},{7,3},{8,12},{9,13},{10,... | collective-permute-start | bytes 95240 | tf_op jit(solution)/shard_map/ppermute | solution.py:660
  7.2 4.0 %collective-permute-start.2 = (f32[20,128]{1,0:T(8,128)S(1)}, f32[20,128]{1,0:T(8,128)S(1)}, u32[]{:S(2)}, u32[]{:S(2)}) collective-permute-start(f32[20,128]{1,0:T(8,128)S(1)} %get-tuple-element.23.refs_0_), channel_id=1, source_target_pairs={{0,8},{1,9},{2,10},{3,11},{4,12},{5,13},{6,14},{7,15},{8,0},{9,1},... | collective-permute-start | bytes 30728 | tf_op jit(solution)/shard_map/ppermute | solution.py:660
  11.2 3.8 %collective-permute-start.3 = (f32[16,256]{1,0:T(8,128)S(1)}, f32[16,256]{1,0:T(8,128)S(1)}, u32[]{:S(2)}, u32[]{:S(2)}) collective-permute-start(f32[16,256]{1,0:T(8,128)S(1)} %airgap_far.1), channel_id=1, source_target_pairs={{0,3},{1,17},{2,18},{3,0},{4,7},{5,21},{6,22},{7,4},{8,11},{9,25},... | collective-permute-start | bytes 49160 | tf_op jit(solution)/shard_map/ppermute | solution.py:660
  11.3 3.9 %collective-permute-start.4 = (f32[45,256]{1,0:T(8,128)S(1)}, f32[45,256]{1,0:T(8,128)S(1)}, u32[]{:S(2)}, u32[]{:S(2)}) collective-permute-start(f32[45,256]{1,0:T(8,128)S(1)} %get-tuple-element.25), channel_id=1, source_target_pairs={{0,3},{1,2},{2,1},{3,0},{4,7},{5,6},{6,5},{7,4},{8,11},{9,10},{10,... | collective-permute-start | bytes 138248 | tf_op jit(solution)/shard_map/ppermute | solution.py:660
  13.1 2.1 %collective-permute-start.5 = (f32[45,256]{1,0:T(8,128)S(1)}, f32[45,256]{1,0:T(8,128)S(1)}, u32[]{:S(2)}, u32[]{:S(2)}) collective-permute-start(f32[45,256]{1,0:T(8,128)S(1)} %get-tuple-element.26), channel_id=1, source_target_pairs={{0,1},{1,0},{2,3},{3,2},{4,5},{5,4},{6,7},{7,6},{8,9},{9,8},{10,11... | collective-permute-start | bytes 138248 | tf_op jit(solution)/shard_map/ppermute | solution.py:660

commit v7 on v6

--- a/solution.py
+++ b/solution.py
@@ -173,7 +173,7 @@
     )(*(pltpu.with_memory_space_constraint(x, pltpu.HBM) for x in (nu, sat, pot, cur, mat, flux, jitter)))
 
 
-def columns_kernel(_offset, pot_ref, cur_ref, mat_ref, strips_ref, slots_ref):
+def columns_kernel(_offset, pot_ref, cur_ref, mat_ref, cols_ref, slots_ref, strips_ref):
     fields, layers = pot_ref.shape[0], mat_ref.shape[0]
     rows, cols = mat_ref.shape[1:]
     total = 2 * fields + layers
@@ -200,6 +200,10 @@
 
     for g in range(groups):
         strips_ref[g * cols : (g + 1) * cols, :] = slots_ref[g].T
+    for j in range(total):
+        b = slot_base(j, cols)
+        cols_ref[j, 0:8, 0:rows] = strips_ref[b + high_own - 2 : b + high_own + 6, :]
+        cols_ref[j, 8:16, 0:rows] = strips_ref[b : b + 8, :]
 
 
 def columns(offset, pot, cur, mat):
@@ -208,29 +212,30 @@
     groups = -(-total // (cols // slot))
     return pl.pallas_call(
         columns_kernel,
-        out_shape=jax.ShapeDtypeStruct((groups * cols, rows), f32),
+        out_shape=jax.ShapeDtypeStruct((total, 16, rows + 128), f32),
         in_specs=[SMEM] + [VMEM] * 3,
         out_specs=VMEM,
-        scratch_shapes=[pltpu.VMEM((groups, rows, cols), f32)],
+        scratch_shapes=[pltpu.VMEM((groups, rows, cols), f32), pltpu.VMEM((groups * cols, rows), f32)],
         compiler_params=params(),
         cost_estimate=pl.CostEstimate(flops=8_000_000, bytes_accessed=3_000_000, transcendentals=0),
         name="turn_columns",
     )(offset, pot, cur, mat)
 
 
-def middle_kernel(fields, layers, odd_ref, even_ref, strips_ref, _coef, ro_ref, re_ref, turned_ref, rim_ref):
+def middle_kernel(fields, layers, n_order, odd_ref, even_ref, strips_ref, *refs):
+    ro_ref, re_ref, turned_ref, rim_ref = refs[n_order:]
     cols = even_ref.shape[1]
     send = rim_rows(fields, layers)
     odd_r = lax.rem(lax.axis_index("rad"), 2) == 1
     odd_a = lax.rem(lax.axis_index("az"), 2) == 1
 
+    rows = ro_ref.shape[1]
     rim_ref[0:send, :] = jnp.where(odd_a, odd_ref[0:send, :], even_ref[0:send, :])
     rim_ref[64 : 64 + send, :] = jnp.where(odd_a, even_ref[0:send, :], odd_ref[0:send, :])
     turned_ref[...] = rim_ref[...].T
 
     for j, (n, at) in enumerate(layout(fields, layers)):
-        b = slot_base(j, cols) + high_own
-        lo, hi = strips_ref[b : b + n, :], strips_ref[b - n : b, :]
+        lo, hi = strips_ref[j, 2 : 2 + n, 0:rows], strips_ref[j, 13 - n : 13, 0:rows]
         re_ref[at : at + n, :] = jnp.where(odd_r, lo, hi)
         ro_ref[at : at + n, :] = jnp.where(odd_r, hi, lo)
     lo, hi = turned_ref[0:halo, :], turned_ref[cols - halo : cols, :]
@@ -238,19 +243,19 @@
     ro_ref[send : send + halo, 0:128] = jnp.where(odd_r, hi, lo)
 
 
-def middle(strips, odd_got, even_got, coef, fields, layers):
+def middle(strips, odd_got, even_got, order, fields, layers):
     cols = even_got.shape[1]
-    rows = strips.shape[1]
+    rows = strips.shape[2] - 128
     send = rim_rows(fields, layers)
-    arrays = (odd_got, even_got, strips, coef)
+    arrays = (odd_got, even_got, strips, *order)
     return pl.pallas_call(
-        functools.partial(middle_kernel, fields, layers),
+        functools.partial(middle_kernel, fields, layers, len(order)),
         out_shape=[
             jax.ShapeDtypeStruct((send + halo, rows), f32),
             jax.ShapeDtypeStruct((send + halo, rows), f32),
             jax.ShapeDtypeStruct((cols, 128), f32),
         ],
-        in_specs=[VMEM] * 3 + [ANY],
+        in_specs=[VMEM] * 3 + [ANY] * len(order),
         out_specs=[VMEM] * 3,
         scratch_shapes=[pltpu.VMEM((128, cols), f32)],
         compiler_params=params(),
@@ -451,9 +456,9 @@
     )(table, pot, cur, mat, odd_got, even_got, coef, one, main)[2]
 
 
-def deposit_kernel(cycle, starts, bases, fields, rows, n_order, off_ref, *refs):
+def deposit_kernel(cycle, starts, bases, fields, rows, added, n_order, off_ref, *refs):
     n = len(starts)
-    pan_refs, air_refs, vals_ref = refs[:n], refs[n + n_order : -1], refs[-1]
+    pan_refs, air_refs, vals_ref = refs[:n], refs[n + added + n_order : -1], refs[-1]
     r, a = lax.axis_index("rad"), lax.axis_index("az")
     size = lax.axis_size("rad")
     stator = (r == size // 2) | (r == size // 2 - 1)
@@ -489,6 +494,8 @@
             before = jnp.sum(jnp.where(before, values, 0.0), axis=1, keepdims=True)
             outside = jnp.where(lane == channel, after, jnp.where(lane == channel + 16, before, 0.0))
             air_ref[fields : fields + 1, 0:128] = jnp.sum(outside, axis=0, keepdims=True)
+            if added:
+                air_ref[...] += refs[n][...]
 
     @pl.when(jnp.logical_not(stator))
     def _():
@@ -496,18 +503,18 @@
             air_ref[...] = jnp.zeros_like(air_ref)
 
 
-def deposit(name, offset, pans, starts, order, bases, fields, rows, cycle):
+def deposit(name, offset, pans, starts, order, bases, fields, rows, cycle, added=()):
     panels = sum(p.shape[0] - first for p, first in zip(pans, starts)) // (fields + 1) * 128
     return pl.pallas_call(
-        functools.partial(deposit_kernel, cycle, starts, bases, fields, rows, len(order)),
+        functools.partial(deposit_kernel, cycle, starts, bases, fields, rows, len(added), len(order)),
         out_shape=[jax.ShapeDtypeStruct((16, rows), f32) for _ in bases],
-        in_specs=[SMEM] + [VMEM] * len(pans) + [ANY] * len(order),
+        in_specs=[SMEM] + [VMEM] * (len(pans) + len(added)) + [ANY] * len(order),
         out_specs=[VMEM] * len(bases),
         scratch_shapes=[pltpu.VMEM((16, panels), f32)],
         compiler_params=params(),
         cost_estimate=pl.CostEstimate(flops=4_000_000, bytes_accessed=500_000, transcendentals=0),
         name=name,
-    )(offset, *pans, *order)
+    )(offset, *pans, *added, *order)
 
 
 def air_kernel(n, fields, *refs):
@@ -537,8 +544,8 @@
 
 
 def rim_kernel(
-    table_ref, main_ref, air_ref, strips_ref, turned_ref, ro_ref, re_ref,
-    out_hbm, merged_ref, cols_ref, corner_ref, back_ref, sem,
+    table_ref, main_ref, air_ref, _cols, turned_ref, ro_ref, re_ref,
+    out_hbm, cols_ref, merged_ref, corner_ref, back_ref, sem,
 ):
     fields, rows, cols = main_ref.shape
     total = cols_ref.shape[0]
@@ -562,9 +569,6 @@
     corner = corner_ref[...]
     lane = lax.broadcasted_iota(jnp.int32, (16, 128), 1)
     for j, (n, at) in enumerate(layout(fields, layers)):
-        b = slot_base(j, cols)
-        cols_ref[j, 0:8, 0:rows] = strips_ref[b + high_own - 2 : b + high_own + 6, :]
-        cols_ref[j, 8:16, 0:rows] = strips_ref[b : b + 8, :]
         m = min(n, 2)
         cols_ref[j, 2 - m : 2, 0:rows] = left(at + n - m, m)
         cols_ref[j, 13 : 13 + n, 0:rows] = right(at, n)
@@ -632,19 +636,19 @@
     arrays = (main, air, strips, turned, ro_got, re_got)
     return pl.pallas_call(
         rim_kernel,
-        out_shape=jax.ShapeDtypeStruct(main.shape, f32),
+        out_shape=[jax.ShapeDtypeStruct(main.shape, f32), jax.ShapeDtypeStruct(strips.shape, f32)],
         in_specs=[VMEM] * (1 + len(arrays)),
-        out_specs=ANY,
+        out_specs=[ANY, VMEM],
+        input_output_aliases={3: 1},
         scratch_shapes=[
             pltpu.VMEM(main.shape, f32),
-            pltpu.VMEM((total, 16, rows + 128), f32),
             pltpu.VMEM((16, 128), f32),
             pltpu.VMEM((128, rows), f32),
             pltpu.SemaphoreType.DMA((fields,)),
         ],
         compiler_params=params(),
         name="rims",
-    )(table, *arrays)
+    )(table, *arrays)[0]
 
 
 def local(potential, current, material, nu_table, sat_table, panel_flux, panel_jitter, rotor_offset):
@@ -687,10 +691,16 @@
             held = jnp.concatenate([held, swap(held, lambda a, r, bit=bit: a ^ bit, same)], axis=0)
             bit *= 2
         pans, starts = [held], [0]
-    ro_send, re_send, turned = middle(strips, odd_got, even_got, coef, fields, layers)
+    early = ()
+    if 4 < az <= 8:
+        early = deposit("airgap_early", rotor_offset, pans[:2], starts[:2], (coef, strips), [4], fields, rows, cycle)
+    ro_send, re_send, turned = middle(strips, odd_got, even_got, (coef, *early), fields, layers)
     airs = []
     if az > 4:
-        send = deposit("airgap_far", rotor_offset, pans, starts, (turned,), [4], fields, rows, cycle)[0]
+        rest = slice(2 if early else 0, None)
+        send = deposit(
+            "airgap_far", rotor_offset, pans[rest], starts[rest], (turned,), [4], fields, rows, cycle, early
+        )[0]
         airs.append(
             swap(send, lambda a, r: a ^ 4 if beside(r) else a, lambda r: r if beside(r) else rad - 1 - r)
         )

time: 17.3 us -> 17.2 us (level)
  transfers between devices with their start and end apart: 6 -> 6, of which waited for: 1 -> 1; matrix products, arithmetic and copies ran while one was open for 0% -> 0% of each run, Pallas kernels for 21% -> 22%
where the time goes in v7:
time: 17.2 us; the launch traced here: 17 us
  starting transfers between devices  8.72 us (51%)
  Pallas kernels  6.67 us (39%)
  waiting for transfers between devices  0.8 us (5%)
  between operations  0.76 us (4%)
    ppermute x6, starting transfers between devices, swap(): return lax.ppermute(x, ('az', 'rad'), pairs)  8.72 us
    pallas_call x1, Pallas kernels, rims(): pl.pallas_call(rim_kernel, out_shape=[jax.ShapeDtypeStruct(main.shape, f3...  1.84 us
    pallas_call x1, Pallas kernels, inner(): pl.pallas_call(inner_kernel, out_shape=[jax.ShapeDtypeStruct((layers, row...  1.42 us
    pallas_call x1, Pallas kernels, edges(): pl.pallas_call(edges_kernel, out_shape=[jax.ShapeDtypeStruct((send + pan_...  1.12 us
    pallas_call x1, Pallas kernels, outer(): pl.pallas_call(outer_kernel, out_shape=[jax.ShapeDtypeStruct(coef.shape,...  1.12 us
    pallas_call x1, Pallas kernels, columns(): pl.pallas_call(columns_kernel, out_shape=jax.ShapeDtypeStruct((total, 16,...  0.91 us
    ppermute x6, waiting for transfers between devices, swap(): return lax.ppermute(x, ('az', 'rad'), pairs)  0.8 us
  transfers between devices with their start and end apart: 6, of which 1 were waited for; matrix products, arithmetic and copies ran while one was open for 0% of the time, Pallas kernels for 22%

profile of v7, /device:TPU:0, one launch (start us, length us, event | category | flops | bytes accessed | tf_op | source)
XLA Modules:
  0.0 17.0 jit_solution(7314517675364847460)
XLA Ops:
  0.0 0.0 copy-start
  0.0 0.0 copy-start.1
  0.0 1.1 %pack_rows.1 = (f32[62,128]{1,0:T(8,128)S(1)}, f32[62,128]{1,0:T(8,128)S(1)}, f32[20,128]{1,0:T(8,128)S(1)}, f32[16,128]{1,0:T(8,128)S(1)}) custom-call(f32[8]{0:T(128)} %nu_hbm.1, f32[8]{0:T(128)} %sat_hbm.1, f32[9,256,128]{2,1,0:T(8,128)} %bitcast.4, f32[9,256,128]{2,1,0:T(8,128)} %bitcast.8, s32[3,256,128]{2,1,0:T(8,128)} %mat_ref.5, f32[9,256]{1,0:T(8,128)} %flux_hbm.1, ...), custom_call_target="tpu_custom_call" | custom-call | flops 1000000 | bytes 400000 | tf_op jit(solution)/shard_map/pack_rows/pallas_call | solution.py:148
  1.1 6.0 %collective-permute-start = (f32[62,128]{1,0:T(8,128)S(1)}, f32[62,128]{1,0:T(8,128)S(1)}, u32[]{:S(2)}, u32[]{:S(2)}) collective-permute-start(f32[62,128]{1,0:T(8,128)S(1)} %get-tuple-element.18), channel_id=1, source_target_pairs={{0,28},{1,29},{2,30},{3,31},{4,8},{5,9},{6,10},{7,11},{8,4},{9,5},... | collective-permute-start | bytes 95240 | tf_op jit(solution)/shard_map/ppermute | solution.py:664
  7.2 0.0 collective-permute-start.1
  7.2 0.1 collective-permute-start.2
  7.9 0.0 copy-done
  7.9 0.0 copy-done.1
  7.9 0.0 copy-done.2
  8.0 0.9 %turn_columns.1.refs_3_.strips_ref._cols = f32[21,16,384]{2,1,0:T(8,128)S(1)} custom-call(s32[1]{0:T(128)S(6)} %copy.17._offset.off_ref, f32[9,256,128]{2,1,0:T(8,128)S(1)} %bitcast.5, f32[9,256,128]{2,1,0:T(8,128)S(1)} %bitcast.9, s32[3,256,128]{2,1,0:T(8,128)S(1)} %copy-done.2), custom_call_target="tpu_custom_call" | custom-call | flops 8000000 | bytes 3000000 | tf_op jit(solution)/shard_map/turn_columns/pallas_call | solution.py:213
  8.9 1.4 %inner_rows.1 = (f32[3,288,128]{2,1,0:T(8,128)S(1)}, f32[9,272,128]{2,1,0:T(8,128)S(1)}, f32[9,256,128]{2,1,0:T(8,128)S(1)}) custom-call(f32[16,128]{1,0:T(8,128)S(1)} %get-tuple-element.17.table_ref, f32[9,256,128]{2,1,0:T(8,128)S(1)} %bitcast.6, f32[9,256,128]{2,1,0:T(8,128)S(1)} %bitcast.10, s32[3,256,128]{2,1,0:T(8,128)S(1)} %copy-done.2), custom_call_target="tpu_custom_call" | custom-call | flops 20000000 | bytes 4000000 | tf_op jit(solution)/shard_map/inner_rows/pallas_call | solution.py:370
  10.3 0.0 collective-permute-done.odd_ref.refs_1_
  10.3 0.8 %collective-permute-done.1.even_ref.refs_0_.refs_2_ = f32[62,128]{1,0:T(8,128)S(1)} collective-permute-done((f32[62,128]{1,0:T(8,128)S(1)}, f32[62,128]{1,0:T(8,128)S(1)}, u32[]{:S(2)}, u32[]{:S(2)}) %collective-permute-start.1) | collective-permute-done | bytes 31776 | tf_op jit(solution)/shard_map/ppermute | solution.py:664
  11.1 0.1 pack_columns.1
  11.2 0.0 collective-permute-done.2.refs_1_.refs_3_
  11.2 0.1 collective-permute-start.3
  11.3 1.7 %collective-permute-start.4 = (f32[45,256]{1,0:T(8,128)S(1)}, f32[45,256]{1,0:T(8,128)S(1)}, u32[]{:S(2)}, u32[]{:S(2)}) collective-permute-start(f32[45,256]{1,0:T(8,128)S(1)} %get-tuple-element.26), channel_id=1, source_target_pairs={{0,3},{1,2},{2,1},{3,0},{4,7},{5,6},{6,5},{7,4},{8,11},{9,10},{10,... | collective-permute-start | bytes 138248 | tf_op jit(solution)/shard_map/ppermute | solution.py:664
  13.1 0.8 %collective-permute-start.5 = (f32[45,256]{1,0:T(8,128)S(1)}, f32[45,256]{1,0:T(8,128)S(1)}, u32[]{:S(2)}, u32[]{:S(2)}) collective-permute-start(f32[45,256]{1,0:T(8,128)S(1)} %get-tuple-element.27), channel_id=1, source_target_pairs={{0,1},{1,0},{2,3},{3,2},{4,5},{5,4},{6,7},{7,6},{8,9},{9,8},{10,11... | collective-permute-start | bytes 138248 | tf_op jit(solution)/shard_map/ppermute | solution.py:664
  13.8 1.1 %outer_rows.1 = (f32[3,288,128]{2,1,0:T(8,128)S(1)}, f32[9,272,128]{2,1,0:T(8,128)S(1)}, f32[9,256,128]{2,1,0:T(8,128)S(1)}) custom-call(f32[16,128]{1,0:T(8,128)S(1)} %get-tuple-element.17.table_ref, f32[9,256,128]{2,1,0:T(8,128)S(1)} %bitcast.7, f32[9,256,128]{2,1,0:T(8,128)S(1)} %bitcast.11, ...), custom_call_target="tpu_custom_call", output_to_operand_aliasing={{0}: (6, {}), {1}: (7, {}), {2}: (8, {})} | custom-call | flops 20000000 | bytes 4000000 | tf_op jit(solution)/shard_map/outer_rows/pallas_call | solution.py:442
  15.0 0.0 collective-permute-done.3.refs_0_
  15.0 0.1 airgap_sum.1.air_ref
  15.1 0.0 collective-permute-done.4.ro_ref
  15.1 0.0 collective-permute-done.5.re_ref
  15.1 1.8 %rims.1 = (f32[9,256,128]{2,1,0:T(8,128)}, f32[21,16,384]{2,1,0:T(8,128)S(1)}) custom-call(f32[16,128]{1,0:T(8,128)S(1)} %get-tuple-element.17.table_ref, f32[9,256,128]{2,1,0:T(8,128)S(1)} %get-tuple-element.23.refs_4_.refs_2_.main_ref, f32[16,384]{1,0:T(8,128)S(1)} %airgap_sum.1.air_ref, ...), custom_call_target="tpu_custom_call", output_to_operand_aliasing={{1}: (3, {})} | custom-call | tf_op jit(solution)/shard_map/rims/pallas_call | solution.py:637
  (4 shorter events, 0.1 us)
Async XLA Ops:
  0.0 7.9 %copy-start = (f32[3,3,256,128]{3,2,1,0:T(8,128)S(1)}, f32[3,3,256,128]{3,2,1,0:T(8,128)}, u32[]{:S(2)}) copy-start(f32[3,3,256,128]{3,2,1,0:T(8,128)} %param.8) | copy-start | bytes 3538948
  0.0 7.9 %copy-start.1 = (f32[3,3,256,128]{3,2,1,0:T(8,128)S(1)}, f32[3,3,256,128]{3,2,1,0:T(8,128)}, u32[]{:S(2)}) copy-start(f32[3,3,256,128]{3,2,1,0:T(8,128)} %param.9) | copy-start | bytes 3538948
  0.0 7.9 %copy-start.2 = (s32[3,256,128]{2,1,0:T(8,128)S(1)}, s32[3,256,128]{2,1,0:T(8,128)}, u32[]{:S(2)}) copy-start(s32[3,256,128]{2,1,0:T(8,128)} %mat_ref.5) | copy-start | bytes 1179652
  1.1 9.2 %collective-permute-start = (f32[62,128]{1,0:T(8,128)S(1)}, f32[62,128]{1,0:T(8,128)S(1)}, u32[]{:S(2)}, u32[]{:S(2)}) collective-permute-start(f32[62,128]{1,0:T(8,128)S(1)} %get-tuple-element.18), channel_id=1, source_target_pairs={{0,28},{1,29},{2,30},{3,31},{4,8},{5,9},{6,10},{7,11},{8,4},{9,5},... | collective-permute-start | bytes 95240 | tf_op jit(solution)/shard_map/ppermute | solution.py:664
  7.2 3.9 %collective-permute-start.1 = (f32[62,128]{1,0:T(8,128)S(1)}, f32[62,128]{1,0:T(8,128)S(1)}, u32[]{:S(2)}, u32[]{:S(2)}) collective-permute-start(f32[62,128]{1,0:T(8,128)S(1)} %get-tuple-element.19), channel_id=1, source_target_pairs={{0,4},{1,5},{2,6},{3,7},{4,0},{5,1},{6,2},{7,3},{8,12},{9,13},{10,... | collective-permute-start | bytes 95240 | tf_op jit(solution)/shard_map/ppermute | solution.py:664
  7.2 4.0 %collective-permute-start.2 = (f32[20,128]{1,0:T(8,128)S(1)}, f32[20,128]{1,0:T(8,128)S(1)}, u32[]{:S(2)}, u32[]{:S(2)}) collective-permute-start(f32[20,128]{1,0:T(8,128)S(1)} %get-tuple-element.24.refs_0_), channel_id=1, source_target_pairs={{0,8},{1,9},{2,10},{3,11},{4,12},{5,13},{6,14},{7,15},{8,0},{9,1},... | collective-permute-start | bytes 30728 | tf_op jit(solution)/shard_map/ppermute | solution.py:664
  11.2 3.7 %collective-permute-start.3 = (f32[16,256]{1,0:T(8,128)S(1)}, f32[16,256]{1,0:T(8,128)S(1)}, u32[]{:S(2)}, u32[]{:S(2)}) collective-permute-start(f32[16,256]{1,0:T(8,128)S(1)} %airgap_far.1), channel_id=1, source_target_pairs={{0,3},{1,17},{2,18},{3,0},{4,7},{5,21},{6,22},{7,4},{8,11},{9,25},... | collective-permute-start | bytes 49160 | tf_op jit(solution)/shard_map/ppermute | solution.py:664
  11.3 3.8 %collective-permute-start.4 = (f32[45,256]{1,0:T(8,128)S(1)}, f32[45,256]{1,0:T(8,128)S(1)}, u32[]{:S(2)}, u32[]{:S(2)}) collective-permute-start(f32[45,256]{1,0:T(8,128)S(1)} %get-tuple-element.26), channel_id=1, source_target_pairs={{0,3},{1,2},{2,1},{3,0},{4,7},{5,6},{6,5},{7,4},{8,11},{9,10},{10,... | collective-permute-start | bytes 138248 | tf_op jit(solution)/shard_map/ppermute | solution.py:664
  13.1 2.0 %collective-permute-start.5 = (f32[45,256]{1,0:T(8,128)S(1)}, f32[45,256]{1,0:T(8,128)S(1)}, u32[]{:S(2)}, u32[]{:S(2)}) collective-permute-start(f32[45,256]{1,0:T(8,128)S(1)} %get-tuple-element.27), channel_id=1, source_target_pairs={{0,1},{1,0},{2,3},{3,2},{4,5},{5,4},{6,7},{7,6},{8,9},{9,8},{10,11... | collective-permute-start | bytes 138248 | tf_op jit(solution)/shard_map/ppermute | solution.py:664

commit v8 on v7

--- a/solution.py
+++ b/solution.py
@@ -104,9 +104,10 @@
 ):
     fields, layers = pot_ref.shape[1], mat_ref.shape[1]
     rows = pot_hbm.shape[1]
-    pairs = [(flux_hbm, flux_ref), (jit_hbm, jit_ref), (nu_hbm, nu_ref), (sat_hbm, sat_ref)]
+    pairs = []
     for hbm, ref in ((pot_hbm, pot_ref), (cur_hbm, cur_ref), (mat_hbm, mat_ref)):
         pairs += [(hbm.at[:, 0:8, :], ref.at[0]), (hbm.at[:, rows - 8 : rows, :], ref.at[1])]
+    pairs += [(flux_hbm, flux_ref), (jit_hbm, jit_ref), (nu_hbm, nu_ref), (sat_hbm, sat_ref)]
     copies = [pltpu.make_async_copy(src, dst, sems.at[n]) for n, (src, dst) in enumerate(pairs)]
     for copy in copies:
         copy.start()

time: 17.2 us -> 17.2 us (level)
  no operation moved by 1% of the time
where the time goes in v8:
time: 17.2 us; the launch traced here: 16.9 us
  starting transfers between devices  8.72 us (51%)
  Pallas kernels  6.66 us (39%)
  waiting for transfers between devices  0.79 us (5%)
  between operations  0.76 us (4%)
    ppermute x6, starting transfers between devices, swap(): return lax.ppermute(x, ('az', 'rad'), pairs)  8.72 us
    pallas_call x1, Pallas kernels, rims(): pl.pallas_call(rim_kernel, out_shape=[jax.ShapeDtypeStruct(main.shape, f3...  1.84 us
    pallas_call x1, Pallas kernels, inner(): pl.pallas_call(inner_kernel, out_shape=[jax.ShapeDtypeStruct((layers, row...  1.42 us
    pallas_call x1, Pallas kernels, outer(): pl.pallas_call(outer_kernel, out_shape=[jax.ShapeDtypeStruct(coef.shape,...  1.12 us
    pallas_call x1, Pallas kernels, edges(): pl.pallas_call(edges_kernel, out_shape=[jax.ShapeDtypeStruct((send + pan_...  1.11 us
    pallas_call x1, Pallas kernels, columns(): pl.pallas_call(columns_kernel, out_shape=jax.ShapeDtypeStruct((total, 16,...  0.91 us
    ppermute x6, waiting for transfers between devices, swap(): return lax.ppermute(x, ('az', 'rad'), pairs)  0.79 us
  transfers between devices with their start and end apart: 6, of which 1 were waited for; matrix products, arithmetic and copies ran while one was open for 0% of the time, Pallas kernels for 22%

profile of v8, /device:TPU:0, one launch (start us, length us, event | category | flops | bytes accessed | tf_op | source)
XLA Modules:
  0.0 16.9 jit_solution(9963605363353717499)
XLA Ops:
  0.0 0.0 copy-start
  0.0 0.0 copy-start.1
  0.0 1.1 %pack_rows.1 = (f32[62,128]{1,0:T(8,128)S(1)}, f32[62,128]{1,0:T(8,128)S(1)}, f32[20,128]{1,0:T(8,128)S(1)}, f32[16,128]{1,0:T(8,128)S(1)}) custom-call(f32[8]{0:T(128)} %nu_hbm.1, f32[8]{0:T(128)} %sat_hbm.1, f32[9,256,128]{2,1,0:T(8,128)} %bitcast.4, f32[9,256,128]{2,1,0:T(8,128)} %bitcast.8, s32[3,256,128]{2,1,0:T(8,128)} %mat_ref.5, f32[9,256]{1,0:T(8,128)} %flux_hbm.1, ...), custom_call_target="tpu_custom_call" | custom-call | flops 1000000 | bytes 400000 | tf_op jit(solution)/shard_map/pack_rows/pallas_call | solution.py:149
  1.1 6.0 %collective-permute-start = (f32[62,128]{1,0:T(8,128)S(1)}, f32[62,128]{1,0:T(8,128)S(1)}, u32[]{:S(2)}, u32[]{:S(2)}) collective-permute-start(f32[62,128]{1,0:T(8,128)S(1)} %get-tuple-element.18), channel_id=1, source_target_pairs={{0,28},{1,29},{2,30},{3,31},{4,8},{5,9},{6,10},{7,11},{8,4},{9,5},... | collective-permute-start | bytes 95240 | tf_op jit(solution)/shard_map/ppermute | solution.py:665
  7.2 0.0 collective-permute-start.1
  7.2 0.1 collective-permute-start.2
  7.9 0.0 copy-done
  7.9 0.0 copy-done.1
  7.9 0.0 copy-done.2
  7.9 0.9 %turn_columns.1.refs_3_.strips_ref._cols = f32[21,16,384]{2,1,0:T(8,128)S(1)} custom-call(s32[1]{0:T(128)S(6)} %copy.17._offset.off_ref, f32[9,256,128]{2,1,0:T(8,128)S(1)} %bitcast.5, f32[9,256,128]{2,1,0:T(8,128)S(1)} %bitcast.9, s32[3,256,128]{2,1,0:T(8,128)S(1)} %copy-done.2), custom_call_target="tpu_custom_call" | custom-call | flops 8000000 | bytes 3000000 | tf_op jit(solution)/shard_map/turn_columns/pallas_call | solution.py:214
  8.9 1.4 %inner_rows.1 = (f32[3,288,128]{2,1,0:T(8,128)S(1)}, f32[9,272,128]{2,1,0:T(8,128)S(1)}, f32[9,256,128]{2,1,0:T(8,128)S(1)}) custom-call(f32[16,128]{1,0:T(8,128)S(1)} %get-tuple-element.17.table_ref, f32[9,256,128]{2,1,0:T(8,128)S(1)} %bitcast.6, f32[9,256,128]{2,1,0:T(8,128)S(1)} %bitcast.10, s32[3,256,128]{2,1,0:T(8,128)S(1)} %copy-done.2), custom_call_target="tpu_custom_call" | custom-call | flops 20000000 | bytes 4000000 | tf_op jit(solution)/shard_map/inner_rows/pallas_call | solution.py:371
  10.3 0.0 collective-permute-done.odd_ref.refs_1_
  10.3 0.8 %collective-permute-done.1.even_ref.refs_0_.refs_2_ = f32[62,128]{1,0:T(8,128)S(1)} collective-permute-done((f32[62,128]{1,0:T(8,128)S(1)}, f32[62,128]{1,0:T(8,128)S(1)}, u32[]{:S(2)}, u32[]{:S(2)}) %collective-permute-start.1) | collective-permute-done | bytes 31776 | tf_op jit(solution)/shard_map/ppermute | solution.py:665
  11.1 0.1 pack_columns.1
  11.2 0.0 collective-permute-done.2.refs_1_.refs_3_
  11.2 0.1 collective-permute-start.3
  11.3 1.7 %collective-permute-start.4 = (f32[45,256]{1,0:T(8,128)S(1)}, f32[45,256]{1,0:T(8,128)S(1)}, u32[]{:S(2)}, u32[]{:S(2)}) collective-permute-start(f32[45,256]{1,0:T(8,128)S(1)} %get-tuple-element.26), channel_id=1, source_target_pairs={{0,3},{1,2},{2,1},{3,0},{4,7},{5,6},{6,5},{7,4},{8,11},{9,10},{10,... | collective-permute-start | bytes 138248 | tf_op jit(solution)/shard_map/ppermute | solution.py:665
  13.1 0.8 %collective-permute-start.5 = (f32[45,256]{1,0:T(8,128)S(1)}, f32[45,256]{1,0:T(8,128)S(1)}, u32[]{:S(2)}, u32[]{:S(2)}) collective-permute-start(f32[45,256]{1,0:T(8,128)S(1)} %get-tuple-element.27), channel_id=1, source_target_pairs={{0,1},{1,0},{2,3},{3,2},{4,5},{5,4},{6,7},{7,6},{8,9},{9,8},{10,11... | collective-permute-start | bytes 138248 | tf_op jit(solution)/shard_map/ppermute | solution.py:665
  13.8 1.1 %outer_rows.1 = (f32[3,288,128]{2,1,0:T(8,128)S(1)}, f32[9,272,128]{2,1,0:T(8,128)S(1)}, f32[9,256,128]{2,1,0:T(8,128)S(1)}) custom-call(f32[16,128]{1,0:T(8,128)S(1)} %get-tuple-element.17.table_ref, f32[9,256,128]{2,1,0:T(8,128)S(1)} %bitcast.7, f32[9,256,128]{2,1,0:T(8,128)S(1)} %bitcast.11, ...), custom_call_target="tpu_custom_call", output_to_operand_aliasing={{0}: (6, {}), {1}: (7, {}), {2}: (8, {})} | custom-call | flops 20000000 | bytes 4000000 | tf_op jit(solution)/shard_map/outer_rows/pallas_call | solution.py:443
  15.0 0.0 collective-permute-done.3.refs_0_
  15.0 0.1 airgap_sum.1.air_ref
  15.1 0.0 collective-permute-done.4.ro_ref
  15.1 0.0 collective-permute-done.5.re_ref
  15.1 1.8 %rims.1 = (f32[9,256,128]{2,1,0:T(8,128)}, f32[21,16,384]{2,1,0:T(8,128)S(1)}) custom-call(f32[16,128]{1,0:T(8,128)S(1)} %get-tuple-element.17.table_ref, f32[9,256,128]{2,1,0:T(8,128)S(1)} %get-tuple-element.23.refs_4_.refs_2_.main_ref, f32[16,384]{1,0:T(8,128)S(1)} %airgap_sum.1.air_ref, ...), custom_call_target="tpu_custom_call", output_to_operand_aliasing={{1}: (3, {})} | custom-call | tf_op jit(solution)/shard_map/rims/pallas_call | solution.py:638
  (4 shorter events, 0.1 us)
Async XLA Ops:
  0.0 7.9 %copy-start = (f32[3,3,256,128]{3,2,1,0:T(8,128)S(1)}, f32[3,3,256,128]{3,2,1,0:T(8,128)}, u32[]{:S(2)}) copy-start(f32[3,3,256,128]{3,2,1,0:T(8,128)} %param.8) | copy-start | bytes 3538948
  0.0 7.9 %copy-start.1 = (f32[3,3,256,128]{3,2,1,0:T(8,128)S(1)}, f32[3,3,256,128]{3,2,1,0:T(8,128)}, u32[]{:S(2)}) copy-start(f32[3,3,256,128]{3,2,1,0:T(8,128)} %param.9) | copy-start | bytes 3538948
  0.0 7.9 %copy-start.2 = (s32[3,256,128]{2,1,0:T(8,128)S(1)}, s32[3,256,128]{2,1,0:T(8,128)}, u32[]{:S(2)}) copy-start(s32[3,256,128]{2,1,0:T(8,128)} %mat_ref.5) | copy-start | bytes 1179652
  1.1 9.2 %collective-permute-start = (f32[62,128]{1,0:T(8,128)S(1)}, f32[62,128]{1,0:T(8,128)S(1)}, u32[]{:S(2)}, u32[]{:S(2)}) collective-permute-start(f32[62,128]{1,0:T(8,128)S(1)} %get-tuple-element.18), channel_id=1, source_target_pairs={{0,28},{1,29},{2,30},{3,31},{4,8},{5,9},{6,10},{7,11},{8,4},{9,5},... | collective-permute-start | bytes 95240 | tf_op jit(solution)/shard_map/ppermute | solution.py:665
  7.2 3.9 %collective-permute-start.1 = (f32[62,128]{1,0:T(8,128)S(1)}, f32[62,128]{1,0:T(8,128)S(1)}, u32[]{:S(2)}, u32[]{:S(2)}) collective-permute-start(f32[62,128]{1,0:T(8,128)S(1)} %get-tuple-element.19), channel_id=1, source_target_pairs={{0,4},{1,5},{2,6},{3,7},{4,0},{5,1},{6,2},{7,3},{8,12},{9,13},{10,... | collective-permute-start | bytes 95240 | tf_op jit(solution)/shard_map/ppermute | solution.py:665
  7.2 4.0 %collective-permute-start.2 = (f32[20,128]{1,0:T(8,128)S(1)}, f32[20,128]{1,0:T(8,128)S(1)}, u32[]{:S(2)}, u32[]{:S(2)}) collective-permute-start(f32[20,128]{1,0:T(8,128)S(1)} %get-tuple-element.24.refs_0_), channel_id=1, source_target_pairs={{0,8},{1,9},{2,10},{3,11},{4,12},{5,13},{6,14},{7,15},{8,0},{9,1},... | collective-permute-start | bytes 30728 | tf_op jit(solution)/shard_map/ppermute | solution.py:665
  11.2 3.8 %collective-permute-start.3 = (f32[16,256]{1,0:T(8,128)S(1)}, f32[16,256]{1,0:T(8,128)S(1)}, u32[]{:S(2)}, u32[]{:S(2)}) collective-permute-start(f32[16,256]{1,0:T(8,128)S(1)} %airgap_far.1), channel_id=1, source_target_pairs={{0,3},{1,17},{2,18},{3,0},{4,7},{5,21},{6,22},{7,4},{8,11},{9,25},... | collective-permute-start | bytes 49160 | tf_op jit(solution)/shard_map/ppermute | solution.py:665
  11.3 3.8 %collective-permute-start.4 = (f32[45,256]{1,0:T(8,128)S(1)}, f32[45,256]{1,0:T(8,128)S(1)}, u32[]{:S(2)}, u32[]{:S(2)}) collective-permute-start(f32[45,256]{1,0:T(8,128)S(1)} %get-tuple-element.26), channel_id=1, source_target_pairs={{0,3},{1,2},{2,1},{3,0},{4,7},{5,6},{6,5},{7,4},{8,11},{9,10},{10,... | collective-permute-start | bytes 138248 | tf_op jit(solution)/shard_map/ppermute | solution.py:665
  13.1 2.0 %collective-permute-start.5 = (f32[45,256]{1,0:T(8,128)S(1)}, f32[45,256]{1,0:T(8,128)S(1)}, u32[]{:S(2)}, u32[]{:S(2)}) collective-permute-start(f32[45,256]{1,0:T(8,128)S(1)} %get-tuple-element.27), channel_id=1, source_target_pairs={{0,1},{1,0},{2,3},{3,2},{4,5},{5,4},{6,7},{7,6},{8,9},{9,8},{10,11... | collective-permute-start | bytes 138248 | tf_op jit(solution)/shard_map/ppermute | solution.py:665

commit v9 on v8

--- a/solution.py
+++ b/solution.py
@@ -467,7 +467,7 @@
     @pl.when(stator)
     def _():
         lanes = vals_ref.shape[1]
-        vals_ref[...] = jnp.zeros_like(vals_ref)
+        vals_ref[8:16, :] = jnp.zeros((8, lanes), f32)
         t = 0
         for ref, first in zip(pan_refs, starts):
             for at in range(first, ref.shape[0], fields + 1):

time: 17.2 us -> 17.2 us (level)
  no operation moved by 1% of the time
where the time goes in v9:
time: 17.2 us; the launch traced here: 16.9 us
  starting transfers between devices  8.72 us (51%)
  Pallas kernels  6.66 us (39%)
  waiting for transfers between devices  0.79 us (5%)
  between operations  0.76 us (4%)
    ppermute x6, starting transfers between devices, swap(): return lax.ppermute(x, ('az', 'rad'), pairs)  8.72 us
    pallas_call x1, Pallas kernels, rims(): pl.pallas_call(rim_kernel, out_shape=[jax.ShapeDtypeStruct(main.shape, f3...  1.84 us
    pallas_call x1, Pallas kernels, inner(): pl.pallas_call(inner_kernel, out_shape=[jax.ShapeDtypeStruct((layers, row...  1.42 us
    pallas_call x1, Pallas kernels, outer(): pl.pallas_call(outer_kernel, out_shape=[jax.ShapeDtypeStruct(coef.shape,...  1.12 us
    pallas_call x1, Pallas kernels, edges(): pl.pallas_call(edges_kernel, out_shape=[jax.ShapeDtypeStruct((send + pan_...  1.11 us
    pallas_call x1, Pallas kernels, columns(): pl.pallas_call(columns_kernel, out_shape=jax.ShapeDtypeStruct((total, 16,...  0.91 us
    ppermute x6, waiting for transfers between devices, swap(): return lax.ppermute(x, ('az', 'rad'), pairs)  0.79 us
  transfers between devices with their start and end apart: 6, of which 1 were waited for; matrix products, arithmetic and copies ran while one was open for 0% of the time, Pallas kernels for 22%

profile of v9, /device:TPU:0, one launch (start us, length us, event | category | flops | bytes accessed | tf_op | source)
XLA Modules:
  0.0 16.9 jit_solution(9963605363353717499)
XLA Ops:
  0.0 0.0 copy-start
  0.0 0.0 copy-start.1
  0.0 1.1 %pack_rows.1 = (f32[62,128]{1,0:T(8,128)S(1)}, f32[62,128]{1,0:T(8,128)S(1)}, f32[20,128]{1,0:T(8,128)S(1)}, f32[16,128]{1,0:T(8,128)S(1)}) custom-call(f32[8]{0:T(128)} %nu_hbm.1, f32[8]{0:T(128)} %sat_hbm.1, f32[9,256,128]{2,1,0:T(8,128)} %bitcast.4, f32[9,256,128]{2,1,0:T(8,128)} %bitcast.8, s32[3,256,128]{2,1,0:T(8,128)} %mat_ref.5, f32[9,256]{1,0:T(8,128)} %flux_hbm.1, ...), custom_call_target="tpu_custom_call" | custom-call | flops 1000000 | bytes 400000 | tf_op jit(solution)/shard_map/pack_rows/pallas_call | solution.py:149
  1.1 6.0 %collective-permute-start = (f32[62,128]{1,0:T(8,128)S(1)}, f32[62,128]{1,0:T(8,128)S(1)}, u32[]{:S(2)}, u32[]{:S(2)}) collective-permute-start(f32[62,128]{1,0:T(8,128)S(1)} %get-tuple-element.18), channel_id=1, source_target_pairs={{0,28},{1,29},{2,30},{3,31},{4,8},{5,9},{6,10},{7,11},{8,4},{9,5},... | collective-permute-start | bytes 95240 | tf_op jit(solution)/shard_map/ppermute | solution.py:665
  7.2 0.0 collective-permute-start.1
  7.2 0.1 collective-permute-start.2
  7.9 0.0 copy-done
  7.9 0.0 copy-done.1
  7.9 0.0 copy-done.2
  7.9 0.9 %turn_columns.1.refs_3_.strips_ref._cols = f32[21,16,384]{2,1,0:T(8,128)S(1)} custom-call(s32[1]{0:T(128)S(6)} %copy.17._offset.off_ref, f32[9,256,128]{2,1,0:T(8,128)S(1)} %bitcast.5, f32[9,256,128]{2,1,0:T(8,128)S(1)} %bitcast.9, s32[3,256,128]{2,1,0:T(8,128)S(1)} %copy-done.2), custom_call_target="tpu_custom_call" | custom-call | flops 8000000 | bytes 3000000 | tf_op jit(solution)/shard_map/turn_columns/pallas_call | solution.py:214
  8.9 1.4 %inner_rows.1 = (f32[3,288,128]{2,1,0:T(8,128)S(1)}, f32[9,272,128]{2,1,0:T(8,128)S(1)}, f32[9,256,128]{2,1,0:T(8,128)S(1)}) custom-call(f32[16,128]{1,0:T(8,128)S(1)} %get-tuple-element.17.table_ref, f32[9,256,128]{2,1,0:T(8,128)S(1)} %bitcast.6, f32[9,256,128]{2,1,0:T(8,128)S(1)} %bitcast.10, s32[3,256,128]{2,1,0:T(8,128)S(1)} %copy-done.2), custom_call_target="tpu_custom_call" | custom-call | flops 20000000 | bytes 4000000 | tf_op jit(solution)/shard_map/inner_rows/pallas_call | solution.py:371
  10.3 0.0 collective-permute-done.odd_ref.refs_1_
  10.3 0.8 %collective-permute-done.1.even_ref.refs_0_.refs_2_ = f32[62,128]{1,0:T(8,128)S(1)} collective-permute-done((f32[62,128]{1,0:T(8,128)S(1)}, f32[62,128]{1,0:T(8,128)S(1)}, u32[]{:S(2)}, u32[]{:S(2)}) %collective-permute-start.1) | collective-permute-done | bytes 31776 | tf_op jit(solution)/shard_map/ppermute | solution.py:665
  11.1 0.1 pack_columns.1
  11.2 0.0 collective-permute-done.2.refs_1_.refs_3_
  11.2 0.1 collective-permute-start.3
  11.3 1.7 %collective-permute-start.4 = (f32[45,256]{1,0:T(8,128)S(1)}, f32[45,256]{1,0:T(8,128)S(1)}, u32[]{:S(2)}, u32[]{:S(2)}) collective-permute-start(f32[45,256]{1,0:T(8,128)S(1)} %get-tuple-element.26), channel_id=1, source_target_pairs={{0,3},{1,2},{2,1},{3,0},{4,7},{5,6},{6,5},{7,4},{8,11},{9,10},{10,... | collective-permute-start | bytes 138248 | tf_op jit(solution)/shard_map/ppermute | solution.py:665
  13.1 0.8 %collective-permute-start.5 = (f32[45,256]{1,0:T(8,128)S(1)}, f32[45,256]{1,0:T(8,128)S(1)}, u32[]{:S(2)}, u32[]{:S(2)}) collective-permute-start(f32[45,256]{1,0:T(8,128)S(1)} %get-tuple-element.27), channel_id=1, source_target_pairs={{0,1},{1,0},{2,3},{3,2},{4,5},{5,4},{6,7},{7,6},{8,9},{9,8},{10,11... | collective-permute-start | bytes 138248 | tf_op jit(solution)/shard_map/ppermute | solution.py:665
  13.8 1.1 %outer_rows.1 = (f32[3,288,128]{2,1,0:T(8,128)S(1)}, f32[9,272,128]{2,1,0:T(8,128)S(1)}, f32[9,256,128]{2,1,0:T(8,128)S(1)}) custom-call(f32[16,128]{1,0:T(8,128)S(1)} %get-tuple-element.17.table_ref, f32[9,256,128]{2,1,0:T(8,128)S(1)} %bitcast.7, f32[9,256,128]{2,1,0:T(8,128)S(1)} %bitcast.11, ...), custom_call_target="tpu_custom_call", output_to_operand_aliasing={{0}: (6, {}), {1}: (7, {}), {2}: (8, {})} | custom-call | flops 20000000 | bytes 4000000 | tf_op jit(solution)/shard_map/outer_rows/pallas_call | solution.py:443
  15.0 0.0 collective-permute-done.3.refs_0_
  15.0 0.1 airgap_sum.1.air_ref
  15.1 0.0 collective-permute-done.4.ro_ref
  15.1 0.0 collective-permute-done.5.re_ref
  15.1 1.8 %rims.1 = (f32[9,256,128]{2,1,0:T(8,128)}, f32[21,16,384]{2,1,0:T(8,128)S(1)}) custom-call(f32[16,128]{1,0:T(8,128)S(1)} %get-tuple-element.17.table_ref, f32[9,256,128]{2,1,0:T(8,128)S(1)} %get-tuple-element.23.refs_4_.refs_2_.main_ref, f32[16,384]{1,0:T(8,128)S(1)} %airgap_sum.1.air_ref, ...), custom_call_target="tpu_custom_call", output_to_operand_aliasing={{1}: (3, {})} | custom-call | tf_op jit(solution)/shard_map/rims/pallas_call | solution.py:638
  (4 shorter events, 0.1 us)
Async XLA Ops:
  0.0 7.9 %copy-start = (f32[3,3,256,128]{3,2,1,0:T(8,128)S(1)}, f32[3,3,256,128]{3,2,1,0:T(8,128)}, u32[]{:S(2)}) copy-start(f32[3,3,256,128]{3,2,1,0:T(8,128)} %param.8) | copy-start | bytes 3538948
  0.0 7.9 %copy-start.1 = (f32[3,3,256,128]{3,2,1,0:T(8,128)S(1)}, f32[3,3,256,128]{3,2,1,0:T(8,128)}, u32[]{:S(2)}) copy-start(f32[3,3,256,128]{3,2,1,0:T(8,128)} %param.9) | copy-start | bytes 3538948
  0.0 7.9 %copy-start.2 = (s32[3,256,128]{2,1,0:T(8,128)S(1)}, s32[3,256,128]{2,1,0:T(8,128)}, u32[]{:S(2)}) copy-start(s32[3,256,128]{2,1,0:T(8,128)} %mat_ref.5) | copy-start | bytes 1179652
  1.1 9.2 %collective-permute-start = (f32[62,128]{1,0:T(8,128)S(1)}, f32[62,128]{1,0:T(8,128)S(1)}, u32[]{:S(2)}, u32[]{:S(2)}) collective-permute-start(f32[62,128]{1,0:T(8,128)S(1)} %get-tuple-element.18), channel_id=1, source_target_pairs={{0,28},{1,29},{2,30},{3,31},{4,8},{5,9},{6,10},{7,11},{8,4},{9,5},... | collective-permute-start | bytes 95240 | tf_op jit(solution)/shard_map/ppermute | solution.py:665
  7.2 3.9 %collective-permute-start.1 = (f32[62,128]{1,0:T(8,128)S(1)}, f32[62,128]{1,0:T(8,128)S(1)}, u32[]{:S(2)}, u32[]{:S(2)}) collective-permute-start(f32[62,128]{1,0:T(8,128)S(1)} %get-tuple-element.19), channel_id=1, source_target_pairs={{0,4},{1,5},{2,6},{3,7},{4,0},{5,1},{6,2},{7,3},{8,12},{9,13},{10,... | collective-permute-start | bytes 95240 | tf_op jit(solution)/shard_map/ppermute | solution.py:665
  7.2 4.0 %collective-permute-start.2 = (f32[20,128]{1,0:T(8,128)S(1)}, f32[20,128]{1,0:T(8,128)S(1)}, u32[]{:S(2)}, u32[]{:S(2)}) collective-permute-start(f32[20,128]{1,0:T(8,128)S(1)} %get-tuple-element.24.refs_0_), channel_id=1, source_target_pairs={{0,8},{1,9},{2,10},{3,11},{4,12},{5,13},{6,14},{7,15},{8,0},{9,1},... | collective-permute-start | bytes 30728 | tf_op jit(solution)/shard_map/ppermute | solution.py:665
  11.2 3.8 %collective-permute-start.3 = (f32[16,256]{1,0:T(8,128)S(1)}, f32[16,256]{1,0:T(8,128)S(1)}, u32[]{:S(2)}, u32[]{:S(2)}) collective-permute-start(f32[16,256]{1,0:T(8,128)S(1)} %airgap_far.1), channel_id=1, source_target_pairs={{0,3},{1,17},{2,18},{3,0},{4,7},{5,21},{6,22},{7,4},{8,11},{9,25},... | collective-permute-start | bytes 49160 | tf_op jit(solution)/shard_map/ppermute | solution.py:665
  11.3 3.8 %collective-permute-start.4 = (f32[45,256]{1,0:T(8,128)S(1)}, f32[45,256]{1,0:T(8,128)S(1)}, u32[]{:S(2)}, u32[]{:S(2)}) collective-permute-start(f32[45,256]{1,0:T(8,128)S(1)} %get-tuple-element.26), channel_id=1, source_target_pairs={{0,3},{1,2},{2,1},{3,0},{4,7},{5,6},{6,5},{7,4},{8,11},{9,10},{10,... | collective-permute-start | bytes 138248 | tf_op jit(solution)/shard_map/ppermute | solution.py:665
  13.1 2.0 %collective-permute-start.5 = (f32[45,256]{1,0:T(8,128)S(1)}, f32[45,256]{1,0:T(8,128)S(1)}, u32[]{:S(2)}, u32[]{:S(2)}) collective-permute-start(f32[45,256]{1,0:T(8,128)S(1)} %get-tuple-element.27), channel_id=1, source_target_pairs={{0,1},{1,0},{2,3},{3,2},{4,5},{5,4},{6,7},{7,6},{8,9},{9,8},{10,11... | collective-permute-start | bytes 138248 | tf_op jit(solution)/shard_map/ppermute | solution.py:665
